TPU v7x, 128 devices: a whole 4x4x4 slice. The times are simulated.
128 devices in a mesh: lat: 8 (over y, core), lon: 16 (over x, z).
Axes of the slice: x: 4, y: 4, z: 4, core: 2. Of those that a mesh axis runs over, the one named last changes fastest.
Arguments:
- spectra: float32 [1800, 128, 1024], P(None, 'lon', 'lat'), may hold values from 0 to 2.1, as said below
- sea_mask: int32 [128, 1024], P('lon', 'lat'), may hold values 0 or 1
- atm_wind: float32 [2, 262144], P(None, ('lat', 'lon')), may hold values from -10 to 10
- wind_row: int32 [128, 1024], P('lon', 'lat'), may hold values from 0 to 262143, as said below
- owner: int32 [128, 1024], P('lon', 'lat'), may hold values from 0 to 65535, as said below
- weight: int32 [128, 1024], P('lon', 'lat'), may hold values from 1 to 8
Outputs:
- spectra_out: float32 [1800, 128, 1024], P(None, 'lon', 'lat')
- wave_stress: float32 [2, 65536], P(None, ('lat', 'lon'))
- roughness: float32 [65536], P(('lat', 'lon'))
Inputs may be any that keep to these rules, and one draw needn't show every extreme that they name: `spectra`: Positive. `wind_row`: A grid point in latitude band i (rows i * 128 to (i + 1) * 128 - 1) reads a row of band i: row // 32768 == i; any sector of the band. A grid point in latitude band i sends to a cell of band i: owner // 8192 == i; any sector of the band. Some cells receive no point.
All inputs are finite; a program needn't handle non-finite values. No bound on the sum of `sea_mask` on one device may be relied on, other than what follows from the above.
Results may differ from a plain program's by a relative error of at most 0.00024.
Values sent between devices are 32-bit elements; how exact they have to be, the bound alone decides.
No kernel may reach another device: no remote copies, remote signals or barrier semaphores. Data moves between devices by JAX's collectives and lax.ppermute only.
A program may use at most 256 MiB of HBM per device.

v0:
```python
import math

import jax
import jax.numpy as jnp
from jax import lax
from jax.sharding import PartitionSpec as P

NF = 50
ND = 36
XC_DEV = 512
STEPS = 2


def extended(block, sides, width, periodic):
    for axis, dim in sides:
        count = lax.axis_size(axis)
        forward = [(i, i + 1) for i in range(count - 1)]
        if periodic:
            forward.append((count - 1, 0))
        backward = [(target, source) for source, target in forward]
        low = lax.ppermute(
            lax.slice_in_dim(block, block.shape[dim] - width, None, axis=dim), axis, forward
        )
        high = lax.ppermute(lax.slice_in_dim(block, 0, width, axis=dim), axis, backward)
        block = jnp.concatenate([low, block, high], axis=dim)
    return block


def bin_tables(nfreq, ndir):
    index = jnp.arange(nfreq * ndir, dtype=jnp.int32)
    fpos = (index // ndir).astype(jnp.float32)
    dpos = (index % ndir).astype(jnp.float32)
    freq_b = 1.07 ** (fpos - (nfreq - 1))
    theta = 2.0 * math.pi * (dpos + 0.5) / ndir
    cos_b = jnp.cos(theta)
    sin_b = jnp.sin(theta)
    cour_b = 0.7 * (3.0 / 7.0) ** (fpos / (nfreq - 1))
    slope_b = 250.0 * freq_b**4 / ndir
    push_scale = 800.0 * freq_b**2 / ndir
    push_b = jnp.stack([push_scale * cos_b, push_scale * sin_b], axis=1)
    return (freq_b, cos_b, sin_b, cour_b, slope_b, push_b)


def wind_rate(wind_u, wind_v, freq_b, cos_b, sin_b):
    along = cos_b[:, None, None] * wind_u[None] + sin_b[:, None, None] * wind_v[None]
    return 0.2 * freq_b[:, None, None] * jnp.maximum(3.0 * freq_b[:, None, None] * along - 1.0, 0.0)


def force_terms(energy, rate_in, freq_b, slope_b):
    msq = jnp.einsum("bxy,b->xy", energy, slope_b, precision=lax.Precision.HIGHEST)
    return energy * (1.0 + rate_in) / (1.0 + 4.0 * freq_b[:, None, None] * msq[None])


def advect(padded, cx_b, cy_b):
    center = padded[:, 1:-1, 1:-1]
    west = padded[:, :-2, 1:-1]
    east = padded[:, 2:, 1:-1]
    south = padded[:, 1:-1, :-2]
    north = padded[:, 1:-1, 2:]
    cxp = jnp.maximum(cx_b, 0.0)[:, None, None]
    cxm = jnp.minimum(cx_b, 0.0)[:, None, None]
    cyp = jnp.maximum(cy_b, 0.0)[:, None, None]
    cym = jnp.minimum(cy_b, 0.0)[:, None, None]
    return (
        center
        - cxp * (center - west)
        - cxm * (east - center)
        - cyp * (center - south)
        - cym * (north - center)
    )


def body(spectra, sea_mask, atm_wind, wind_row, owner, weight):
    nbins, plon, plat = spectra.shape
    freq_b, cos_b, sin_b, cour_b, slope_b, push_b = bin_tables(NF, ND)
    cx_b = cour_b * cos_b
    cy_b = cour_b * sin_b
    lon_count = lax.axis_size("lon")
    lat_pos = lax.axis_index("lat")
    atm_dev = atm_wind.shape[1]
    fetched = lax.all_gather(atm_wind, "lon", axis=1, tiled=True)
    local = wind_row - lat_pos * lon_count * atm_dev
    picked = jnp.take(fetched, local.reshape(-1), axis=1).reshape(2, plon, plat)
    wind_u = picked[0]
    wind_v = picked[1]
    maskf = sea_mask.astype(jnp.float32)
    energy = spectra * maskf[None]
    rate_in = wind_rate(wind_u, wind_v, freq_b, cos_b, sin_b)
    for step in range(STEPS):
        forced = force_terms(energy, rate_in, freq_b, slope_b)
        widened = extended(forced, (("lon", 1),), 1, True)
        padded = extended(widened, (("lat", 2),), 1, False)
        energy = advect(padded, cx_b, cy_b) * maskf[None]
    push = jnp.einsum("bxy,bk->kxy", rate_in * energy, push_b, precision=lax.Precision.HIGHEST)
    share = weight.astype(jnp.float32) * maskf
    tau = 0.02 * (wind_u * wind_u + wind_v * wind_v) + 0.25
    terms = jnp.stack([share, share * tau, share * push[0], share * push[1]]).reshape(4, -1)
    band_start = lat_pos * lon_count * XC_DEV
    partial_cells = (
        jnp.zeros((4, lon_count * XC_DEV), jnp.float32)
        .at[:, (owner - band_start).reshape(-1)]
        .add(terms)
    )
    sums = lax.psum_scatter(partial_cells, "lon", scatter_dimension=1, tiled=True)
    total_w = jnp.maximum(sums[0], 1.0)
    wave_stress = sums[2:4] / total_w[None]
    ratio = (sums[2] * sums[2] + sums[3] * sums[3]) / jnp.maximum(sums[1], 1.0) ** 2
    roughness = jnp.sqrt(1.0 + ratio) * sums[1] / total_w
    return (energy, wave_stress, roughness)


def solution(mesh):
    in_specs = (
        P(None, "lon", "lat"),
        P("lon", "lat"),
        P(None, ("lat", "lon")),
        P("lon", "lat"),
        P("lon", "lat"),
        P("lon", "lat"),
    )
    out_specs = (P(None, "lon", "lat"), P(None, ("lat", "lon")), P(("lat", "lon")))
    return jax.shard_map(body, mesh=mesh, in_specs=in_specs, out_specs=out_specs, check_vma=False)
```

profile of v0, /device:TPU:0, one launch (start us, length us, event | category | flops | bytes accessed | tf_op | source)
XLA Modules:
  0.0 431.9 jit_solution(15247272113473088366)
XLA Ops:
  9.2 94.9 %all_gather.3 = f32[2,32768]{0,1:T(8,128)} all-gather(f32[2,2048]{0,1:T(8,128)S(1)} %copy.48), channel_id=1, replica_groups=mesh['lat'=8,'lon'=16] {'lon'}, dimensions={1}, use_global_device_ids=true | all-gather | bytes 278528 | tf_op jit(solution)/shard_map/all_gather | solution.py:81
  104.0 8.6 %gather_fusion = f32[1024,2]{1,0:T(8,128)S(1)} fusion(f32[2,32768]{0,1:T(8,128)} %all_gather.3, s32[1024]{0:T(1024)S(1)} %broadcast_clamp_fusion), kind=kCustom, calls=%fused_computation | custom fusion | bytes 20480 | tf_op jit(solution)/shard_map/jit(_take)/gather | solution.py:83
  113.4 8.6 %fusion.29 = f32[1,8,128]{2,0,1:T(1,128)S(1)} fusion(f32[1800,1,1]{0,1,2:T(1,128)S(1)} %reshape.258, f32[1800,8,128]{2,1,0:T(8,128)} %param.6, f32[8,128]{1,0:T(8,128)S(1)} %convert_element_type.127), kind=kOutput, calls=%fused_computation.53 | convolution fusion | flops 23961600 | bytes 7388192 | tf_op jit(solution)/shard_map/bxy,b->xy/dot_general | solution.py:50
  122.0 7.3 %add_divide_fusion.1 = f32[1800,8,128]{2,0,1:T(8,128)S(1)} fusion(f32[1800,8,128]{2,1,0:T(8,128)} %param.6, f32[8,128]{1,0:T(8,128)S(1)} %bitcast.43, f32[1800]{0:T(1024)S(1)} %get-tuple-element.38, f32[8,128]{1,0:T(8,128)S(1)} %bitcast.39, f32[1800]{0:T(1024)S(1)} %get-tuple-element.36, f32[8,128]{1,0:T(8,128)S(1)} %bitcast.36, ...), kind=kLoop, calls=%fused_computation.50 | loop fusion | flops 23961600 | bytes 14797984 | tf_op jit(solution)/shard_map/div | solution.py:51
  129.9 4.9 %collective-permute-start.1 = (f32[1800,1,128]{2,0,1:T(8,128)S(1)}, f32[1800,1,128]{2,0,1:T(8,128)}, u32[]{:S(2)}, u32[]{:S(2)}) collective-permute-start(f32[1800,1,128]{2,0,1:T(8,128)S(1)} %get-tuple-element.31), channel_id=1, source_target_pairs={{1,0},{2,1},{3,2},{4,3},{5,4},{6,5},{7,6},{8,7},{9,8},{10,9},{11,1... | collective-permute-start | bytes 2764808 | tf_op jit(solution)/shard_map/ppermute | solution.py:24
  134.9 18.8 %collective-permute-done = f32[1800,1,128]{2,0,1:T(8,128)S(1)} collective-permute-done((f32[1800,1,128]{2,0,1:T(8,128)S(1)}, f32[1800,1,128]{2,0,1:T(8,128)S(1)}, u32[]{:S(2)}, u32[]{:S(2)}) %collective-permute-start) | collective-permute-done | bytes 921632 | tf_op jit(solution)/shard_map/ppermute | solution.py:21
  153.7 2.1 pad_maximum_fusion
  155.9 7.7 %fusion.76 = (f32[1800,10,1]{2,0,1:T(8,128)}, f32[1800,10,1]{2,0,1:T(8,128)}) fusion(f32[1800,10,128]{2,0,1:T(8,128)S(1)} %pad_maximum_fusion), kind=kLoop, calls=%fused_computation.139 | loop fusion | bytes 288000 | tf_op jit(solution)/shard_map/slice | solution.py:22
  163.6 7.2 %copy.49 = f32[1800,10,1]{0,1,2:T(8,128)S(1)} copy(f32[1800,10,1]{2,0,1:T(8,128)} %get-tuple-element.26) | data formatting | bytes 144000 | tf_op jit(solution)/shard_map/slice | solution.py:22
  172.1 7.2 %copy.51 = f32[1800,10,1]{0,1,2:T(8,128)S(1)} copy(f32[1800,10,1]{2,0,1:T(8,128)} %get-tuple-element.27) | data formatting | bytes 144000 | tf_op jit(solution)/shard_map/slice | solution.py:24
  179.3 1.5 collective-permute-start.3
  180.8 5.2 %copy.50 = f32[1800,10,1]{2,0,1:T(8,128)} copy(f32[1800,10,1]{0,1,2:T(8,128)S(1)} %collective-permute-done.2) | data formatting | bytes 144000 | tf_op jit(solution)/shard_map/ppermute | solution.py:21
  186.0 5.1 %copy.52 = f32[1800,10,1]{2,0,1:T(8,128)} copy(f32[1800,10,1]{0,1,2:T(8,128)S(1)} %collective-permute-done.3) | data formatting | bytes 144000 | tf_op jit(solution)/shard_map/ppermute | solution.py:24
  191.1 28.9 %fusion.81 = f32[1,8,128]{2,0,1:T(1,128)S(1)} fusion(f32[1800,1,1]{0,1,2:T(1,128)S(1)} %reshape.258, f32[1800,8,128]{2,0,1:T(8,128)} %copy-done.1, f32[1800,10,1]{2,0,1:T(8,128)} %copy.52, f32[1800,1,128]{2,0,1:T(8,128)} %collective-permute-done.1, f32[1800,1,128]{2,0,1:T(8,128)} %copy-done.3, f32[1800,10,1]{2,0,1:T(8,128)} %copy.50, ...), kind=kOutput, calls=%fused_computation.144 | convolution fusion | flops 60825600 | bytes 9404192 | tf_op jit(solution)/shard_map/bxy,b->xy/dot_general | solution.py:50
  220.1 13.8 %add_divide_fusion = f32[1800,8,128]{2,0,1:T(8,128)S(1)} fusion(f32[8,128]{1,0:T(8,128)S(1)} %bitcast.52, f32[1800]{0:T(1024)S(1)} %get-tuple-element.38, f32[8,128]{1,0:T(8,128)S(1)} %bitcast.40, f32[1800]{0:T(1024)S(1)} %get-tuple-element.36, f32[8,128]{1,0:T(8,128)S(1)} %bitcast.37, f32[1800]{0:T(1024)S(1)} %get-tuple-element.37, ...), kind=kLoop, calls=%fused_computation.49 | loop fusion | flops 60825600 | bytes 16813984 | tf_op jit(solution)/shard_map/div | solution.py:51
  233.9 3.0 copy-done
  238.0 5.3 %collective-permute-start.5 = (f32[1800,1,128]{2,0,1:T(8,128)S(1)}, f32[1800,1,128]{2,0,1:T(8,128)S(1)}, u32[]{:S(2)}, u32[]{:S(2)}) collective-permute-start(f32[1800,1,128]{2,0,1:T(8,128)S(1)} %get-tuple-element.29), channel_id=1, source_target_pairs={{1,0},{2,1},{3,2},{4,3},{5,4},{6,5},{7,6},{8,7},{9,8},{10,9},{11,1... | collective-permute-start | bytes 2764808 | tf_op jit(solution)/shard_map/ppermute | solution.py:24
  243.7 19.2 %collective-permute-done.4 = f32[1800,1,128]{2,0,1:T(8,128)S(1)} collective-permute-done((f32[1800,1,128]{2,0,1:T(8,128)}, f32[1800,1,128]{2,0,1:T(8,128)S(1)}, u32[]{:S(2)}, u32[]{:S(2)}) %collective-permute-start.4) | collective-permute-done | bytes 921632 | tf_op jit(solution)/shard_map/ppermute | solution.py:21
  262.8 3.5 pad_maximum_fusion.1
  266.3 7.7 %fusion.75 = (f32[1800,10,1]{2,0,1:T(8,128)}, f32[1800,10,1]{2,0,1:T(8,128)}) fusion(f32[1800,10,128]{2,0,1:T(8,128)S(1)} %pad_maximum_fusion.1), kind=kLoop, calls=%fused_computation.138 | loop fusion | bytes 288000 | tf_op jit(solution)/shard_map/slice | solution.py:22
  274.0 7.2 %copy.53 = f32[1800,10,1]{0,1,2:T(8,128)S(1)} copy(f32[1800,10,1]{2,0,1:T(8,128)} %get-tuple-element.24) | data formatting | bytes 144000 | tf_op jit(solution)/shard_map/slice | solution.py:22
  281.2 3.8 collective-permute-start.6
  285.0 7.2 %copy.55 = f32[1800,10,1]{0,1,2:T(8,128)S(1)} copy(f32[1800,10,1]{2,0,1:T(8,128)} %get-tuple-element.25) | data formatting | bytes 144000 | tf_op jit(solution)/shard_map/slice | solution.py:24
  292.2 1.5 collective-permute-start.7
  293.7 5.2 %copy.54 = f32[1800,10,1]{2,0,1:T(8,128)} copy(f32[1800,10,1]{0,1,2:T(8,128)S(1)} %collective-permute-done.6) | data formatting | bytes 144000 | tf_op jit(solution)/shard_map/ppermute | solution.py:21
  298.9 5.1 %copy.56 = f32[1800,10,1]{2,0,1:T(8,128)} copy(f32[1800,10,1]{0,1,2:T(8,128)S(1)} %collective-permute-done.7) | data formatting | bytes 144000 | tf_op jit(solution)/shard_map/ppermute | solution.py:24
  304.0 19.1 %fusion.3 = f32[1800,8,128]{2,0,1:T(8,128)S(1)} fusion(f32[1800,8,128]{2,0,1:T(8,128)} %copy-done, f32[1800,10,1]{2,0,1:T(8,128)} %copy.56, f32[1800,1,128]{2,0,1:T(8,128)S(1)} %collective-permute-done.5, f32[1800,1,128]{2,0,1:T(8,128)S(1)} %collective-permute-done.4, f32[1800,10,1]{2,0,1:T(8,128)} %copy.54, f32[1800]{0:T(1024)S(1)} %get-tuple-element.40, ...), kind=kLoop, calls=%fused_computation.8 | loop fusion | flops 38707200 | bytes 16765696 | tf_op jit(solution)/shard_map/mul | solution.py:93
  323.1 5.6 %fusion.26 = f32[2,8,128]{2,0,1:T(2,128)S(1)} fusion(f32[1800,8,128]{2,0,1:T(8,128)S(1)} %fusion.3, f32[8,128]{1,0:T(8,128)S(1)} %bitcast.41, f32[1800]{0:T(1024)S(1)} %get-tuple-element.36, f32[8,128]{1,0:T(8,128)S(1)} %bitcast.38, f32[1800]{0:T(1024)S(1)} %get-tuple-element.37, f32[1800]{0:T(1024)S(1)} %get-tuple-element.39, f32[1800]{0:T(1024)S(1)} %fusion.71, ...), kind=kOutput, calls=%fused_computation.47 | convolution fusion | flops 58986000 | bytes 7432384 | tf_op jit(solution)/shard_map/bxy,bk->kxy/dot_general | solution.py:94
  329.0 8.5 %scatter_custom_fusion = f32[4,8192]{0,1:T(8,128)} fusion(s32[1024]{0:T(1024)S(1)} %bitcast.53, f32[1024,4]{1,0:T(8,128)S(1)} %copy.58, f32[]{:T(128)} %constant.83.clone.1), kind=kCustom, calls=%fused_computation.63 | custom fusion | flops 4096 | bytes 131076 | tf_op jit(solution)/shard_map/scatter-add | solution.py:102
  337.6 10.6 %copy.59 = f32[1800,8,128]{2,1,0:T(8,128)} copy(f32[1800,8,128]{2,0,1:T(8,128)} %copy-done.2) | data formatting | bytes 14745600
  348.1 72.3 %reduce-scatter.2.cloned.1.call-done = f32[4,512]{0,1:T(8,128)} async-done(((f32[4,8192]{0,1:T(8,128)}), f32[4,512]{0,1:T(8,128)}) %reduce-scatter.2.cloned.1.call-update) | async-done | bytes 8208 | tf_op jit(solution)/shard_map/reduce_scatter | solution.py:104
  420.5 1.7 fusion.42
  (58 shorter events, 8.8 us)
Async XLA Ops:
  7.2 413.3 %reduce-scatter.2.cloned.1.call-start = ((), (), s32[]{:S(2)}) async-start(), calls=%async_computation.1 | async-start | bytes 4456448 | tf_op jit(solution)/shard_map/reduce_scatter | solution.py:104
  9.1 104.2 %copy-start.5 = (s32[8,128]{1,0:T(8,128)S(1)}, s32[8,128]{1,0:T(8,128)}, u32[]{:S(2)}) copy-start(s32[8,128]{1,0:T(8,128)} %param.7) | copy-start | bytes 12292
  129.3 26.6 %copy-start.1 = (f32[1800,8,128]{2,0,1:T(8,128)}, f32[1800,8,128]{2,0,1:T(8,128)S(1)}, u32[]{:S(2)}) copy-start(f32[1800,8,128]{2,0,1:T(8,128)S(1)} %add_divide_fusion.1) | copy-start | bytes 22118404
  129.4 24.3 %collective-permute-start = (f32[1800,1,128]{2,0,1:T(8,128)S(1)}, f32[1800,1,128]{2,0,1:T(8,128)S(1)}, u32[]{:S(2)}, u32[]{:S(2)}) collective-permute-start(f32[1800,1,128]{2,0,1:T(8,128)S(1)} %get-tuple-element.30), channel_id=1, source_target_pairs={{0,1},{1,2},{2,3},{3,4},{4,5},{5,6},{6,7},{7,8},{8,9},{9,10},{10,1... | collective-permute-start | bytes 2764808 | tf_op jit(solution)/shard_map/ppermute | solution.py:21
  129.9 23.8 %collective-permute-start.1 = (f32[1800,1,128]{2,0,1:T(8,128)S(1)}, f32[1800,1,128]{2,0,1:T(8,128)}, u32[]{:S(2)}, u32[]{:S(2)}) collective-permute-start(f32[1800,1,128]{2,0,1:T(8,128)S(1)} %get-tuple-element.31), channel_id=1, source_target_pairs={{1,0},{2,1},{3,2},{4,3},{5,4},{6,5},{7,6},{8,7},{9,8},{10,9},{11,1... | collective-permute-start | bytes 2764808 | tf_op jit(solution)/shard_map/ppermute | solution.py:24
  153.7 2.1 copy-start.3
  170.8 10.0 %collective-permute-start.2 = (f32[1800,10,1]{0,1,2:T(8,128)S(1)}, f32[1800,10,1]{0,1,2:T(8,128)S(1)}, u32[]{:S(2)}, u32[]{:S(2)}) collective-permute-start(f32[1800,10,1]{0,1,2:T(8,128)S(1)} %copy.49), channel_id=1, source_target_pairs={{0,16},{16,32},{32,48},{48,64},{64,80},{80,96},{96,112},{1,17},{17... | collective-permute-start | bytes 216008 | tf_op jit(solution)/shard_map/ppermute | solution.py:21
  179.3 6.7 %collective-permute-start.3 = (f32[1800,10,1]{0,1,2:T(8,128)S(1)}, f32[1800,10,1]{0,1,2:T(8,128)S(1)}, u32[]{:S(2)}, u32[]{:S(2)}) collective-permute-start(f32[1800,10,1]{0,1,2:T(8,128)S(1)} %copy.51), channel_id=1, source_target_pairs={{16,0},{32,16},{48,32},{64,48},{80,64},{96,80},{112,96},{17,1},{33... | collective-permute-start | bytes 216008 | tf_op jit(solution)/shard_map/ppermute | solution.py:24
  186.0 34.0 %slice-start = ((s8[7372800]{0:T(1024)(128)(4,1)}), s8[3178496]{0:T(1024)(128)(4,1)S(1)}, s32[]{:S(2)}) async-start(s8[7372800]{0:T(1024)(128)(4,1)} %bitcast.34), calls=%async_computation.2 | async-start | bytes 6356992
  191.1 28.9 %slice-start.1 = ((s8[7372800]{0:T(1024)(128)(4,1)}), s8[4194304]{0:T(1024)(128)(4,1)S(1)}, s32[]{:S(2)}) async-start(s8[7372800]{0:T(1024)(128)(4,1)} %bitcast.34), calls=%async_computation.3 | async-start | bytes 8388608
  191.1 28.9 %copy-start.4 = (f32[1800,1,128]{2,0,1:T(8,128)S(1)}, f32[1800,1,128]{2,0,1:T(8,128)}, u32[]{:S(2)}) copy-start(f32[1800,1,128]{2,0,1:T(8,128)} %copy-done.3) | copy-start | bytes 2764804
  220.1 23.3 %copy-start.6 = (s32[8,128]{1,0:T(8,128)S(1)}, s32[8,128]{1,0:T(8,128)}, u32[]{:S(2)}) copy-start(s32[8,128]{1,0:T(8,128)} %param.10) | copy-start | bytes 12292
  220.1 23.6 %copy-start.7 = (s32[8,128]{1,0:T(8,128)S(1)}, s32[8,128]{1,0:T(8,128)}, u32[]{:S(2)}) copy-start(s32[8,128]{1,0:T(8,128)} %param.11) | copy-start | bytes 12292
  233.9 3.1 copy-start
  238.0 24.8 %collective-permute-start.4 = (f32[1800,1,128]{2,0,1:T(8,128)}, f32[1800,1,128]{2,0,1:T(8,128)S(1)}, u32[]{:S(2)}, u32[]{:S(2)}) collective-permute-start(f32[1800,1,128]{2,0,1:T(8,128)} %get-tuple-element.28), channel_id=1, source_target_pairs={{0,1},{1,2},{2,3},{3,4},{4,5},{5,6},{6,7},{7,8},{8,9},{9,10},{10,1... | collective-permute-start | bytes 2764808 | tf_op jit(solution)/shard_map/ppermute | solution.py:21
  238.0 24.8 %collective-permute-start.5 = (f32[1800,1,128]{2,0,1:T(8,128)S(1)}, f32[1800,1,128]{2,0,1:T(8,128)S(1)}, u32[]{:S(2)}, u32[]{:S(2)}) collective-permute-start(f32[1800,1,128]{2,0,1:T(8,128)S(1)} %get-tuple-element.29), channel_id=1, source_target_pairs={{1,0},{2,1},{3,2},{4,3},{5,4},{6,5},{7,6},{8,7},{9,8},{10,9},{11,1... | collective-permute-start | bytes 2764808 | tf_op jit(solution)/shard_map/ppermute | solution.py:24
  281.2 12.5 %collective-permute-start.6 = (f32[1800,10,1]{0,1,2:T(8,128)S(1)}, f32[1800,10,1]{0,1,2:T(8,128)S(1)}, u32[]{:S(2)}, u32[]{:S(2)}) collective-permute-start(f32[1800,10,1]{0,1,2:T(8,128)S(1)} %copy.53), channel_id=1, source_target_pairs={{0,16},{16,32},{32,48},{48,64},{64,80},{80,96},{96,112},{1,17},{17... | collective-permute-start | bytes 216008 | tf_op jit(solution)/shard_map/ppermute | solution.py:21
  292.2 6.7 %collective-permute-start.7 = (f32[1800,10,1]{0,1,2:T(8,128)S(1)}, f32[1800,10,1]{0,1,2:T(8,128)S(1)}, u32[]{:S(2)}, u32[]{:S(2)}) collective-permute-start(f32[1800,10,1]{0,1,2:T(8,128)S(1)} %copy.55), channel_id=1, source_target_pairs={{16,0},{32,16},{48,32},{64,48},{80,64},{96,80},{112,96},{17,1},{33... | collective-permute-start | bytes 216008 | tf_op jit(solution)/shard_map/ppermute | solution.py:24
  323.1 5.6 %copy-start.2 = (f32[1800,8,128]{2,0,1:T(8,128)}, f32[1800,8,128]{2,0,1:T(8,128)S(1)}, u32[]{:S(2)}) copy-start(f32[1800,8,128]{2,0,1:T(8,128)S(1)} %fusion.3) | copy-start | bytes 22118404
Sparse Core Ops, SparseCore 0:
  337.7 82.7 reduce-scatter.1
where the time goes:
time: 440 us; the launch traced here: 432 us
  waiting for transfers between devices  110 us (25%)
  blocking collectives  94.9 us (22%)
  local copies, waits for them, and re-layouts  90.7 us (21%)
  other arithmetic  59.2 us (13%)
  matrix products  43.1 us (10%)
  starting transfers between devices  18.8 us (4%)
  between operations  14.9 us (3%)
    all_gather x1, blocking collectives, body(): fetched = lax.all_gather(atm_wind, 'lon', axis=1, tiled=True)  94.9 us
    reduce_scatter x1, waiting for transfers between devices, body(): lax.psum_scatter(partial_cells, 'lon', scatter_dimension=1, tiled=True)  72.3 us
    ppermute x4, waiting for transfers between devices, extended(): lax.ppermute(lax.slice_in_dim(block, block.shape[dim] - width, None, axis...  38 us
    dot_general x2, matrix products, force_terms(): jnp.einsum('bxy,b->xy', energy, slope_b, precision=lax.Precision.HIGHEST)  37.5 us
    slice x6, local copies, waits for them, and re-layouts, extended(): lax.slice_in_dim(block, block.shape[dim] - width, None, axis=dim)  31 us
    div x2, other arithmetic, force_terms(): energy * (1.0 + rate_in) / (1.0 + 4.0 * freq_b[:, None, None] * msq[None])  21.1 us
    mul x1, other arithmetic, body(): energy = advect(padded, cx_b, cy_b) * maskf[None]  19.1 us
    unnamed x23, local copies, waits for them, and re-layouts  15.4 us
  transfers between devices with their start and end apart: 9, of which 3 were waited for; matrix products, arithmetic and copies ran while one was open for 8% of the time, Pallas kernels for 0%

commit v1 on v0

v1 whole, which is shorter than its diff:
```python
import functools
import math

import jax
import jax.numpy as jnp
import numpy as np
from jax import lax
from jax.experimental import pallas as pl
from jax.experimental.pallas import tpu as pltpu
from jax.sharding import PartitionSpec as P

NF = 50
ND = 36
HALF = 18
QUAD = 9
GROUPS = 10
FG = NF // GROUPS
GB = FG * ND
COL = 904
F32 = jnp.float32
BF16 = jnp.bfloat16

_f = np.arange(NF, dtype=np.float64)
_freq = 1.07 ** (_f - (NF - 1))
_theta = 2.0 * math.pi * (np.arange(ND) + 0.5) / ND
_cos = np.cos(_theta)
_sin = np.sin(_theta)
_gain = 0.6 * _freq**2
_base = 1.0 - 0.2 * _freq
_cour = 0.7 * (3.0 / 7.0) ** (_f / (NF - 1))
_slope = 250.0 * _freq**4 / ND
_four = 4.0 * _freq
_push = 800.0 * _freq**2 / ND
EASTWARD = list(range(0, 9)) + list(range(27, 36))
WESTWARD = list(range(9, 27))

SCAL = np.zeros((6, 64), np.float32)
for _i, _t in enumerate((_gain, _base, _cour, _slope, _four, _push)):
    SCAL[_i, :NF] = _t
SCAL = SCAL.reshape(-1)


def scal(sm, kind, f):
    return sm[kind * 64 + f]


def _lane_tables():
    tab = np.zeros((GROUPS, 8, 128), np.float32)
    tab[:, 1] = 1.0
    for g in range(GROUPS):
        for i in range(FG):
            f = g * FG + i
            for d in range(HALF):
                j = i * HALF + d
                tab[g, 0, j] = _gain[f]
                tab[g, 1, j] = _base[f]
                tab[g, 2, j] = _cos[d]
                tab[g, 3, j] = _sin[d]
                tab[g, 4, j] = _four[f]
    return tab


def _dir_tables():
    tab = np.zeros((4, HALF, 128), np.float32)
    for s, dirs in enumerate((EASTWARD, WESTWARD)):
        tab[2 * s] = _cos[dirs][:, None]
        tab[2 * s + 1] = _sin[dirs][:, None]
    return tab


LANE_TAB = _lane_tables()
DIR_TAB = _dir_tables()
FOUR_COL = np.broadcast_to(_four[:, None], (NF, 128)).astype(np.float32)


def quartets():
    for d in range(QUAD):
        yield (d, 17 - d, 18 + d, 35 - d)


def iota(shape, dim):
    return lax.broadcasted_iota(jnp.int32, shape, dim)


def pack_edges(ref, g, lane):
    edge_n = jnp.zeros((8, 128), F32)
    edge_s = jnp.zeros((8, 128), F32)
    for i in range(FG):
        for d in range(HALF):
            j = i * HALF + d
            e = ref[g * GB + i * ND + d]
            edge_n = jnp.where(lane == j, pltpu.roll(e, (j - 127) % 128, 1), edge_n)
            e = ref[g * GB + i * ND + HALF + d]
            edge_s = jnp.where(lane == j, pltpu.roll(e, j, 1) if j else e, edge_s)
    return edge_n, edge_s


def first_kernel(sm, spec_hbm, mask, wrow, spec, to_west, to_east, north, south, msq, sems):
    lane = iota((8, 128), 1)

    def copy(g):
        at = pl.ds(g * GB, GB)
        return pltpu.make_async_copy(spec_hbm.at[at], spec.at[at], sems.at[g])

    for g in range(GROUPS):
        copy(g).start()
    msq[...] = jnp.zeros_like(msq)

    @pl.loop(0, GROUPS)
    def _(g):
        copy(g).wait()
        total = jnp.zeros((8, 128), F32)
        for i in range(FG):
            acc = jnp.zeros((8, 128), F32)
            for d in range(ND):
                e = spec[g * GB + i * ND + d]
                acc = acc + e
                if d in WESTWARD:
                    k = i * HALF + WESTWARD.index(d)
                    for c in range(2):
                        to_west[pl.ds(c * COL + g * FG * HALF + k, 1), :] = e[c : c + 1]
                else:
                    k = i * HALF + EASTWARD.index(d)
                    for c in range(2):
                        to_east[pl.ds(c * COL + g * FG * HALF + k, 1), :] = e[6 + c : 7 + c]
            total = total + scal(sm, 3, g * FG + i) * acc
        msq[...] += total
        north[g], south[g] = pack_edges(spec, g, lane)

    maskf = mask[...].astype(F32)
    msq[...] = msq[...] * maskf
    rows = (msq[...], maskf, wrow[...].astype(F32))
    for c in range(2):
        for r, val in enumerate(rows):
            at = c * COL + 2 * GROUPS * FG * QUAD + r
            to_west[at : at + 1, :] = val[c : c + 1]
            to_east[at : at + 1, :] = val[6 + c : 7 + c]


SMEM = pl.BlockSpec(memory_space=pltpu.SMEM)
VMEM = pl.BlockSpec(memory_space=pltpu.VMEM)
ANY = pl.BlockSpec(memory_space=pl.ANY)
TILE = jax.ShapeDtypeStruct((8, 128), F32)
FIELD = jax.ShapeDtypeStruct((NF * ND, 8, 128), F32)
PARAMS = pltpu.CompilerParams(vmem_limit_bytes=56 * 2**20)


def first_call(spectra, mask, wrow):
    return pl.pallas_call(
        first_kernel,
        in_specs=[SMEM, ANY, VMEM, VMEM],
        out_specs=[VMEM] * 6,
        out_shape=[
            FIELD,
            jax.ShapeDtypeStruct((2 * COL, 128), F32),
            jax.ShapeDtypeStruct((2 * COL, 128), F32),
            jax.ShapeDtypeStruct((GROUPS, 8, 128), F32),
            jax.ShapeDtypeStruct((GROUPS, 8, 128), F32),
            TILE,
        ],
        scratch_shapes=[pltpu.SemaphoreType.DMA((GROUPS,))],
        compiler_params=PARAMS,
        name="first",
    )(jnp.asarray(SCAL), spectra, mask, wrow)


def split3(x):
    a = x.astype(BF16)
    r = x - a.astype(F32)
    b = r.astype(BF16)
    c = (r - b.astype(F32)).astype(BF16)
    return a, b, c


def wind_kernel(
    sm, table, wrow, msq, mask, west, east, north, south, lane_tab, dir_tab, four,
    u_ref, v_ref, side_ref, hx_w, hx_e, hp_w, hp_e, fn, fs,
):
    srcs, _, trows, _ = table.shape
    hi_count = srcs * trows
    rows = [wrow[x : x + 1, :] for x in range(8)]
    at = 2 * GROUPS * FG * QUAD
    for ref in (west, east):
        for c in range(2):
            rows.append(ref[c * COL + at + 2 : c * COL + at + 3, :].astype(jnp.int32))
    local = [r & (hi_count * 128 - 1) for r in rows]
    hi_iota = iota((hi_count, 128), 0)
    hot = jnp.concatenate(
        [jnp.where(hi_iota == (r // 128), 1.0, 0.0).astype(BF16) for r in local], axis=1
    )
    tab = jnp.concatenate(
        [table[:, c].reshape(hi_count, 128) for c in range(2)], axis=1
    )
    got = None
    for part in split3(tab):
        term = lax.dot_general(
            part, hot, (((0,), (0,)), ((), ())), preferred_element_type=F32
        )
        got = term if got is None else got + term
    lo_iota = iota((128, 128), 0)
    us, vs = [], []
    for n, r in enumerate(local):
        pick = lo_iota == (r & 127)
        us.append(jnp.sum(jnp.where(pick, got[0:128, n * 128 : n * 128 + 128], 0.0), axis=0, keepdims=True))
        vs.append(jnp.sum(jnp.where(pick, got[128:256, n * 128 : n * 128 + 128], 0.0), axis=0, keepdims=True))
    for x in range(8):
        u_ref[x : x + 1, :] = us[x]
        v_ref[x : x + 1, :] = vs[x]
    side_ref[0:1, :] = us[9]
    side_ref[1:2, :] = vs[9]
    side_ref[2:3, :] = west[COL + at + 1 : COL + at + 2, :]
    side_ref[3:4, :] = us[10]
    side_ref[4:5, :] = vs[10]
    side_ref[5:6, :] = east[at + 1 : at + 2, :]
    side_ref[6:8, :] = jnp.zeros((2, 128), F32)

    maskf = mask[...].astype(F32)
    for edge, out, lane, sign in ((north, fn, 127, 1.0), (south, fs, 0, -1.0)):
        pick = lambda a: jnp.broadcast_to(a[:, lane : lane + 1], (8, 128))
        ue, ve, me, qe = pick(u_ref[...]), pick(v_ref[...]), pick(maskf), pick(msq[...])
        for g in range(GROUPS):
            lt = lane_tab[g]
            along = sign * (lt[2:3] * ue + lt[3:4] * ve)
            t = jnp.maximum(lt[0:1] * along + lt[1:2], 1.0)
            out[g * 8 : g * 8 + 8, :] = edge[g] * t * (me / (1.0 + lt[4:5] * qe))

    row18 = iota((HALF, 128), 0)
    lane18 = iota((HALF, 128), 1)
    up = row18 < QUAD
    inner = lane18 != jnp.where(up, 0, 127)
    acc = {}
    for s, (ref, near, far, hx, hp) in enumerate(
        ((west, COL, 0, hx_w, hp_w), (east, 0, COL, hx_e, hp_e))
    ):
        cos = dir_tab[2 * s]
        sin = dir_tab[2 * s + 1]
        n_near, n_far = (9, 8) if s == 0 else (10, 11)
        al_near = cos * us[n_near] + sin * vs[n_near]
        al_far = cos * us[n_far] + sin * vs[n_far]
        fac = []
        for base in (near, far):
            q = ref[base + at : base + at + 1, :]
            m = ref[base + at + 1 : base + at + 2, :]
            fac.append(m / (1.0 + four[...] * q))
        acos = jnp.abs(cos)
        asin = jnp.abs(sin)
        for f in range(NF):
            a, b, cr = scal(sm, 0, f), scal(sm, 1, f), scal(sm, 2, f)
            g1 = ref[near + f * HALF : near + f * HALF + HALF, :]
            g2 = ref[far + f * HALF : far + f * HALF + HALF, :]
            g1 = g1 * jnp.maximum(a * al_near + b, 1.0) * fac[0][f : f + 1]
            g2 = g2 * jnp.maximum(a * al_far + b, 1.0) * fac[1][f : f + 1]
            hx[f] = g1
            kx = cr * acos
            ky = cr * asin
            rolled = jnp.where(up, pltpu.roll(g1, 1, 1), pltpu.roll(g1, 127, 1))
            hp[f] = (1.0 - kx - ky) * g1 + kx * g2 + jnp.where(inner, ky * rolled, 0.0)
            grp, i = f // FG, f % FG
            shift_n = i * HALF + (0 if s == 0 else QUAD)
            shift_s = i * HALF + (0 if s == 0 else -QUAD)
            cn = jnp.broadcast_to(g1[:, 127:128], (HALF, 128))
            cs = jnp.broadcast_to(g1[:, 0:1], (HALF, 128))
            cn = jnp.where(up & (lane18 == row18 + shift_n), cn, 0.0)
            cs = jnp.where(jnp.logical_not(up) & (lane18 == row18 + shift_s), cs, 0.0)
            for key, val in (("n", cn), ("s", cs)):
                have = acc.get((key, grp))
                acc[(key, grp)] = val if have is None else have + val
    for key, out in (("n", fn), ("s", fs)):
        for grp in range(GROUPS):
            out[80 + grp : 81 + grp, :] = jnp.sum(acc[(key, grp)], axis=0, keepdims=True)
        out[90:96, :] = jnp.zeros((6, 128), F32)


def wind_call(table, wrow, msq, mask, west, east, north, south):
    vmem = pl.BlockSpec(memory_space=pltpu.VMEM)
    halo = jax.ShapeDtypeStruct((NF, HALF, 128), F32)
    tile = jax.ShapeDtypeStruct((8, 128), F32)
    edge = jax.ShapeDtypeStruct((96, 128), F32)
    return pl.pallas_call(
        wind_kernel,
        in_specs=[pl.BlockSpec(memory_space=pltpu.SMEM)] + [vmem] * 11,
        out_specs=[vmem] * 9,
        out_shape=[tile, tile, tile, halo, halo, halo, halo, edge, edge],
        compiler_params=PARAMS,
        name="winds",
    )(
        jnp.asarray(SCAL), table, wrow, msq, mask, west, east, north, south,
        jnp.asarray(LANE_TAB), jnp.asarray(DIR_TAB), jnp.asarray(FOUR_COL),
    )


def along_table(along, u, v):
    for d in range(ND):
        along[d] = float(_cos[d]) * u + float(_sin[d]) * v


def shifted(gv, d, j, sub, lane, hx_w, hx_e, i, scale, halo_n, halo_s):
    if d in WESTWARD:
        k = WESTWARD.index(d)
        row = hx_e[i, k : k + 1, :]
        row = jnp.broadcast_to(row if scale is None else row * scale[1], (8, 128))
        xs = jnp.where(sub == 7, row, pltpu.roll(gv, 7, 0))
    else:
        k = EASTWARD.index(d)
        row = hx_w[i, k : k + 1, :]
        row = jnp.broadcast_to(row if scale is None else row * scale[0], (8, 128))
        xs = jnp.where(sub == 0, row, pltpu.roll(gv, 1, 0))
    if d < HALF:
        halo = pltpu.roll(halo_n, (-j) % 128, 1) if j else halo_n
        ys = jnp.where(lane == 0, halo, pltpu.roll(gv, 1, 1))
    else:
        halo = pltpu.roll(halo_s, 127 - j, 1)
        ys = jnp.where(lane == 127, halo, pltpu.roll(gv, 127, 1))
    return xs, ys


def step_one_kernel(
    sm, spec, u, v, msq, mask, hx_w, hx_e, rn, rs, lane_tab,
    out, msq2, fn2, fs2, along, edges_n, edges_s,
):
    lane = iota((8, 128), 1)
    sub = iota((8, 128), 0)
    maskf = mask[...].astype(F32)
    along_table(along, u[...], v[...])
    msq2[...] = jnp.zeros_like(msq2)

    @pl.loop(0, GROUPS)
    def _(g):
        total = jnp.zeros((8, 128), F32)
        at = pl.ds(pl.multiple_of(g * 8, 8), 8)
        halo_n = rn[at, :]
        halo_s = rs[at, :]
        for i in range(FG):
            f = g * FG + i
            a, b, cr = scal(sm, 0, f), scal(sm, 1, f), scal(sm, 2, f)
            fac = maskf / (1.0 + scal(sm, 4, f) * msq[...])
            acc = jnp.zeros((8, 128), F32)
            for quartet in quartets():
                d0 = quartet[0]
                kx = cr * float(abs(_cos[d0]))
                ky = cr * float(abs(_sin[d0]))
                k0 = 1.0 - kx - ky
                for d in quartet:
                    j = i * HALF + d % HALF
                    gv = spec[f * ND + d] * jnp.maximum(a * along[d] + b, 1.0) * fac
                    xs, ys = shifted(gv, d, j, sub, lane, hx_w, hx_e, f, None, halo_n, halo_s)
                    e = k0 * gv + kx * xs + ky * ys
                    out[f * ND + d] = e
                    acc = acc + e
            total = total + scal(sm, 3, f) * acc
        msq2[...] += total

    @pl.loop(0, GROUPS)
    def _(g):
        edges_n[g], edges_s[g] = pack_edges(out, g, lane)

    msq2[...] = msq2[...] * maskf
    for edge, dst, at, sign in ((edges_n, fn2, 127, 1.0), (edges_s, fs2, 0, -1.0)):
        pick = lambda z: jnp.broadcast_to(z[:, at : at + 1], (8, 128))
        ue, ve, me, qe = pick(u[...]), pick(v[...]), pick(maskf), pick(msq2[...])
        for q in range(GROUPS):
            lt = lane_tab[q]
            al = sign * (lt[2:3] * ue + lt[3:4] * ve)
            t = jnp.maximum(lt[0:1] * al + lt[1:2], 1.0)
            dst[q * 8 : q * 8 + 8, :] = edge[q] * t * (me / (1.0 + lt[4:5] * qe))


def step_one_call(spectra, u, v, msq, mask, hx_w, hx_e, rn, rs):
    return pl.pallas_call(
        step_one_kernel,
        in_specs=[SMEM] + [VMEM] * 10,
        out_specs=[VMEM] * 4,
        out_shape=[
            FIELD,
            TILE,
            jax.ShapeDtypeStruct((80, 128), F32),
            jax.ShapeDtypeStruct((80, 128), F32),
        ],
        scratch_shapes=[
            pltpu.VMEM((ND, 8, 128), F32),
            pltpu.VMEM((GROUPS, 8, 128), F32),
            pltpu.VMEM((GROUPS, 8, 128), F32),
        ],
        compiler_params=PARAMS,
        name="step_one",
    )(jnp.asarray(SCAL), spectra, u, v, msq, mask, hx_w, hx_e, rn, rs, jnp.asarray(LANE_TAB))


def halo_kernel(sm, hp_w, hp_e, rn, rs, side, dir_tab, hq_w, hq_e):
    row18 = iota((HALF, 128), 0)
    lane18 = iota((HALF, 128), 1)
    up = row18 < QUAD
    place = lane18 == jnp.where(up, 0, 127)
    for s, (hp, hq) in enumerate(((hp_w, hq_w), (hp_e, hq_e))):
        cos = dir_tab[2 * s]
        sin = dir_tab[2 * s + 1]
        asin = jnp.abs(sin)
        along = cos * side[3 * s : 3 * s + 1, :] + sin * side[3 * s + 1 : 3 * s + 2, :]
        for f in range(NF):
            a, b, cr = scal(sm, 0, f), scal(sm, 1, f), scal(sm, 2, f)
            grp, i = f // FG, f % FG
            shift = jnp.where(up, i * HALF + (0 if s == 0 else QUAD), i * HALF + (0 if s == 0 else -QUAD))
            src = jnp.where(up, rn[80 + grp : 81 + grp, :], rs[80 + grp : 81 + grp, :])
            col = jnp.sum(jnp.where(lane18 == row18 + shift, src, 0.0), axis=1, keepdims=True)
            e = hp[f] + jnp.where(place, (cr * asin) * col, 0.0)
            hq[f] = e * jnp.maximum(a * along + b, 1.0)


def halo_call(hp_w, hp_e, rn, rs, side):
    vmem = pl.BlockSpec(memory_space=pltpu.VMEM)
    halo = jax.ShapeDtypeStruct((NF, HALF, 128), F32)
    return pl.pallas_call(
        halo_kernel,
        in_specs=[pl.BlockSpec(memory_space=pltpu.SMEM)] + [vmem] * 6,
        out_specs=[vmem] * 2,
        out_shape=[halo, halo],
        compiler_params=PARAMS,
        name="halo_columns",
    )(jnp.asarray(SCAL), hp_w, hp_e, rn, rs, side, jnp.asarray(DIR_TAB))


def step_two_kernel(
    sm, spec, u, v, msq, mask, msq_w, msq_e, side, hq_w, hq_e, rn, rs, owner, weight,
    out, cells, along, push, field, sems,
):
    lane = iota((8, 128), 1)
    sub = iota((8, 128), 0)
    maskf = mask[...].astype(F32)
    along_table(along, u[...], v[...])
    push[...] = jnp.zeros_like(push)

    def copy(g):
        at = pl.ds(g * GB, GB)
        return pltpu.make_async_copy(field.at[at], out.at[at], sems.at[g])

    @pl.loop(0, GROUPS)
    def _(g):
        pu = jnp.zeros((8, 128), F32)
        pv = jnp.zeros((8, 128), F32)
        at = pl.ds(pl.multiple_of(g * 8, 8), 8)
        halo_n = rn[at, :]
        halo_s = rs[at, :]
        for i in range(FG):
            f = g * FG + i
            a, b, cr, four = scal(sm, 0, f), scal(sm, 1, f), scal(sm, 2, f), scal(sm, 4, f)
            fac = maskf / (1.0 + four * msq[...])
            scale = (
                side[2:3, :] / (1.0 + four * msq_w[7:8, :]),
                side[5:6, :] / (1.0 + four * msq_e[0:1, :]),
            )
            fu = jnp.zeros((8, 128), F32)
            fv = jnp.zeros((8, 128), F32)
            for quartet in quartets():
                d0 = quartet[0]
                kx = cr * float(abs(_cos[d0]))
                ky = cr * float(abs(_sin[d0]))
                k0 = 1.0 - kx - ky
                q = []
                for d in quartet:
                    j = i * HALF + d % HALF
                    t = jnp.maximum(a * along[d] + b, 1.0)
                    gv = spec[f * ND + d] * t * fac
                    xs, ys = shifted(gv, d, j, sub, lane, hq_w, hq_e, f, scale, halo_n, halo_s)
                    e = (k0 * gv + kx * xs + ky * ys) * maskf
                    field[f * ND + d] = e
                    q.append((t - 1.0) * e)
                lo = q[0] - q[2]
                hi = q[1] - q[3]
                fu = fu + float(_cos[d0]) * (lo - hi)
                fv = fv + float(_sin[d0]) * (lo + hi)
            pu = pu + scal(sm, 5, f) * fu
            pv = pv + scal(sm, 5, f) * fv
        push[0] += pu
        push[1] += pv
        copy(g).start()

    def finish():
        uu, vv = u[...], v[...]
        share = weight[...].astype(F32) * maskf
        tau = 0.02 * (uu * uu + vv * vv) + 0.25
        terms = (share, share * tau, share * push[0], share * push[1])
        parts = [split3(t) for t in terms]
        dests = cells.shape[0]
        own = owner[...] & (dests * 512 - 1)
        hi_own = own // 128
        lo_own = own & 127
        row = iota((dests * 16, 128), 0)
        want = (row // 16) * 4 + row % 4
        lo_iota = iota((128, 128), 0)
        kind = iota((16, 128), 0) // 4
        total = jnp.zeros((dests * 16, 128), F32)
        for x in range(8):
            hot = jnp.where(lo_iota == lo_own[x : x + 1], 1.0, 0.0).astype(BF16)
            match = want == hi_own[x : x + 1]
            for p in range(3):
                rows = [parts[k][p][x : x + 1].astype(F32) for k in range(4)]
                tile = jnp.where(
                    kind == 0, rows[0],
                    jnp.where(kind == 1, rows[1], jnp.where(kind == 2, rows[2], rows[3])),
                )
                lhs = jnp.where(match, jnp.concatenate([tile] * dests, axis=0), 0.0).astype(BF16)
                total = total + lax.dot_general(
                    lhs, hot, (((1,), (1,)), ((), ())), preferred_element_type=F32
                )
        cells[...] = total.reshape(dests, 16, 128)

    finish()
    for g in range(GROUPS):
        copy(g).wait()


def step_two_call(spec, u, v, msq, mask, msq_w, msq_e, side, hq_w, hq_e, rn, rs, owner, weight, dests):
    return pl.pallas_call(
        step_two_kernel,
        in_specs=[SMEM] + [VMEM] * 14,
        out_specs=[ANY, VMEM],
        out_shape=[FIELD, jax.ShapeDtypeStruct((dests, 16, 128), F32)],
        scratch_shapes=[
            pltpu.VMEM((ND, 8, 128), F32),
            pltpu.VMEM((2, 8, 128), F32),
            pltpu.VMEM((NF * ND, 8, 128), F32),
            pltpu.SemaphoreType.DMA((GROUPS,)),
        ],
        compiler_params=PARAMS,
        name="step_two",
    )(
        jnp.asarray(SCAL), spec, u, v, msq, mask, msq_w, msq_e, side, hq_w, hq_e, rn, rs,
        owner, weight,
    )


def cell_kernel(parts, stress, rough):
    sums = jnp.sum(parts[...], axis=0)
    w, a, bx, by = (sums[4 * k : 4 * k + 4] for k in range(4))
    total_w = jnp.maximum(w, 1.0)
    sx = bx / total_w
    sy = by / total_w
    low = jnp.maximum(a, 1.0)
    r = jnp.sqrt(1.0 + (bx * bx + by * by) / (low * low)) * a / total_w
    for n in range(4):
        at = slice(n * 128, n * 128 + 128)
        stress[0:1, at] = sx[n : n + 1]
        stress[1:2, at] = sy[n : n + 1]
        rough[0:1, at] = r[n : n + 1]


def cell_call(parts):
    return pl.pallas_call(
        cell_kernel,
        out_shape=[jax.ShapeDtypeStruct((2, 512), F32), jax.ShapeDtypeStruct((1, 512), F32)],
        name="cells",
    )(parts)


def body(spectra, sea_mask, atm_wind, wind_row, owner, weight):
    lons = lax.axis_size("lon")
    lats = lax.axis_size("lat")
    eastward = [(i, (i + 1) % lons) for i in range(lons)]
    westward = [(i, (i - 1) % lons) for i in range(lons)]
    northward = [(i, i + 1) for i in range(lats - 1)]
    southward = [(i + 1, i) for i in range(lats - 1)]

    spectra, to_west, to_east, north, south, msq1 = first_call(spectra, sea_mask, wind_row)
    from_west = lax.ppermute(to_east, "lon", eastward)
    from_east = lax.ppermute(to_west, "lon", westward)
    rows = atm_wind.reshape(1, 2, 16, 128)
    table = lax.all_to_all(jnp.broadcast_to(rows, (lons, 2, 16, 128)), "lon", 0, 0)
    u, v, side, hx_w, hx_e, hp_w, hp_e, fn, fs = wind_call(
        table, wind_row, msq1, sea_mask, from_west, from_east, north, south
    )
    rn = lax.ppermute(fn, "lat", northward)
    rs = lax.ppermute(fs, "lat", southward)
    energy, msq2, fn2, fs2 = step_one_call(
        spectra, u, v, msq1, sea_mask, hx_w, hx_e, rn, rs
    )
    rn2 = lax.ppermute(fn2, "lat", northward)
    rs2 = lax.ppermute(fs2, "lat", southward)
    msq_w = lax.ppermute(msq2, "lon", eastward)
    msq_e = lax.ppermute(msq2, "lon", westward)
    hq_w, hq_e = halo_call(hp_w, hp_e, rn, rs, side)
    energy, cells = step_two_call(
        energy, u, v, msq2, sea_mask, msq_w, msq_e, side, hq_w, hq_e, rn2, rs2,
        owner, weight, lons,
    )
    parts = lax.all_to_all(cells, "lon", 0, 0)
    stress, rough = cell_call(parts)
    return energy, stress, rough.reshape(512)


def solution(mesh):
    in_specs = (
        P(None, "lon", "lat"),
        P("lon", "lat"),
        P(None, ("lat", "lon")),
        P("lon", "lat"),
        P("lon", "lat"),
        P("lon", "lat"),
    )
    out_specs = (P(None, "lon", "lat"), P(None, ("lat", "lon")), P(("lat", "lon")))
    return jax.shard_map(body, mesh=mesh, in_specs=in_specs, out_specs=out_specs, check_vma=False)
```

time: 440 us -> 113 us (0.26)
  the two profiles are of different devices: /device:TPU:0 before, /device:TPU:1 now
where the time goes in v1:
time: 113 us; the launch traced here: 111 us
  Pallas kernels  43.1 us (38%)
  blocking collectives  35.4 us (31%)
  starting transfers between devices  22.7 us (20%)
  waiting for transfers between devices  6.93 us (6%)
  local copies, waits for them, and re-layouts  2.51 us (2%)
    all_to_all x1, blocking collectives, body(): lax.all_to_all(jnp.broadcast_to(rows, (lons, 2, 16, 128)), 'lon', 0, 0)  24.4 us
    pallas_call x1, Pallas kernels, step_one_call(): pl.pallas_call(step_one_kernel, in_specs=[SMEM] + [VMEM] * 10, out_specs=...  13.7 us
    all_to_all x1, blocking collectives, body(): parts = lax.all_to_all(cells, 'lon', 0, 0)  11 us
    pallas_call x1, Pallas kernels, step_two_call(): pl.pallas_call(step_two_kernel, in_specs=[SMEM] + [VMEM] * 14, out_specs=...  10.9 us
    pallas_call x1, Pallas kernels, first_call(): pl.pallas_call(first_kernel, in_specs=[SMEM, ANY, VMEM, VMEM], out_specs=...  9.15 us
    pallas_call x1, Pallas kernels, wind_call(): pl.pallas_call(wind_kernel, in_specs=[pl.BlockSpec(memory_space=pltpu.SME...  5.11 us
    ppermute x1, starting transfers between devices, body(): rn = lax.ppermute(fn, 'lat', northward)  4.87 us
    ppermute x1, starting transfers between devices, body(): msq_e = lax.ppermute(msq2, 'lon', westward)  4.66 us
  transfers between devices with their start and end apart: 8, of which 2 were waited for; matrix products, arithmetic and copies ran while one was open for 0% of the time, Pallas kernels for 2%

profile of v1, /device:TPU:1, one launch (start us, length us, event | category | flops | bytes accessed | tf_op | source)
XLA Modules:
  0.0 111.4 jit_solution(4142907105283014501)
XLA Ops:
  0.6 0.0 copy-start.6
  0.6 9.2 %first.1 = (f32[1800,8,128]{2,1,0:T(8,128)}, f32[1808,128]{1,0:T(8,128)}, f32[1808,128]{1,0:T(8,128)}, f32[10,8,128]{2,1,0:T(8,128)}, f32[10,8,128]{2,1,0:T(8,128)}, /*index=5*/f32[8,128]{1,0:T(8,128)}) custom-call(f32[384]{0:T(512)} %constant.8.clone.sm, f32[1800,8,128]{2,1,0:T(8,128)} %spec_hbm.1, s32[8,128]{1,0:T(8,128)} %mask.7, s32[8,128]{1,0:T(8,128)} %wrow.3), custom_call_target="tpu_custom_call" | custom-call | tf_op jit(solution)/shard_map/first/pallas_call | solution.py:149
  9.8 2.5 %collective-permute-start = (f32[1808,128]{1,0:T(8,128)}, f32[1808,128]{1,0:T(8,128)S(1)}, u32[]{:S(2)}, u32[]{:S(2)}) collective-permute-start(f32[1808,128]{1,0:T(8,128)} %get-tuple-element.30), channel_id=1, source_target_pairs={{0,1},{1,2},{2,3},{3,4},{4,5},{5,6},{6,7},{7,8},{8,9},{9,10},{10,1... | collective-permute-start | bytes 2777096 | tf_op jit(solution)/shard_map/ppermute | solution.py:564
  12.3 4.4 %collective-permute-start.1 = (f32[1808,128]{1,0:T(8,128)}, f32[1808,128]{1,0:T(8,128)S(1)}, u32[]{:S(2)}, u32[]{:S(2)}) collective-permute-start(f32[1808,128]{1,0:T(8,128)} %get-tuple-element.31), channel_id=1, source_target_pairs={{0,15},{1,0},{2,1},{3,2},{4,3},{5,4},{6,5},{7,6},{8,7},{9,8},{10,9... | collective-permute-start | bytes 2777096 | tf_op jit(solution)/shard_map/ppermute | solution.py:565
  16.7 0.0 copy-done.6
  16.8 24.4 %all_to_all.10.table = f32[16,2,16,128]{3,2,1,0:T(8,128)} all-to-all(f32[16,2,16,128]{3,2,1,0:T(8,128)S(1)} %broadcast_in_dim.8), channel_id=1, replica_groups=mesh['lat'=8,'lon'=16] {'lon'}, dimensions={0} | all-to-all | bytes 524288 | tf_op jit(solution)/shard_map/all_to_all | solution.py:567
  41.2 0.0 collective-permute-done.west
  41.2 0.0 collective-permute-done.1.east
  41.2 0.9 copy-done
  42.1 0.3 copy-done.1
  42.5 5.1 %winds.1 = (f32[8,128]{1,0:T(8,128)}, f32[8,128]{1,0:T(8,128)}, f32[8,128]{1,0:T(8,128)}, f32[50,18,128]{2,1,0:T(8,128)}, f32[50,18,128]{2,1,0:T(8,128)}, /*inde...) custom-call(f32[384]{0:T(512)} %constant.8.clone.sm, ...), custom_call_target="tpu_custom_call" | custom-call | tf_op jit(solution)/shard_map/winds/pallas_call | solution.py:279
  47.6 4.9 %collective-permute-start.2 = (f32[96,128]{1,0:T(8,128)}, f32[96,128]{1,0:T(8,128)S(1)}, u32[]{:S(2)}, u32[]{:S(2)}) collective-permute-start(f32[96,128]{1,0:T(8,128)} %get-tuple-element.38), channel_id=1, source_target_pairs={{0,16},{16,32},{32,48},{48,64},{64,80},{80,96},{96,112},{1,17},{17... | collective-permute-start | bytes 147464 | tf_op jit(solution)/shard_map/ppermute | solution.py:571
  52.4 1.9 %collective-permute-start.3 = (f32[96,128]{1,0:T(8,128)}, f32[96,128]{1,0:T(8,128)S(1)}, u32[]{:S(2)}, u32[]{:S(2)}) collective-permute-start(f32[96,128]{1,0:T(8,128)} %get-tuple-element.39), channel_id=1, source_target_pairs={{16,0},{32,16},{48,32},{64,48},{80,64},{96,80},{112,96},{17,1},{33... | collective-permute-start | bytes 147464 | tf_op jit(solution)/shard_map/ppermute | solution.py:572
  54.4 0.0 collective-permute-done.2.rn
  54.4 3.7 %collective-permute-done.3.rs = f32[96,128]{1,0:T(8,128)S(1)} collective-permute-done((f32[96,128]{1,0:T(8,128)}, f32[96,128]{1,0:T(8,128)S(1)}, u32[]{:S(2)}, u32[]{:S(2)}) %collective-permute-start.3) | collective-permute-done | bytes 49184 | tf_op jit(solution)/shard_map/ppermute | solution.py:572
  58.1 0.0 copy-done.2
  58.1 0.6 copy-done.3
  58.7 13.7 %step_one.1 = (f32[1800,8,128]{2,1,0:T(8,128)}, f32[8,128]{1,0:T(8,128)}, f32[80,128]{1,0:T(8,128)}, f32[80,128]{1,0:T(8,128)}) custom-call(f32[384]{0:T(512)} %constant.8.clone.sm, f32[1800,8,128]{2,1,0:T(8,128)} %get-tuple-element.28.spec, f32[8,128]{1,0:T(8,128)} %get-tuple-element.34.u, f32[8,128]{1,0:T(8,128)} %get-tuple-element.35.v, ...), custom_call_target="tpu_custom_call" | custom-call | tf_op jit(solution)/shard_map/step_one/pallas_call | solution.py:369
  72.4 2.0 %collective-permute-start.6 = (f32[80,128]{1,0:T(8,128)}, f32[80,128]{1,0:T(8,128)S(1)}, u32[]{:S(2)}, u32[]{:S(2)}) collective-permute-start(f32[80,128]{1,0:T(8,128)} %get-tuple-element.47), channel_id=1, source_target_pairs={{0,16},{16,32},{32,48},{48,64},{64,80},{80,96},{96,112},{1,17},{17... | collective-permute-start | bytes 122888 | tf_op jit(solution)/shard_map/ppermute | solution.py:576
  74.4 2.3 %collective-permute-start.7 = (f32[80,128]{1,0:T(8,128)}, f32[80,128]{1,0:T(8,128)S(1)}, u32[]{:S(2)}, u32[]{:S(2)}) collective-permute-start(f32[80,128]{1,0:T(8,128)} %get-tuple-element.48), channel_id=1, source_target_pairs={{16,0},{32,16},{48,32},{64,48},{80,64},{96,80},{112,96},{17,1},{33... | collective-permute-start | bytes 122888 | tf_op jit(solution)/shard_map/ppermute | solution.py:577
  76.7 4.7 %collective-permute-start.5 = (f32[8,128]{1,0:T(8,128)}, f32[8,128]{1,0:T(8,128)S(1)}, u32[]{:S(2)}, u32[]{:S(2)}) collective-permute-start(f32[8,128]{1,0:T(8,128)} %get-tuple-element.41.msq), channel_id=1, source_target_pairs={{0,15},{1,0},{2,1},{3,2},{4,3},{5,4},{6,5},{7,6},{8,7},{9,8},{10,9... | collective-permute-start | bytes 12296 | tf_op jit(solution)/shard_map/ppermute | solution.py:579
  81.4 0.0 collective-permute-start.4
  81.4 2.7 %halo_columns.1 = (f32[50,18,128]{2,1,0:T(8,128)}, f32[50,18,128]{2,1,0:T(8,128)}) custom-call(f32[384]{0:T(512)} %constant.8.clone.sm, f32[50,18,128]{2,1,0:T(8,128)} %get-tuple-element.43.hp_w, f32[50,18,128]{2,1,0:T(8,128)} %get-tuple-element.44.hp_e, f32[96,128]{1,0:T(8,128)} %copy-done.2, f32[96,128]{1,0:T(8,128)} %copy-done.3, ...), custom_call_target="tpu_custom_call" | custom-call | tf_op jit(solution)/shard_map/halo_columns/pallas_call | solution.py:412
  84.1 0.0 collective-permute-done.5.msq_e
  84.1 3.2 %collective-permute-done.4.msq_w = f32[8,128]{1,0:T(8,128)S(1)} collective-permute-done((f32[8,128]{1,0:T(8,128)}, f32[8,128]{1,0:T(8,128)S(1)}, u32[]{:S(2)}, u32[]{:S(2)}) %collective-permute-start.4) | collective-permute-done | bytes 4128 | tf_op jit(solution)/shard_map/ppermute | solution.py:578
  87.3 0.0 collective-permute-done.6.rn
  87.4 0.0 collective-permute-done.7.rs
  87.4 0.6 copy-done.8
  87.9 0.0 copy-done.4
  88.0 10.9 %step_two.1 = (f32[1800,8,128]{2,1,0:T(8,128)}, f32[16,16,128]{2,1,0:T(8,128)}) custom-call(f32[384]{0:T(512)} %constant.8.clone.sm, f32[1800,8,128]{2,1,0:T(8,128)} %get-tuple-element.40.spec, f32[8,128]{1,0:T(8,128)} %get-tuple-element.34.u, f32[8,128]{1,0:T(8,128)} %get-tuple-element.35.v, f32[8,128]{1,0:T(8,128)} %get-tuple-element.41.msq, ...), custom_call_target="tpu_custom_call" | custom-call | tf_op jit(solution)/shard_map/step_two/pallas_call | solution.py:513
  98.9 11.0 %all_to_all.11.parts = f32[16,16,128]{2,1,0:T(8,128)} all-to-all(f32[16,16,128]{2,1,0:T(8,128)} %get-tuple-element.50), channel_id=1, replica_groups=mesh['lat'=8,'lon'=16] {'lon'}, dimensions={0} | all-to-all | bytes 262144 | tf_op jit(solution)/shard_map/all_to_all | solution.py:585
  109.9 1.5 %cells.1 = (f32[2,512]{1,0:T(2,128)}, f32[1,512]{1,0:T(1,128)}) custom-call(f32[16,16,128]{2,1,0:T(8,128)} %all_to_all.11.parts), custom_call_target="tpu_custom_call" | custom-call | tf_op jit(solution)/shard_map/cells/pallas_call | solution.py:548
  (12 shorter events, 0.0 us)
Async XLA Ops:
  0.6 16.1 %copy-start.6 = (f32[2,2048]{1,0:T(2,128)S(1)}, f32[2,2048]{1,0:T(2,128)}, u32[]{:S(2)}) copy-start(f32[2,2048]{1,0:T(2,128)} %param.12) | copy-start | bytes 49156
  9.8 31.4 %collective-permute-start = (f32[1808,128]{1,0:T(8,128)}, f32[1808,128]{1,0:T(8,128)S(1)}, u32[]{:S(2)}, u32[]{:S(2)}) collective-permute-start(f32[1808,128]{1,0:T(8,128)} %get-tuple-element.30), channel_id=1, source_target_pairs={{0,1},{1,2},{2,3},{3,4},{4,5},{5,6},{6,7},{7,8},{8,9},{9,10},{10,1... | collective-permute-start | bytes 2777096 | tf_op jit(solution)/shard_map/ppermute | solution.py:564
  12.3 28.9 %collective-permute-start.1 = (f32[1808,128]{1,0:T(8,128)}, f32[1808,128]{1,0:T(8,128)S(1)}, u32[]{:S(2)}, u32[]{:S(2)}) collective-permute-start(f32[1808,128]{1,0:T(8,128)} %get-tuple-element.31), channel_id=1, source_target_pairs={{0,15},{1,0},{2,1},{3,2},{4,3},{5,4},{6,5},{7,6},{8,7},{9,8},{10,9... | collective-permute-start | bytes 2777096 | tf_op jit(solution)/shard_map/ppermute | solution.py:565
  41.2 0.9 copy-start
  41.2 1.3 %copy-start.1 = (f32[1808,128]{1,0:T(8,128)}, f32[1808,128]{1,0:T(8,128)S(1)}, u32[]{:S(2)}) copy-start(f32[1808,128]{1,0:T(8,128)S(1)} %collective-permute-done.1.east) | copy-start | bytes 2777092
  47.6 6.8 %collective-permute-start.2 = (f32[96,128]{1,0:T(8,128)}, f32[96,128]{1,0:T(8,128)S(1)}, u32[]{:S(2)}, u32[]{:S(2)}) collective-permute-start(f32[96,128]{1,0:T(8,128)} %get-tuple-element.38), channel_id=1, source_target_pairs={{0,16},{16,32},{32,48},{48,64},{64,80},{80,96},{96,112},{1,17},{17... | collective-permute-start | bytes 147464 | tf_op jit(solution)/shard_map/ppermute | solution.py:571
  52.4 5.6 %collective-permute-start.3 = (f32[96,128]{1,0:T(8,128)}, f32[96,128]{1,0:T(8,128)S(1)}, u32[]{:S(2)}, u32[]{:S(2)}) collective-permute-start(f32[96,128]{1,0:T(8,128)} %get-tuple-element.39), channel_id=1, source_target_pairs={{16,0},{32,16},{48,32},{64,48},{80,64},{96,80},{112,96},{17,1},{33... | collective-permute-start | bytes 147464 | tf_op jit(solution)/shard_map/ppermute | solution.py:572
  54.4 3.7 %copy-start.2 = (f32[96,128]{1,0:T(8,128)}, f32[96,128]{1,0:T(8,128)S(1)}, u32[]{:S(2)}) copy-start(f32[96,128]{1,0:T(8,128)S(1)} %collective-permute-done.2.rn) | copy-start | bytes 147460
  58.1 0.6 copy-start.3
  72.4 15.0 %collective-permute-start.6 = (f32[80,128]{1,0:T(8,128)}, f32[80,128]{1,0:T(8,128)S(1)}, u32[]{:S(2)}, u32[]{:S(2)}) collective-permute-start(f32[80,128]{1,0:T(8,128)} %get-tuple-element.47), channel_id=1, source_target_pairs={{0,16},{16,32},{32,48},{48,64},{64,80},{80,96},{96,112},{1,17},{17... | collective-permute-start | bytes 122888 | tf_op jit(solution)/shard_map/ppermute | solution.py:576
  74.4 13.0 %collective-permute-start.7 = (f32[80,128]{1,0:T(8,128)}, f32[80,128]{1,0:T(8,128)S(1)}, u32[]{:S(2)}, u32[]{:S(2)}) collective-permute-start(f32[80,128]{1,0:T(8,128)} %get-tuple-element.48), channel_id=1, source_target_pairs={{16,0},{32,16},{48,32},{64,48},{80,64},{96,80},{112,96},{17,1},{33... | collective-permute-start | bytes 122888 | tf_op jit(solution)/shard_map/ppermute | solution.py:577
  76.7 7.4 %collective-permute-start.5 = (f32[8,128]{1,0:T(8,128)}, f32[8,128]{1,0:T(8,128)S(1)}, u32[]{:S(2)}, u32[]{:S(2)}) collective-permute-start(f32[8,128]{1,0:T(8,128)} %get-tuple-element.41.msq), channel_id=1, source_target_pairs={{0,15},{1,0},{2,1},{3,2},{4,3},{5,4},{6,5},{7,6},{8,7},{9,8},{10,9... | collective-permute-start | bytes 12296 | tf_op jit(solution)/shard_map/ppermute | solution.py:579
  81.4 6.0 %collective-permute-start.4 = (f32[8,128]{1,0:T(8,128)}, f32[8,128]{1,0:T(8,128)S(1)}, u32[]{:S(2)}, u32[]{:S(2)}) collective-permute-start(f32[8,128]{1,0:T(8,128)} %get-tuple-element.41.msq), channel_id=1, source_target_pairs={{0,1},{1,2},{2,3},{3,4},{4,5},{5,6},{6,7},{7,8},{8,9},{9,10},{10,1... | collective-permute-start | bytes 12296 | tf_op jit(solution)/shard_map/ppermute | solution.py:578
  84.1 3.3 %copy-start.7 = (f32[8,128]{1,0:T(8,128)}, f32[8,128]{1,0:T(8,128)S(1)}, u32[]{:S(2)}) copy-start(f32[8,128]{1,0:T(8,128)S(1)} %collective-permute-done.5.msq_e) | copy-start | bytes 12292
  87.3 0.6 copy-start.8
  87.4 0.6 copy-start.4
  87.4 0.6 copy-start.5

commit v2 on v1

v2 whole, which is shorter than its diff:
```python
import functools
import math

import jax
import jax.numpy as jnp
import numpy as np
from jax import lax
from jax.experimental import pallas as pl
from jax.experimental.pallas import tpu as pltpu
from jax.sharding import PartitionSpec as P

NF = 50
ND = 36
HALF = 18
QUAD = 9
GROUPS = 10
FG = NF // GROUPS
GB = FG * ND
ROWS = NF * HALF
COL = ROWS + 4
F32 = jnp.float32
BF16 = jnp.bfloat16

_f = np.arange(NF, dtype=np.float64)
_freq = 1.07 ** (_f - (NF - 1))
_theta = 2.0 * math.pi * (np.arange(ND) + 0.5) / ND
_cos = np.cos(_theta)
_sin = np.sin(_theta)
_gain = 0.6 * _freq**2
_base = 1.0 - 0.2 * _freq
_cour = 0.7 * (3.0 / 7.0) ** (_f / (NF - 1))
_slope = 250.0 * _freq**4 / ND
_four = 4.0 * _freq
_push = 800.0 * _freq**2 / ND
EASTWARD = list(range(0, 9)) + list(range(27, 36))
WESTWARD = list(range(9, 27))

SCAL = np.zeros((6, 64), np.float32)
for _i, _t in enumerate((_gain, _base, _cour, _slope, _four, _push)):
    SCAL[_i, :NF] = _t
SCAL = SCAL.reshape(-1)


def scal(sm, kind, f):
    return sm[kind * 64 + f]


def _lane_tables():
    tab = np.zeros((GROUPS, 8, 128), np.float32)
    tab[:, 1] = 1.0
    for g in range(GROUPS):
        for i in range(FG):
            f = g * FG + i
            for d in range(HALF):
                j = i * HALF + d
                tab[g, 0, j] = _gain[f]
                tab[g, 1, j] = _base[f]
                tab[g, 2, j] = _cos[d]
                tab[g, 3, j] = _sin[d]
                tab[g, 4, j] = _four[f]
    return tab


def _dir_tables():
    tab = np.zeros((4, HALF, 128), np.float32)
    for s, dirs in enumerate((EASTWARD, WESTWARD)):
        tab[2 * s] = _cos[dirs][:, None]
        tab[2 * s + 1] = _sin[dirs][:, None]
    return tab


LANE_TAB = _lane_tables()
DIR_TAB = _dir_tables()
FOUR_COL = np.broadcast_to(_four[:, None], (NF, 128)).astype(np.float32)


def quartets():
    for d in range(QUAD):
        yield (d, 17 - d, 18 + d, 35 - d)


def iota(shape, dim):
    return lax.broadcasted_iota(jnp.int32, shape, dim)


def pack_edges(ref, g, lane):
    edge_n = jnp.zeros((8, 128), F32)
    edge_s = jnp.zeros((8, 128), F32)
    for i in range(FG):
        for d in range(HALF):
            j = i * HALF + d
            e = ref[g * GB + i * ND + d]
            edge_n = jnp.where(lane == j, pltpu.roll(e, (j - 127) % 128, 1), edge_n)
            e = ref[g * GB + i * ND + HALF + d]
            edge_s = jnp.where(lane == j, pltpu.roll(e, j, 1) if j else e, edge_s)
    return edge_n, edge_s


def first_kernel(spec_hbm, near_w, near_e, north, south, msq, spec, sems):
    lane = iota((8, 128), 1)

    def copy(g):
        at = pl.ds(g * GB, GB)
        return pltpu.make_async_copy(spec_hbm.at[at], spec.at[at], sems.at[g])

    for g in range(GROUPS):
        copy(g).start()
    msq[...] = jnp.zeros_like(msq)

    def group(g, growth):
        copy(g).wait()
        total = jnp.zeros((8, 128), F32)
        for i in range(FG):
            acc = jnp.zeros((8, 128), F32)
            for d in range(ND):
                e = spec[g * GB + i * ND + d]
                acc = acc + e
                if d in WESTWARD:
                    k = pl.ds(g * FG * HALF + i * HALF + WESTWARD.index(d), 1)
                    near_w[k, :] = e[0:1]
                else:
                    k = pl.ds(g * FG * HALF + i * HALF + EASTWARD.index(d), 1)
                    near_e[k, :] = e[7:8]
            total = total + float(_slope[i]) * acc
        msq[...] += growth * total
        north[g], south[g] = pack_edges(spec, g, lane)
        return growth * float(_slope[FG] / _slope[0])

    lax.fori_loop(0, GROUPS, group, jnp.float32(1.0))
    q = msq[...]
    for near, x in ((near_w, 0), (near_e, 7)):
        near[ROWS : ROWS + 1, :] = q[x : x + 1]
        near[ROWS + 1 : COL, :] = jnp.zeros((COL - ROWS - 1, 128), F32)


def sector_kernel(mask, winds, wrow, mine):
    for c in range(2):
        for r in range(16):
            mine[0, 16 * c + r : 16 * c + r + 1, :] = winds[c : c + 1, 128 * r : 128 * r + 128]
    mine[0, 32:40, :] = wrow[...].astype(F32)
    mine[0, 40:48, :] = mask[...].astype(F32)
    rows = mine[0]
    for n in range(1, mine.shape[0]):
        mine[n] = rows


SMEM = pl.BlockSpec(memory_space=pltpu.SMEM)
VMEM = pl.BlockSpec(memory_space=pltpu.VMEM)
HBM = pl.BlockSpec(memory_space=pltpu.HBM)
TILE = jax.ShapeDtypeStruct((8, 128), F32)
FIELD = jax.ShapeDtypeStruct((NF * ND, 8, 128), F32)
BUFFER = pltpu.VMEM((NF * ND, 8, 128), F32)
PARAMS = pltpu.CompilerParams(vmem_limit_bytes=30 * 2**20)
MIDDLE = pltpu.CompilerParams(vmem_limit_bytes=43 * 2**20)
WIDE = pltpu.CompilerParams(vmem_limit_bytes=48 * 2**20)
ALONE = pltpu.CompilerParams(vmem_limit_bytes=54 * 2**20)


def first_call(spectra):
    edge = jax.ShapeDtypeStruct((COL, 128), F32)
    pack = jax.ShapeDtypeStruct((GROUPS, 8, 128), F32)
    return pl.pallas_call(
        first_kernel,
        in_specs=[HBM],
        out_specs=[VMEM] * 5,
        out_shape=[edge, edge, pack, pack, TILE],
        scratch_shapes=[BUFFER, pltpu.SemaphoreType.DMA((GROUPS,))],
        compiler_params=WIDE,
        name="first",
    )(spectra)


def sector_call(mask, winds, wrow, lons):
    return pl.pallas_call(
        sector_kernel,
        in_specs=[VMEM] * 3,
        out_specs=VMEM,
        out_shape=jax.ShapeDtypeStruct((lons, 48, 128), F32),
        compiler_params=ALONE,
        name="sector",
    )(mask, winds, wrow)


def split3(x):
    a = x.astype(BF16)
    r = x - a.astype(F32)
    b = r.astype(BF16)
    c = (r - b.astype(F32)).astype(BF16)
    return a, b, c


def wind_kernel(
    me_ref, table, wrow, msq, mask, north, south, lane_tab,
    u_ref, v_ref, side_ref, fn, fs,
):
    srcs = table.shape[0]
    me = me_ref[0]
    hi_count = srcs * 16
    west = table.at[(me + srcs - 1) & (srcs - 1)]
    east = table.at[(me + 1) & (srcs - 1)]
    rows = [wrow[x : x + 1, :] for x in range(8)]
    for ref, x in ((west, 7), (east, 0)):
        rows.append(ref[32 + x : 33 + x, :].astype(jnp.int32))
    local = [r & (hi_count * 128 - 1) for r in rows]
    hi_iota = iota((hi_count, 128), 0)
    hots = []
    for r in local:
        hots.append(jnp.where(hi_iota == r // 128, 1.0, 0.0).astype(BF16))
    hot = jnp.concatenate(hots, axis=1)
    tab = jnp.concatenate(
        [table[:, 16 * c : 16 * c + 16].reshape(hi_count, 128) for c in range(2)], axis=1
    )
    got = None
    for part in split3(tab):
        term = lax.dot_general(
            part, hot, (((0,), (0,)), ((), ())), preferred_element_type=F32
        )
        got = term if got is None else got + term
    lo_iota = iota((128, 128), 0)
    us, vs = [], []
    for n, r in enumerate(local):
        pick = lo_iota == (r & 127)
        at = slice(n * 128, n * 128 + 128)
        us.append(jnp.sum(jnp.where(pick, got[0:128, at], 0.0), axis=0, keepdims=True))
        vs.append(jnp.sum(jnp.where(pick, got[128:256, at], 0.0), axis=0, keepdims=True))
    for x in range(8):
        u_ref[x : x + 1, :] = us[x]
        v_ref[x : x + 1, :] = vs[x]
    for n, (ref, x) in enumerate(((west, 7), (east, 0))):
        side_ref[3 * n : 3 * n + 1, :] = us[8 + n]
        side_ref[3 * n + 1 : 3 * n + 2, :] = vs[8 + n]
        side_ref[3 * n + 2 : 3 * n + 3, :] = ref[40 + x : 41 + x, :]
    side_ref[6:8, :] = jnp.zeros((2, 128), F32)

    maskf = mask[...].astype(F32)
    for edge, out, lane, sign in ((north, fn, 127, 1.0), (south, fs, 0, -1.0)):
        pick = lambda a: jnp.broadcast_to(a[:, lane : lane + 1], (8, 128))
        ue, ve, me_, qe = pick(u_ref[...]), pick(v_ref[...]), pick(maskf), pick(msq[...])
        for g in range(GROUPS):
            lt = lane_tab[g]
            along = sign * (lt[2:3] * ue + lt[3:4] * ve)
            t = jnp.maximum(lt[0:1] * along + lt[1:2], 1.0)
            out[g * 8 : g * 8 + 8, :] = edge[g] * t * (me_ / (1.0 + lt[4:5] * qe))


def wind_call(me, table, wrow, msq, mask, north, south):
    edge = jax.ShapeDtypeStruct((80, 128), F32)
    return pl.pallas_call(
        wind_kernel,
        in_specs=[SMEM] + [VMEM] * 7,
        out_specs=[VMEM] * 5,
        out_shape=[TILE, TILE, TILE, edge, edge],
        compiler_params=PARAMS,
        name="winds",
    )(me, table, wrow, msq, mask, north, south, jnp.asarray(LANE_TAB))


def forced_column(sm, src, dst, s, u_row, v_row, mask_row, msq_row, dir_tab, four):
    along = dir_tab[2 * s] * u_row + dir_tab[2 * s + 1] * v_row
    fac = mask_row / (1.0 + four[...] * msq_row)
    for f in range(NF):
        at = slice(f * HALF, f * HALF + HALF)
        t = jnp.maximum(scal(sm, 0, f) * along + scal(sm, 1, f), 1.0)
        dst[at, :] = src[at, :] * t * fac[f : f + 1]


def along_table(along, u, v):
    for d in range(ND):
        along[d] = float(_cos[d]) * u + float(_sin[d]) * v


def shifted(gv, d, j, sub, lane, hx_w, hx_e, row0, halo_n, halo_s):
    if d in WESTWARD:
        k = WESTWARD.index(d)
        row = hx_e[pl.ds(row0 + k, 1), :]
        row = jnp.broadcast_to(row, (8, 128))
        xs = jnp.where(sub == 7, row, pltpu.roll(gv, 7, 0))
    else:
        k = EASTWARD.index(d)
        row = hx_w[pl.ds(row0 + k, 1), :]
        row = jnp.broadcast_to(row, (8, 128))
        xs = jnp.where(sub == 0, row, pltpu.roll(gv, 1, 0))
    if d < HALF:
        halo = pltpu.roll(halo_n, (-j) % 128, 1) if j else halo_n
        ys = jnp.where(lane == 0, halo, pltpu.roll(gv, 1, 1))
    else:
        halo = pltpu.roll(halo_s, 127 - j, 1)
        ys = jnp.where(lane == 127, halo, pltpu.roll(gv, 127, 1))
    return xs, ys


def step_one_kernel(
    sm, spec_hbm, u, v, msq, mask, near_w, near_e, side, rn, rs, lane_tab, dir_tab, four_tab,
    out, msq2, fn2, fs2, to_w, to_e, spec, along, edges_n, edges_s, hx_w, hx_e, sems,
):
    def copy(g):
        at = pl.ds(g * GB, GB)
        return pltpu.make_async_copy(spec_hbm.at[at], spec.at[at], sems.at[g])

    for g in range(GROUPS):
        copy(g).start()
    for s, near, hx in ((0, near_w, hx_w), (1, near_e, hx_e)):
        rows = (side[3 * s + r : 3 * s + r + 1, :] for r in range(3))
        forced_column(sm, near, hx, s, *rows, near[ROWS : ROWS + 1, :], dir_tab, four_tab)
    lane = iota((8, 128), 1)
    sub = iota((8, 128), 0)
    maskf = mask[...].astype(F32)
    along_table(along, u[...], v[...])
    msq2[...] = jnp.zeros_like(msq2)

    @pl.loop(0, GROUPS)
    def _(g):
        copy(g).wait()
        last = jnp.maximum(g - 1, 0)
        edges_n[last], edges_s[last] = pack_edges(out, last, lane)
        total = jnp.zeros((8, 128), F32)
        at = pl.ds(pl.multiple_of(g * 8, 8), 8)
        halo_n = rn[at, :]
        halo_s = rs[at, :]
        for i in range(FG):
            f = g * FG + i
            a, b, cr = scal(sm, 0, f), scal(sm, 1, f), scal(sm, 2, f)
            fac = maskf / (1.0 + scal(sm, 4, f) * msq[...])
            acc = jnp.zeros((8, 128), F32)
            for quartet in quartets():
                d0 = quartet[0]
                kx = cr * float(abs(_cos[d0]))
                ky = cr * float(abs(_sin[d0]))
                k0 = 1.0 - kx - ky
                for d in quartet:
                    j = i * HALF + d % HALF
                    gv = spec[f * ND + d] * jnp.maximum(a * along[d] + b, 1.0) * fac
                    xs, ys = shifted(gv, d, j, sub, lane, hx_w, hx_e, f * HALF, halo_n, halo_s)
                    e = k0 * gv + kx * xs + ky * ys
                    out[f * ND + d] = e
                    acc = acc + e
                    if d in WESTWARD:
                        to_w[pl.ds(f * HALF + WESTWARD.index(d), 1), :] = e[0:1]
                    else:
                        to_e[pl.ds(f * HALF + EASTWARD.index(d), 1), :] = e[7:8]
            total = total + scal(sm, 3, f) * acc
        msq2[...] += total

    edges_n[GROUPS - 1], edges_s[GROUPS - 1] = pack_edges(out, GROUPS - 1, lane)

    msq2[...] = msq2[...] * maskf
    for edge, dst, at, sign in ((edges_n, fn2, 127, 1.0), (edges_s, fs2, 0, -1.0)):
        pick = lambda z: jnp.broadcast_to(z[:, at : at + 1], (8, 128))
        ue, ve, me, qe = pick(u[...]), pick(v[...]), pick(maskf), pick(msq2[...])
        for q in range(GROUPS):
            lt = lane_tab[q]
            al = sign * (lt[2:3] * ue + lt[3:4] * ve)
            t = jnp.maximum(lt[0:1] * al + lt[1:2], 1.0)
            dst[q * 8 : q * 8 + 8, :] = edge[q] * t * (me / (1.0 + lt[4:5] * qe))
    for s, col, x in ((0, to_e, 7), (1, to_w, 0)):
        rows = (z[x : x + 1] for z in (u[...], v[...], maskf, msq2[...]))
        forced_column(sm, col, col, s, *rows, dir_tab, four_tab)
        col[ROWS:COL, :] = jnp.zeros((COL - ROWS, 128), F32)


def step_one_call(spectra, u, v, msq, mask, near_w, near_e, side, rn, rs):
    edge = jax.ShapeDtypeStruct((80, 128), F32)
    column = jax.ShapeDtypeStruct((COL, 128), F32)
    return pl.pallas_call(
        step_one_kernel,
        in_specs=[SMEM, HBM] + [VMEM] * 12,
        out_specs=[VMEM] * 6,
        out_shape=[FIELD, TILE, edge, edge, column, column],
        scratch_shapes=[
            BUFFER,
            pltpu.VMEM((ND, 8, 128), F32),
            pltpu.VMEM((GROUPS, 8, 128), F32),
            pltpu.VMEM((GROUPS, 8, 128), F32),
            pltpu.VMEM((COL, 128), F32),
            pltpu.VMEM((COL, 128), F32),
            pltpu.SemaphoreType.DMA((GROUPS,)),
        ],
        compiler_params=MIDDLE,
        name="step_one",
    )(
        jnp.asarray(SCAL), spectra, u, v, msq, mask, near_w, near_e, side, rn, rs,
        jnp.asarray(LANE_TAB), jnp.asarray(DIR_TAB), jnp.asarray(FOUR_COL),
    )


def step_two_kernel(
    sm, spec, u, v, msq, mask, hq_w, hq_e, rn, rs, owner, weight,
    out, cells, along, push, field, sems,
):
    lane = iota((8, 128), 1)
    sub = iota((8, 128), 0)
    maskf = mask[...].astype(F32)
    along_table(along, u[...], v[...])
    push[...] = jnp.zeros_like(push)

    def copy(g):
        at = pl.ds(g * GB, GB)
        return pltpu.make_async_copy(field.at[at], out.at[at], sems.at[g])

    @pl.loop(0, GROUPS)
    def _(g):
        pu = jnp.zeros((8, 128), F32)
        pv = jnp.zeros((8, 128), F32)
        at = pl.ds(pl.multiple_of(g * 8, 8), 8)
        halo_n = rn[at, :]
        halo_s = rs[at, :]
        for i in range(FG):
            f = g * FG + i
            a, b, cr, four = scal(sm, 0, f), scal(sm, 1, f), scal(sm, 2, f), scal(sm, 4, f)
            fac = maskf / (1.0 + four * msq[...])
            fu = jnp.zeros((8, 128), F32)
            fv = jnp.zeros((8, 128), F32)
            for quartet in quartets():
                d0 = quartet[0]
                kx = cr * float(abs(_cos[d0]))
                ky = cr * float(abs(_sin[d0]))
                k0 = 1.0 - kx - ky
                q = []
                for d in quartet:
                    j = i * HALF + d % HALF
                    t = jnp.maximum(a * along[d] + b, 1.0)
                    gv = spec[f * ND + d] * t * fac
                    xs, ys = shifted(gv, d, j, sub, lane, hq_w, hq_e, f * HALF, halo_n, halo_s)
                    e = (k0 * gv + kx * xs + ky * ys) * maskf
                    field[f * ND + d] = e
                    q.append((t - 1.0) * e)
                lo = q[0] - q[2]
                hi = q[1] - q[3]
                fu = fu + float(_cos[d0]) * (lo - hi)
                fv = fv + float(_sin[d0]) * (lo + hi)
            pu = pu + scal(sm, 5, f) * fu
            pv = pv + scal(sm, 5, f) * fv
        push[0] += pu
        push[1] += pv
        copy(g).start()

    def finish():
        uu, vv = u[...], v[...]
        share = weight[...].astype(F32) * maskf
        tau = 0.02 * (uu * uu + vv * vv) + 0.25
        terms = (share, share * tau, share * push[0], share * push[1])
        parts = [split3(t) for t in terms]
        dests = cells.shape[0]
        own = owner[...] & (dests * 512 - 1)
        hi_own = own // 128
        lo_own = own & 127
        row = iota((dests * 16, 128), 0)
        want = (row // 16) * 4 + row % 4
        lo_iota = iota((128, 128), 0)
        kind = iota((16, 128), 0) // 4
        total = jnp.zeros((dests * 16, 128), F32)
        for x in range(8):
            hot = jnp.where(lo_iota == lo_own[x : x + 1], 1.0, 0.0).astype(BF16)
            match = want == hi_own[x : x + 1]
            for p in range(3):
                rows = [parts[k][p][x : x + 1].astype(F32) for k in range(4)]
                tile = jnp.where(
                    kind == 0, rows[0],
                    jnp.where(kind == 1, rows[1], jnp.where(kind == 2, rows[2], rows[3])),
                )
                lhs = jnp.where(match, jnp.concatenate([tile] * dests, axis=0), 0.0).astype(BF16)
                total = total + lax.dot_general(
                    lhs, hot, (((1,), (1,)), ((), ())), preferred_element_type=F32
                )
        cells[...] = total.reshape(dests, 16, 128)

    finish()
    for g in range(GROUPS):
        copy(g).wait()


def step_two_call(spec, u, v, msq, mask, hq_w, hq_e, rn, rs, owner, weight, dests):
    return pl.pallas_call(
        step_two_kernel,
        in_specs=[SMEM] + [VMEM] * 11,
        out_specs=[HBM, VMEM],
        out_shape=[FIELD, jax.ShapeDtypeStruct((dests, 16, 128), F32)],
        scratch_shapes=[
            pltpu.VMEM((ND, 8, 128), F32),
            pltpu.VMEM((2, 8, 128), F32),
            BUFFER,
            pltpu.SemaphoreType.DMA((GROUPS,)),
        ],
        compiler_params=PARAMS,
        name="step_two",
    )(jnp.asarray(SCAL), spec, u, v, msq, mask, hq_w, hq_e, rn, rs, owner, weight)


def cell_kernel(parts, stress, rough):
    sums = jnp.sum(parts[...], axis=0)
    w, a, bx, by = (sums[4 * k : 4 * k + 4] for k in range(4))
    total_w = jnp.maximum(w, 1.0)
    sx = bx / total_w
    sy = by / total_w
    low = jnp.maximum(a, 1.0)
    r = jnp.sqrt(1.0 + (bx * bx + by * by) / (low * low)) * a / total_w
    for n in range(4):
        at = slice(n * 128, n * 128 + 128)
        stress[0:1, at] = sx[n : n + 1]
        stress[1:2, at] = sy[n : n + 1]
        rough[0:1, at] = r[n : n + 1]


def cell_call(parts):
    return pl.pallas_call(
        cell_kernel,
        out_shape=[jax.ShapeDtypeStruct((2, 512), F32), jax.ShapeDtypeStruct((1, 512), F32)],
        name="cells",
    )(parts)


def body(spectra, sea_mask, atm_wind, wind_row, owner, weight):
    lons = lax.axis_size("lon")
    lats = lax.axis_size("lat")
    eastward = [(i, (i + 1) % lons) for i in range(lons)]
    westward = [(i, (i - 1) % lons) for i in range(lons)]
    northward = [(i, i + 1) for i in range(lats - 1)]
    southward = [(i + 1, i) for i in range(lats - 1)]

    me = lax.axis_index("lon").astype(jnp.int32)
    mine = sector_call(sea_mask, atm_wind, wind_row, lons)
    near_w, near_e, north, south, msq1 = first_call(spectra)
    table = lax.all_to_all(mine, "lon", 0, 0)
    near_w, near_e, table = lax.optimization_barrier((near_w, near_e, table))
    from_west = lax.ppermute(near_e, "lon", eastward)
    from_east = lax.ppermute(near_w, "lon", westward)
    u, v, side, fn, fs = wind_call(
        me.reshape(1), table, wind_row, msq1, sea_mask, north, south
    )
    rn = lax.ppermute(fn, "lat", northward)
    rs = lax.ppermute(fs, "lat", southward)
    energy, msq2, fn2, fs2, to_w, to_e = step_one_call(
        spectra, u, v, msq1, sea_mask, from_west, from_east, side, rn, rs
    )
    from_west = lax.ppermute(to_e, "lon", eastward)
    from_east = lax.ppermute(to_w, "lon", westward)
    rn = lax.ppermute(fn2, "lat", northward)
    rs = lax.ppermute(fs2, "lat", southward)
    energy, cells = step_two_call(
        energy, u, v, msq2, sea_mask, from_west, from_east, rn, rs, owner, weight, lons
    )
    parts = lax.all_to_all(cells, "lon", 0, 0)
    stress, rough = cell_call(parts)
    return energy, stress, rough.reshape(512)


def solution(mesh):
    in_specs = (
        P(None, "lon", "lat"),
        P("lon", "lat"),
        P(None, ("lat", "lon")),
        P("lon", "lat"),
        P("lon", "lat"),
        P("lon", "lat"),
    )
    out_specs = (P(None, "lon", "lat"), P(None, ("lat", "lon")), P(("lat", "lon")))
    return jax.shard_map(body, mesh=mesh, in_specs=in_specs, out_specs=out_specs, check_vma=False)
```

time: 113 us -> 82.9 us (0.73)
  blocking collectives: 35.4 us -> 13.2 us
  Pallas kernels: 43.1 us -> 24.2 us
  starting transfers between devices: 22.7 us -> 30.9 us
  waiting for transfers between devices: 6.93 us -> 13 us
  local copies, waits for them, and re-layouts: 2.51 us -> 0.05 us
    all_to_all x1 -> x0, blocking collectives: 24.4 us -> none  [body(): lax.all_to_all(jnp.broadcast_to(rows, (lons, 2, 16, 128)), 'lon', 0, 0)]
    pallas_call x5, Pallas kernels: 41.6 us -> 22.7 us  [the longest x1 8.86 us: step_one_call(): pl.pallas_call(step_one_kernel, in_specs=[SMEM, HBM] + [VMEM] * 12, out_s...]
    all_to_all x0 -> x1, starting transfers between devices: none -> 8.43 us  [body(): table = lax.all_to_all(mine, 'lon', 0, 0)]
    all_to_all x0 -> x1, waiting for transfers between devices: none -> 3.84 us  [body(): table = lax.all_to_all(mine, 'lon', 0, 0)]
    ppermute x6, waiting for transfers between devices: 3.26 us -> 5.75 us  [the longest x1 3.68 us: body(): rs = lax.ppermute(fs2, 'lat', southward)]
    unnamed x19 -> x16, local copies, waits for them, and re-layouts: 2.49 us -> 0.05 us
    all_to_all x1, blocking collectives: 11 us -> 13.2 us  [body(): parts = lax.all_to_all(cells, 'lon', 0, 0)]
    ppermute x6, starting transfers between devices: 15.9 us -> 14.3 us  [the longest x1 4.77 us: body(): from_east = lax.ppermute(to_w, 'lon', westward)]
  transfers between devices with their start and end apart: 8 -> 9, of which waited for: 2 -> 4; matrix products, arithmetic and copies ran while one was open for 0% -> 0% of each run, Pallas kernels for 2% -> 6%
where the time goes in v2:
time: 82.9 us; the launch traced here: 82.1 us
  starting transfers between devices  30.9 us (37%)
  Pallas kernels  24.2 us (29%)
  blocking collectives  13.2 us (16%)
  waiting for transfers between devices  13 us (16%)
    all_to_all x1, blocking collectives, body(): parts = lax.all_to_all(cells, 'lon', 0, 0)  13.2 us
    pallas_call x1, Pallas kernels, step_one_call(): pl.pallas_call(step_one_kernel, in_specs=[SMEM, HBM] + [VMEM] * 12, out_s...  8.86 us
    all_to_all x1, starting transfers between devices, body(): table = lax.all_to_all(mine, 'lon', 0, 0)  8.43 us
    pallas_call x1, Pallas kernels, step_two_call(): pl.pallas_call(step_two_kernel, in_specs=[SMEM] + [VMEM] * 11, out_specs=...  7.02 us
    ppermute x1, starting transfers between devices, body(): rn = lax.ppermute(fn, 'lat', northward)  6.16 us
    ppermute x1, starting transfers between devices, body(): from_east = lax.ppermute(to_w, 'lon', westward)  4.77 us
    ppermute x1, starting transfers between devices, body(): from_east = lax.ppermute(near_w, 'lon', westward)  4.48 us
    pallas_call x1, Pallas kernels, first_call(): pl.pallas_call(first_kernel, in_specs=[HBM], out_specs=[VMEM] * 5, out_sh...  4.39 us
  transfers between devices with their start and end apart: 9, of which 4 were waited for; matrix products, arithmetic and copies ran while one was open for 0% of the time, Pallas kernels for 6%

profile of v2, /device:TPU:1, one launch (start us, length us, event | category | flops | bytes accessed | tf_op | source)
XLA Modules:
  0.0 82.1 jit_solution(16479826494430171397)
XLA Ops:
  0.6 0.0 copy-start
  0.6 0.0 copy-start.5
  0.7 0.0 copy-start.3
  0.7 0.0 copy-start.2
  0.7 1.5 %sector.1 = f32[16,48,128]{2,1,0:T(8,128)} custom-call(s32[8,128]{1,0:T(8,128)} %mask.7, f32[2,2048]{1,0:T(2,128)} %winds.2, s32[8,128]{1,0:T(8,128)} %wrow.3), custom_call_target="tpu_custom_call" | custom-call | tf_op jit(solution)/shard_map/sector/pallas_call | solution.py:174
  2.2 8.4 %all-to-all-start = ((f32[16,48,128]{2,1,0:T(8,128)}), f32[16,48,128]{2,1,0:T(8,128)S(1)}, u32[]{:S(2)}, u32[]{:S(2)}) async-start(f32[16,48,128]{2,1,0:T(8,128)} %sector.1), calls=%async_computation | async-start | bytes 786432 | tf_op jit(solution)/shard_map/all_to_all | solution.py:523
  10.7 0.0 copy-start.6
  10.7 0.0 copy-start.7
  10.7 4.4 %first.1 = (f32[904,128]{1,0:T(8,128)S(1)}, f32[904,128]{1,0:T(8,128)S(1)}, f32[10,8,128]{2,1,0:T(8,128)S(1)}, f32[10,8,128]{2,1,0:T(8,128)S(1)}, f32[8,128]{1,0:T(8,128)S(1)}) custom-call(f32[1800,8,128]{2,1,0:T(8,128)} %spec_hbm.3), custom_call_target="tpu_custom_call" | custom-call | tf_op jit(solution)/shard_map/first/pallas_call | solution.py:162
  15.1 3.8 %all-to-all-done.table = f32[16,48,128]{2,1,0:T(8,128)S(1)} async-done(((f32[16,48,128]{2,1,0:T(8,128)}), f32[16,48,128]{2,1,0:T(8,128)S(1)}, u32[]{:S(2)}, u32[]{:S(2)}) %all-to-all-start) | async-done | bytes 393248 | tf_op jit(solution)/shard_map/all_to_all | solution.py:523
  18.9 0.3 collective-permute-start
  19.2 4.5 %collective-permute-start.1 = (f32[904,128]{1,0:T(8,128)S(1)}, f32[904,128]{1,0:T(8,128)S(1)}, u32[]{:S(2)}, u32[]{:S(2)}) collective-permute-start(f32[904,128]{1,0:T(8,128)S(1)} %get-tuple-element.35), channel_id=1, source_target_pairs={{0,15},{1,0},{2,1},{3,2},{4,3},{5,4},{6,5},{7,6},{8,7},{9,8},{10,9... | collective-permute-start | bytes 1388552 | tf_op jit(solution)/shard_map/ppermute | solution.py:526
  23.7 0.0 copy-done.1
  23.7 0.9 %winds.3 = (f32[8,128]{1,0:T(8,128)S(1)}, f32[8,128]{1,0:T(8,128)S(1)}, f32[8,128]{1,0:T(8,128)S(1)}, f32[80,128]{1,0:T(8,128)S(1)}, f32[80,128]{1,0:T(8,128)S(1)}) custom-call(s32[1]{0:T(128)} %bitcast.me_ref, f32[16,48,128]{2,1,0:T(8,128)S(1)} %all-to-all-done.table, s32[8,128]{1,0:T(8,128)S(1)} %copy-done.4, f32[8,128]{1,0:T(8,128)S(1)} %get-tuple-element.29.msq, ...), custom_call_target="tpu_custom_call" | custom-call | tf_op jit(solution)/shard_map/winds/pallas_call | solution.py:248
  24.6 6.2 %collective-permute-start.2 = (f32[80,128]{1,0:T(8,128)S(1)}, f32[80,128]{1,0:T(8,128)S(1)}, u32[]{:S(2)}, u32[]{:S(2)}) collective-permute-start(f32[80,128]{1,0:T(8,128)S(1)} %get-tuple-element.37), channel_id=1, source_target_pairs={{0,16},{16,32},{32,48},{48,64},{64,80},{80,96},{96,112},{1,17},{17... | collective-permute-start | bytes 122888 | tf_op jit(solution)/shard_map/ppermute | solution.py:530
  30.8 1.9 %collective-permute-start.3 = (f32[80,128]{1,0:T(8,128)S(1)}, f32[80,128]{1,0:T(8,128)S(1)}, u32[]{:S(2)}, u32[]{:S(2)}) collective-permute-start(f32[80,128]{1,0:T(8,128)S(1)} %get-tuple-element.38), channel_id=1, source_target_pairs={{16,0},{32,16},{48,32},{64,48},{80,64},{96,80},{112,96},{17,1},{33... | collective-permute-start | bytes 122888 | tf_op jit(solution)/shard_map/ppermute | solution.py:531
  32.7 0.0 collective-permute-done.2.rn
  32.7 3.4 %collective-permute-done.3.rs = f32[80,128]{1,0:T(8,128)S(1)} collective-permute-done((f32[80,128]{1,0:T(8,128)S(1)}, f32[80,128]{1,0:T(8,128)S(1)}, u32[]{:S(2)}, u32[]{:S(2)}) %collective-permute-start.3) | collective-permute-done | bytes 40992 | tf_op jit(solution)/shard_map/ppermute | solution.py:531
  36.1 0.0 collective-permute-done.near_w
  36.1 0.0 collective-permute-done.1.near_e
  36.1 8.9 %step_one.1 = (f32[1800,8,128]{2,1,0:T(8,128)S(1)}, f32[8,128]{1,0:T(8,128)S(1)}, f32[80,128]{1,0:T(8,128)S(1)}, f32[80,128]{1,0:T(8,128)S(1)}, f32[904,128]{1,0:T(8,128)S(1)}, /*index=5*/f32[904,128]{1,0:T(8,128)S(1)}) custom-call(f32[384]{0:T(512)S(1)} %copy-done.5, f32[1800,8,128]{2,1,0:T(8,128)} %spec_hbm.3, f32[8,128]{1,0:T(8,128)S(1)} %get-tuple-element.32.u, ...), custom_call_target="tpu_custom_call" | custom-call | tf_op jit(solution)/shard_map/step_one/pallas_call | solution.py:364
  45.0 0.1 collective-permute-start.4
  45.1 4.8 %collective-permute-start.5 = (f32[904,128]{1,0:T(8,128)S(1)}, f32[904,128]{1,0:T(8,128)S(1)}, u32[]{:S(2)}, u32[]{:S(2)}) collective-permute-start(f32[904,128]{1,0:T(8,128)S(1)} %get-tuple-element.42), channel_id=1, source_target_pairs={{0,15},{1,0},{2,1},{3,2},{4,3},{5,4},{6,5},{7,6},{8,7},{9,8},{10,9... | collective-permute-start | bytes 1388552 | tf_op jit(solution)/shard_map/ppermute | solution.py:536
  49.9 2.8 %collective-permute-start.6 = (f32[80,128]{1,0:T(8,128)S(1)}, f32[80,128]{1,0:T(8,128)S(1)}, u32[]{:S(2)}, u32[]{:S(2)}) collective-permute-start(f32[80,128]{1,0:T(8,128)S(1)} %get-tuple-element.43), channel_id=1, source_target_pairs={{0,16},{16,32},{32,48},{48,64},{64,80},{80,96},{96,112},{1,17},{17... | collective-permute-start | bytes 122888 | tf_op jit(solution)/shard_map/ppermute | solution.py:537
  52.7 1.9 %collective-permute-start.7 = (f32[80,128]{1,0:T(8,128)S(1)}, f32[80,128]{1,0:T(8,128)S(1)}, u32[]{:S(2)}, u32[]{:S(2)}) collective-permute-start(f32[80,128]{1,0:T(8,128)S(1)} %get-tuple-element.44), channel_id=1, source_target_pairs={{16,0},{32,16},{48,32},{64,48},{80,64},{96,80},{112,96},{17,1},{33... | collective-permute-start | bytes 122888 | tf_op jit(solution)/shard_map/ppermute | solution.py:538
  54.6 0.0 collective-permute-done.6.rn
  54.6 3.7 %collective-permute-done.7.rs = f32[80,128]{1,0:T(8,128)S(1)} collective-permute-done((f32[80,128]{1,0:T(8,128)S(1)}, f32[80,128]{1,0:T(8,128)S(1)}, u32[]{:S(2)}, u32[]{:S(2)}) %collective-permute-start.7) | collective-permute-done | bytes 40992 | tf_op jit(solution)/shard_map/ppermute | solution.py:538
  58.3 2.1 %collective-permute-done.4.hq_w = f32[904,128]{1,0:T(8,128)S(1)} collective-permute-done((f32[904,128]{1,0:T(8,128)S(1)}, f32[904,128]{1,0:T(8,128)S(1)}, u32[]{:S(2)}, u32[]{:S(2)}) %collective-permute-start.4) | collective-permute-done | bytes 462880 | tf_op jit(solution)/shard_map/ppermute | solution.py:535
  60.4 0.0 collective-permute-done.5.hq_e
  60.4 7.0 %step_two.1 = (f32[1800,8,128]{2,1,0:T(8,128)}, f32[16,16,128]{2,1,0:T(8,128)S(1)}) custom-call(f32[384]{0:T(512)S(1)} %copy-done.5, f32[1800,8,128]{2,1,0:T(8,128)S(1)} %get-tuple-element.39.spec, f32[8,128]{1,0:T(8,128)S(1)} %get-tuple-element.32.u, f32[8,128]{1,0:T(8,128)S(1)} %get-tuple-element.33.v, f32[8,128]{1,0:T(8,128)S(1)} %get-tuple-element.40.msq, ...), custom_call_target="tpu_custom_call" | custom-call | tf_op jit(solution)/shard_map/step_two/pallas_call | solution.py:473
  67.4 13.2 %all_to_all.10.parts = f32[16,16,128]{2,1,0:T(8,128)} all-to-all(f32[16,16,128]{2,1,0:T(8,128)S(1)} %get-tuple-element.46), channel_id=1, replica_groups=mesh['lat'=8,'lon'=16] {'lon'}, dimensions={0} | all-to-all | bytes 262144 | tf_op jit(solution)/shard_map/all_to_all | solution.py:542
  80.6 1.5 %cells.1 = (f32[2,512]{1,0:T(2,128)}, f32[1,512]{1,0:T(1,128)}) custom-call(f32[16,16,128]{2,1,0:T(8,128)} %all_to_all.10.parts), custom_call_target="tpu_custom_call" | custom-call | tf_op jit(solution)/shard_map/cells/pallas_call | solution.py:505
  (9 shorter events, 0.0 us)
Async XLA Ops:
  0.6 23.1 %copy-start = (f32[10,8,128]{2,1,0:T(8,128)S(1)}, f32[10,8,128]{2,1,0:T(8,128)}, u32[]{:S(2)}) copy-start(f32[10,8,128]{2,1,0:T(8,128)} %constant.12.clone.lane_tab) | copy-start | bytes 122884
  0.6 35.5 %copy-start.5 = (f32[384]{0:T(512)S(1)}, f32[384]{0:T(512)}, u32[]{:S(2)}) copy-start(f32[384]{0:T(512)} %constant.13.clone.sm) | copy-start | bytes 4612
  0.7 35.5 %copy-start.3 = (f32[50,128]{1,0:T(8,128)S(1)}, f32[50,128]{1,0:T(8,128)}, u32[]{:S(2)}) copy-start(f32[50,128]{1,0:T(8,128)} %constant.15.clone.four_tab) | copy-start | bytes 76804
  0.7 35.5 %copy-start.2 = (f32[4,18,128]{2,1,0:T(8,128)S(1)}, f32[4,18,128]{2,1,0:T(8,128)}, u32[]{:S(2)}) copy-start(f32[4,18,128]{2,1,0:T(8,128)} %constant.14.clone.dir_tab) | copy-start | bytes 110596
  0.7 23.1 %copy-start.1 = (s32[8,128]{1,0:T(8,128)S(1)}, s32[8,128]{1,0:T(8,128)}, u32[]{:S(2)}) copy-start(s32[8,128]{1,0:T(8,128)} %mask.7) | copy-start | bytes 12292
  0.7 23.0 %copy-start.4 = (s32[8,128]{1,0:T(8,128)S(1)}, s32[8,128]{1,0:T(8,128)}, u32[]{:S(2)}) copy-start(s32[8,128]{1,0:T(8,128)} %wrow.3) | copy-start | bytes 12292
  2.2 16.7 %all-to-all-start = ((f32[16,48,128]{2,1,0:T(8,128)}), f32[16,48,128]{2,1,0:T(8,128)S(1)}, u32[]{:S(2)}, u32[]{:S(2)}) async-start(f32[16,48,128]{2,1,0:T(8,128)} %sector.1), calls=%async_computation | async-start | bytes 786432 | tf_op jit(solution)/shard_map/all_to_all | solution.py:523
  10.7 49.7 %copy-start.6 = (s32[8,128]{1,0:T(8,128)S(1)}, s32[8,128]{1,0:T(8,128)}, u32[]{:S(2)}) copy-start(s32[8,128]{1,0:T(8,128)} %owner.1) | copy-start | bytes 12292
  10.7 49.7 %copy-start.7 = (s32[8,128]{1,0:T(8,128)S(1)}, s32[8,128]{1,0:T(8,128)}, u32[]{:S(2)}) copy-start(s32[8,128]{1,0:T(8,128)} %weight.1) | copy-start | bytes 12292
  18.9 17.2 %collective-permute-start = (f32[904,128]{1,0:T(8,128)S(1)}, f32[904,128]{1,0:T(8,128)S(1)}, u32[]{:S(2)}, u32[]{:S(2)}) collective-permute-start(f32[904,128]{1,0:T(8,128)S(1)} %get-tuple-element.34), channel_id=1, source_target_pairs={{0,1},{1,2},{2,3},{3,4},{4,5},{5,6},{6,7},{7,8},{8,9},{9,10},{10,1... | collective-permute-start | bytes 1388552 | tf_op jit(solution)/shard_map/ppermute | solution.py:525
  19.2 16.9 %collective-permute-start.1 = (f32[904,128]{1,0:T(8,128)S(1)}, f32[904,128]{1,0:T(8,128)S(1)}, u32[]{:S(2)}, u32[]{:S(2)}) collective-permute-start(f32[904,128]{1,0:T(8,128)S(1)} %get-tuple-element.35), channel_id=1, source_target_pairs={{0,15},{1,0},{2,1},{3,2},{4,3},{5,4},{6,5},{7,6},{8,7},{9,8},{10,9... | collective-permute-start | bytes 1388552 | tf_op jit(solution)/shard_map/ppermute | solution.py:526
  24.6 8.1 %collective-permute-start.2 = (f32[80,128]{1,0:T(8,128)S(1)}, f32[80,128]{1,0:T(8,128)S(1)}, u32[]{:S(2)}, u32[]{:S(2)}) collective-permute-start(f32[80,128]{1,0:T(8,128)S(1)} %get-tuple-element.37), channel_id=1, source_target_pairs={{0,16},{16,32},{32,48},{48,64},{64,80},{80,96},{96,112},{1,17},{17... | collective-permute-start | bytes 122888 | tf_op jit(solution)/shard_map/ppermute | solution.py:530
  30.8 5.3 %collective-permute-start.3 = (f32[80,128]{1,0:T(8,128)S(1)}, f32[80,128]{1,0:T(8,128)S(1)}, u32[]{:S(2)}, u32[]{:S(2)}) collective-permute-start(f32[80,128]{1,0:T(8,128)S(1)} %get-tuple-element.38), channel_id=1, source_target_pairs={{16,0},{32,16},{48,32},{64,48},{80,64},{96,80},{112,96},{17,1},{33... | collective-permute-start | bytes 122888 | tf_op jit(solution)/shard_map/ppermute | solution.py:531
  45.0 15.3 %collective-permute-start.4 = (f32[904,128]{1,0:T(8,128)S(1)}, f32[904,128]{1,0:T(8,128)S(1)}, u32[]{:S(2)}, u32[]{:S(2)}) collective-permute-start(f32[904,128]{1,0:T(8,128)S(1)} %get-tuple-element.41), channel_id=1, source_target_pairs={{0,1},{1,2},{2,3},{3,4},{4,5},{5,6},{6,7},{7,8},{8,9},{9,10},{10,1... | collective-permute-start | bytes 1388552 | tf_op jit(solution)/shard_map/ppermute | solution.py:535
  45.1 15.3 %collective-permute-start.5 = (f32[904,128]{1,0:T(8,128)S(1)}, f32[904,128]{1,0:T(8,128)S(1)}, u32[]{:S(2)}, u32[]{:S(2)}) collective-permute-start(f32[904,128]{1,0:T(8,128)S(1)} %get-tuple-element.42), channel_id=1, source_target_pairs={{0,15},{1,0},{2,1},{3,2},{4,3},{5,4},{6,5},{7,6},{8,7},{9,8},{10,9... | collective-permute-start | bytes 1388552 | tf_op jit(solution)/shard_map/ppermute | solution.py:536
  49.9 4.7 %collective-permute-start.6 = (f32[80,128]{1,0:T(8,128)S(1)}, f32[80,128]{1,0:T(8,128)S(1)}, u32[]{:S(2)}, u32[]{:S(2)}) collective-permute-start(f32[80,128]{1,0:T(8,128)S(1)} %get-tuple-element.43), channel_id=1, source_target_pairs={{0,16},{16,32},{32,48},{48,64},{64,80},{80,96},{96,112},{1,17},{17... | collective-permute-start | bytes 122888 | tf_op jit(solution)/shard_map/ppermute | solution.py:537
  52.7 5.6 %collective-permute-start.7 = (f32[80,128]{1,0:T(8,128)S(1)}, f32[80,128]{1,0:T(8,128)S(1)}, u32[]{:S(2)}, u32[]{:S(2)}) collective-permute-start(f32[80,128]{1,0:T(8,128)S(1)} %get-tuple-element.44), channel_id=1, source_target_pairs={{16,0},{32,16},{48,32},{64,48},{80,64},{96,80},{112,96},{17,1},{33... | collective-permute-start | bytes 122888 | tf_op jit(solution)/shard_map/ppermute | solution.py:538

commit v3 on v2

v3 whole, which is shorter than its diff:
```python
import functools
import math

import jax
import jax.numpy as jnp
import numpy as np
from jax import lax
from jax.experimental import pallas as pl
from jax.experimental.pallas import tpu as pltpu
from jax.sharding import PartitionSpec as P

NF = 50
ND = 36
HALF = 18
QUAD = 9
GROUPS = 10
FG = NF // GROUPS
TILES = 2 * GROUPS
GB = FG * ND
ROWS = NF * HALF
COL = ROWS + 4
F32 = jnp.float32
BF16 = jnp.bfloat16

_f = np.arange(NF, dtype=np.float64)
_freq = 1.07 ** (_f - (NF - 1))
_theta = 2.0 * math.pi * (np.arange(ND) + 0.5) / ND
_cos = np.cos(_theta)
_sin = np.sin(_theta)
_gain = 0.6 * _freq**2
_base = 1.0 - 0.2 * _freq
_cour = 0.7 * (3.0 / 7.0) ** (_f / (NF - 1))
_slope = 250.0 * _freq**4 / ND
_four = 4.0 * _freq
_push = 800.0 * _freq**2 / ND
EASTWARD = list(range(0, 9)) + list(range(27, 36))
WESTWARD = list(range(9, 27))

SCAL = np.zeros((6, 64), np.float32)
for _i, _t in enumerate((_gain, _base, _cour, _slope, _four, _push)):
    SCAL[_i, :NF] = _t
SCAL = SCAL.reshape(-1)


def scal(sm, kind, f):
    return sm[kind * 64 + f]


def place(i, d):
    return i // 3, (i % 3) * ND + 2 * d


def _lane_tables():
    tab = np.zeros((TILES, 8, 128), np.float32)
    tab[:, 1] = 1.0
    for f in range(NF):
        for d in range(HALF):
            h, j = place(f % FG, d)
            values = (_gain[f], _base[f], _cos[d], _sin[d], _four[f], _cour[f])
            for r, value in enumerate(values):
                tab[2 * (f // FG) + h, r, j : j + 2] = value
    return tab


def _dir_tables():
    tab = np.zeros((4, HALF, 128), np.float32)
    for s, dirs in enumerate((EASTWARD, WESTWARD)):
        tab[2 * s] = _cos[dirs][:, None]
        tab[2 * s + 1] = _sin[dirs][:, None]
    return tab


LANE_TAB = _lane_tables()
DIR_TAB = _dir_tables()
FOUR_COL = np.broadcast_to(_four[:, None], (NF, 128)).astype(np.float32)


def quartets():
    for d in range(QUAD):
        yield (d, 17 - d, 18 + d, 35 - d)


def iota(shape, dim):
    return lax.broadcasted_iota(jnp.int32, shape, dim)


def pack_edges(ref, g, lane):
    pair = lane // 2
    packed = [jnp.zeros((8, 128), F32) for _ in range(4)]
    for i in range(FG):
        for d in range(HALF):
            h, j = place(i, d)
            here = pair == j // 2
            e = ref[g * GB + i * ND + d]
            packed[h] = jnp.where(here, pltpu.roll(e, (j + 2) % 128, 1), packed[h])
            e = ref[g * GB + i * ND + HALF + d]
            packed[2 + h] = jnp.where(here, pltpu.roll(e, j, 1) if j else e, packed[2 + h])
    return packed


def first_kernel(spec_hbm, near_w, near_e, north, south, msq, spec, sems):
    lane = iota((8, 128), 1)

    def copy(g):
        at = pl.ds(g * GB, GB)
        return pltpu.make_async_copy(spec_hbm.at[at], spec.at[at], sems.at[g])

    for g in range(GROUPS):
        copy(g).start()
    msq[...] = jnp.zeros_like(msq)

    def group(g, growth):
        copy(g).wait()
        total = jnp.zeros((8, 128), F32)
        for i in range(FG):
            acc = jnp.zeros((8, 128), F32)
            for d in range(ND):
                e = spec[g * GB + i * ND + d]
                acc = acc + e
                if d in WESTWARD:
                    k = pl.ds(g * FG * HALF + i * HALF + WESTWARD.index(d), 1)
                    near_w[k, :] = e[0:1]
                else:
                    k = pl.ds(g * FG * HALF + i * HALF + EASTWARD.index(d), 1)
                    near_e[k, :] = e[7:8]
            total = total + float(_slope[i]) * acc
        msq[...] += growth * total
        north[2 * g], north[2 * g + 1], south[2 * g], south[2 * g + 1] = pack_edges(spec, g, lane)
        return growth * float(_slope[FG] / _slope[0])

    lax.fori_loop(0, GROUPS, group, jnp.float32(1.0))
    q = msq[...]
    for near, x in ((near_w, 0), (near_e, 7)):
        near[ROWS : ROWS + 1, :] = q[x : x + 1]
        near[ROWS + 1 : COL, :] = jnp.zeros((COL - ROWS - 1, 128), F32)


def sector_kernel(mask, winds, wrow, mine):
    for c in range(2):
        for r in range(16):
            mine[0, 16 * c + r : 16 * c + r + 1, :] = winds[c : c + 1, 128 * r : 128 * r + 128]
    mine[0, 32:40, :] = wrow[...].astype(F32)
    mine[0, 40:48, :] = mask[...].astype(F32)
    mine[0, 48:56, :] = jnp.zeros((8, 128), F32)
    rows = mine[0]
    for n in range(1, mine.shape[0]):
        mine[n] = rows


SMEM = pl.BlockSpec(memory_space=pltpu.SMEM)
VMEM = pl.BlockSpec(memory_space=pltpu.VMEM)
HBM = pl.BlockSpec(memory_space=pltpu.HBM)
TILE = jax.ShapeDtypeStruct((8, 128), F32)
FIELD = jax.ShapeDtypeStruct((NF * ND, 8, 128), F32)
STAGE = jax.ShapeDtypeStruct((4 * NF * ND, 8, 128), F32)
BUFFER = pltpu.VMEM((NF * ND, 8, 128), F32)
PARAMS = pltpu.CompilerParams(vmem_limit_bytes=30 * 2**20)
MIDDLE = pltpu.CompilerParams(vmem_limit_bytes=43 * 2**20)
WIDE = pltpu.CompilerParams(vmem_limit_bytes=48 * 2**20)
ALONE = pltpu.CompilerParams(vmem_limit_bytes=54 * 2**20)


def first_call(spectra):
    edge = jax.ShapeDtypeStruct((COL, 128), F32)
    pack = jax.ShapeDtypeStruct((TILES, 8, 128), F32)
    return pl.pallas_call(
        first_kernel,
        in_specs=[HBM],
        out_specs=[VMEM] * 5,
        out_shape=[edge, edge, pack, pack, TILE],
        scratch_shapes=[BUFFER, pltpu.SemaphoreType.DMA((GROUPS,))],
        compiler_params=WIDE,
        name="first",
    )(spectra)


def sector_call(mask, winds, wrow, lons):
    return pl.pallas_call(
        sector_kernel,
        in_specs=[VMEM] * 3,
        out_specs=VMEM,
        out_shape=jax.ShapeDtypeStruct((lons, 56, 128), F32),
        compiler_params=ALONE,
        name="sector",
    )(mask, winds, wrow)


def split3(x):
    a = x.astype(BF16)
    r = x - a.astype(F32)
    b = r.astype(BF16)
    c = (r - b.astype(F32)).astype(BF16)
    return a, b, c


def wind_kernel(
    me_ref, table, wrow, msq, mask, north, south, lane_tab,
    u_ref, v_ref, side_ref, fn, fs,
):
    srcs = table.shape[0]
    me = me_ref[0]
    hi_count = srcs * 16
    west = table.at[(me + srcs - 1) & (srcs - 1)]
    east = table.at[(me + 1) & (srcs - 1)]
    rows = [wrow[x : x + 1, :] for x in range(8)]
    for ref, x in ((west, 7), (east, 0)):
        rows.append(ref[32 + x : 33 + x, :].astype(jnp.int32))
    local = [r & (hi_count * 128 - 1) for r in rows]
    hi_iota = iota((hi_count, 128), 0)
    hots = []
    for r in local:
        hots.append(jnp.where(hi_iota == r // 128, 1.0, 0.0).astype(BF16))
    hot = jnp.concatenate(hots, axis=1)
    tab = jnp.concatenate(
        [table[:, 16 * c : 16 * c + 16].reshape(hi_count, 128) for c in range(2)], axis=1
    )
    got = None
    for part in split3(tab):
        term = lax.dot_general(
            part, hot, (((0,), (0,)), ((), ())), preferred_element_type=F32
        )
        got = term if got is None else got + term
    lo_iota = iota((128, 128), 0)
    us, vs = [], []
    for n, r in enumerate(local):
        pick = lo_iota == (r & 127)
        at = slice(n * 128, n * 128 + 128)
        us.append(jnp.sum(jnp.where(pick, got[0:128, at], 0.0), axis=0, keepdims=True))
        vs.append(jnp.sum(jnp.where(pick, got[128:256, at], 0.0), axis=0, keepdims=True))
    for x in range(8):
        u_ref[x : x + 1, :] = us[x]
        v_ref[x : x + 1, :] = vs[x]
    for n, (ref, x) in enumerate(((west, 7), (east, 0))):
        side_ref[3 * n : 3 * n + 1, :] = us[8 + n]
        side_ref[3 * n + 1 : 3 * n + 2, :] = vs[8 + n]
        side_ref[3 * n + 2 : 3 * n + 3, :] = ref[40 + x : 41 + x, :]
    side_ref[6:8, :] = jnp.zeros((2, 128), F32)

    maskf = mask[...].astype(F32)
    odd = (iota((8, 128), 1) & 1) == 1
    for edge, out, at, sign in ((north, fn, 126, 1.0), (south, fs, 0, -1.0)):
        pick = lambda a: jnp.where(
            odd,
            jnp.broadcast_to(a[:, at + 1 : at + 2], (8, 128)),
            jnp.broadcast_to(a[:, at : at + 1], (8, 128)),
        )
        ue, ve, me_, qe = pick(u_ref[...]), pick(v_ref[...]), pick(maskf), pick(msq[...])
        for n in range(TILES):
            lt = lane_tab[n]
            along = sign * (lt[2:3] * ue + lt[3:4] * ve)
            t = jnp.maximum(lt[0:1] * along + lt[1:2], 1.0)
            out[n * 8 : n * 8 + 8, :] = edge[n] * t * (me_ / (1.0 + lt[4:5] * qe))


def wind_call(me, table, wrow, msq, mask, north, south):
    edge = jax.ShapeDtypeStruct((TILES * 8, 128), F32)
    return pl.pallas_call(
        wind_kernel,
        in_specs=[SMEM] + [VMEM] * 7,
        out_specs=[VMEM] * 5,
        out_shape=[TILE, TILE, TILE, edge, edge],
        compiler_params=PARAMS,
        name="winds",
    )(me, table, wrow, msq, mask, north, south, jnp.asarray(LANE_TAB))


def bin_lane(s, i, row, up):
    north = 2 * (row + (0 if s == 0 else QUAD)) + 1
    south = 2 * (row + (0 if s == 0 else -QUAD))
    return jnp.where(up, north, south) + (i % 3) * ND


def wind_factor(sm, f, along):
    return jnp.maximum(scal(sm, 0, f) * along + scal(sm, 1, f), 1.0)


def put_row(dst_w, dst_e, f, d, e, x_east, x_west):
    if d in WESTWARD:
        dst_w[pl.ds(f * HALF + WESTWARD.index(d), 1), :] = e[x_west : x_west + 1]
    else:
        dst_e[pl.ds(f * HALF + EASTWARD.index(d), 1), :] = e[x_east : x_east + 1]


def along_table(along, u, v):
    for d in range(ND):
        along[d] = float(_cos[d]) * u + float(_sin[d]) * v


def shifted(gv, d, j, lane, halo_n, halo_s):
    xs = pltpu.roll(gv, 7 if d in WESTWARD else 1, 0)
    if d < HALF:
        halo = pltpu.roll(halo_n, 127 - j, 1)
        ys = jnp.where(lane == 0, halo, pltpu.roll(gv, 1, 1))
    else:
        halo = pltpu.roll(halo_s, 127 - j, 1)
        ys = jnp.where(lane == 127, halo, pltpu.roll(gv, 127, 1))
    return xs, ys


def step_one_kernel(
    sm, spec_hbm, u, v, msq, mask, rn, rs, out, msq2, in_w, in_e, to_w, to_e, spec, along, sems
):
    def copy(g):
        at = pl.ds(g * GB, GB)
        return pltpu.make_async_copy(spec_hbm.at[at], spec.at[at], sems.at[g])

    for g in range(GROUPS):
        copy(g).start()
    lane = iota((8, 128), 1)
    maskf = mask[...].astype(F32)
    along_table(along, u[...], v[...])
    msq2[...] = jnp.zeros_like(msq2)
    for col in (in_w, in_e, to_w, to_e):
        col[ROWS:COL, :] = jnp.zeros((COL - ROWS, 128), F32)

    @pl.loop(0, GROUPS)
    def _(g):
        copy(g).wait()
        total = jnp.zeros((8, 128), F32)
        tiles = [pl.ds(pl.multiple_of(g * 16 + 8 * h, 8), 8) for h in range(2)]
        halo_n = [rn[at, :] for at in tiles]
        halo_s = [rs[at, :] for at in tiles]
        for i in range(FG):
            f = g * FG + i
            cr = scal(sm, 2, f)
            fac = maskf / (1.0 + scal(sm, 4, f) * msq[...])
            a = scal(sm, 0, f) * fac
            b = scal(sm, 1, f) * fac
            acc = jnp.zeros((8, 128), F32)
            for quartet in quartets():
                d0 = quartet[0]
                kx = cr * float(abs(_cos[d0]))
                ky = cr * float(abs(_sin[d0]))
                k0 = 1.0 - kx - ky
                for d in quartet:
                    h, j = place(i, d % HALF)
                    gv = spec[f * ND + d] * jnp.maximum(a * along[d] + b, fac)
                    xs, ys = shifted(gv, d, j, lane, halo_n[h], halo_s[h])
                    e = k0 * gv + kx * xs + ky * ys
                    out[f * ND + d] = e
                    acc = acc + e
                    put_row(to_w, to_e, f, d, e, 7, 0)
                    put_row(in_e, in_w, f, d, e, 0, 7)
            total = total + scal(sm, 3, f) * acc
        msq2[...] += total


def step_one_call(spectra, u, v, msq, mask, rn, rs):
    column = jax.ShapeDtypeStruct((COL, 128), F32)
    return pl.pallas_call(
        step_one_kernel,
        in_specs=[SMEM, HBM] + [VMEM] * 6,
        out_specs=[VMEM] * 6,
        out_shape=[FIELD, TILE, column, column, column, column],
        scratch_shapes=[
            BUFFER,
            pltpu.VMEM((ND, 8, 128), F32),
            pltpu.SemaphoreType.DMA((GROUPS,)),
        ],
        compiler_params=MIDDLE,
        name="step_one",
    )(jnp.asarray(SCAL), spectra, u, v, msq, mask, rn, rs)


def mend_one_kernel(
    sm, near_w, near_e, own_w, own_e, in_w, in_e, to_w, to_e, part, msq, u, v, mask, side, fn, fs,
    lane_tab, dir_tab, four,
    msq2, row_w, row_e, col_w, col_e, fn2, fs2, corner_n, corner_s,
):
    row18 = iota((HALF, 128), 0)
    lane18 = iota((HALF, 128), 1)
    up = row18 < QUAD
    maskf = mask[...].astype(F32)
    msq2[...] = part[...]
    acc = {}
    for s, (near, own, src, dst, x, far) in enumerate(
        ((near_w, own_e, in_w, row_w, 0, 7), (near_e, own_w, in_e, row_e, 7, 0))
    ):
        cos = dir_tab[2 * s]
        sin = dir_tab[2 * s + 1]
        acos = jnp.abs(cos)
        u_row, v_row, mask_row = (side[3 * s + r : 3 * s + r + 1, :] for r in range(3))
        along = cos * u_row + sin * v_row
        fac = mask_row / (1.0 + four[...] * near[ROWS : ROWS + 1, :])
        along_own = cos * u[far : far + 1, :] + sin * v[far : far + 1, :]
        fac_own = maskf[far : far + 1] / (1.0 + four[...] * msq[far : far + 1, :])
        steep = jnp.zeros((HALF, 128), F32)
        for f in range(NF):
            at = slice(f * HALF, f * HALF + HALF)
            g1 = near[at, :] * wind_factor(sm, f, along) * fac[f : f + 1]
            ring = own[at, :] * wind_factor(sm, f, along_own) * fac_own[f : f + 1]
            fix = (scal(sm, 2, f) * acos) * (g1 - ring)
            dst[at, :] = src[at, :] + fix
            steep = steep + scal(sm, 3, f) * fix
            i = f % FG
            tile = 2 * (f // FG) + i // 3
            ends = jnp.where(
                up,
                jnp.broadcast_to(g1[:, 127:128], (HALF, 128)),
                jnp.broadcast_to(g1[:, 0:1], (HALF, 128)),
            )
            ends = jnp.where(lane18 == bin_lane(s, i, row18, up), ends, 0.0)
            for key, val in (("n", jnp.where(up, ends, 0.0)), ("s", jnp.where(up, 0.0, ends))):
                have = acc.get((key, tile))
                acc[(key, tile)] = val if have is None else have + val
        dst[ROWS:COL, :] = jnp.zeros((COL - ROWS, 128), F32)
        msq2[x : x + 1, :] = part[x : x + 1, :] + jnp.sum(steep, axis=0, keepdims=True)
    for key, out in (("n", corner_n), ("s", corner_s)):
        for tile in range(TILES):
            out[tile : tile + 1, :] = jnp.sum(acc[(key, tile)], axis=0, keepdims=True)
    msq2[...] = msq2[...] * maskf

    for s, (src, dst, x) in enumerate(((to_e, col_e, 7), (to_w, col_w, 0))):
        along = dir_tab[2 * s] * u[x : x + 1, :] + dir_tab[2 * s + 1] * v[x : x + 1, :]
        fac = maskf[x : x + 1] / (1.0 + four[...] * msq2[x : x + 1, :])
        for f in range(NF):
            at = slice(f * HALF, f * HALF + HALF)
            dst[at, :] = src[at, :] * wind_factor(sm, f, along) * fac[f : f + 1]
        dst[ROWS:COL, :] = jnp.zeros((COL - ROWS, 128), F32)

    sub = iota((8, 128), 0)
    for own, corner, dst, at, sign in ((fn, corner_n, fn2, 127, 1.0), (fs, corner_s, fs2, 0, -1.0)):
        pick = lambda z: jnp.broadcast_to(z[:, at : at + 1], (8, 128))
        ue, ve, me, qe = pick(u[...]), pick(v[...]), pick(maskf), pick(msq2[...])
        for n in range(TILES):
            lt = lane_tab[n]
            cos, sin = sign * lt[2:3], sign * lt[3:4]
            kx = lt[5:6] * jnp.abs(cos)
            ky = lt[5:6] * jnp.abs(sin)
            g1 = own[n * 8 : n * 8 + 8, :]
            row = corner[n : n + 1, :]
            from_w = jnp.where(sub == 0, row, pltpu.roll(g1, 1, 0))
            from_e = jnp.where(sub == 7, row, pltpu.roll(g1, 7, 0))
            xs = jnp.where(cos > 0.0, from_w, from_e)
            ys = pltpu.roll(g1, 1 if at else 127, 1)
            e = (1.0 - kx - ky) * g1 + kx * xs + ky * ys
            t = jnp.maximum(lt[0:1] * (cos * ue + sin * ve) + lt[1:2], 1.0)
            dst[n * 8 : n * 8 + 8, :] = e * t * (me / (1.0 + lt[4:5] * qe))


def mend_one_call(near_w, near_e, own_w, own_e, in_w, in_e, to_w, to_e, part, msq, u, v, mask, side, fn, fs):
    edge = jax.ShapeDtypeStruct((TILES * 8, 128), F32)
    column = jax.ShapeDtypeStruct((COL, 128), F32)
    return pl.pallas_call(
        mend_one_kernel,
        in_specs=[SMEM] + [VMEM] * 19,
        out_specs=[VMEM] * 7,
        out_shape=[TILE, column, column, column, column, edge, edge],
        scratch_shapes=[pltpu.VMEM((24, 128), F32), pltpu.VMEM((24, 128), F32)],
        compiler_params=PARAMS,
        name="mend_one",
    )(
        jnp.asarray(SCAL), near_w, near_e, own_w, own_e, in_w, in_e, to_w, to_e, part, msq, u, v,
        mask, side, fn, fs, jnp.asarray(LANE_TAB), jnp.asarray(DIR_TAB), jnp.asarray(FOUR_COL),
    )


def step_two_kernel(
    sm, spec, row_w, row_e, u, v, msq, mask, rn, rs, out, push, out_w, out_e, along, field, sems
):
    def copy(g):
        at = pl.ds(g * GB, GB)
        return pltpu.make_async_copy(field.at[at], out.at[at], sems.at[g])

    lane = iota((8, 128), 1)
    sub = iota((8, 128), 0)
    maskf = mask[...].astype(F32)
    along_table(along, u[...], v[...])
    push[...] = jnp.zeros_like(push)

    @pl.loop(0, GROUPS)
    def _(g):
        pu = jnp.zeros((8, 128), F32)
        pv = jnp.zeros((8, 128), F32)
        tiles = [pl.ds(pl.multiple_of(g * 16 + 8 * h, 8), 8) for h in range(2)]
        halo_n = [rn[at, :] for at in tiles]
        halo_s = [rs[at, :] for at in tiles]
        for i in range(FG):
            f = g * FG + i
            a, b, cr = scal(sm, 0, f), scal(sm, 1, f), scal(sm, 2, f)
            fac = maskf / (1.0 + scal(sm, 4, f) * msq[...])
            fu = jnp.zeros((8, 128), F32)
            fv = jnp.zeros((8, 128), F32)
            for quartet in quartets():
                d0 = quartet[0]
                kx = cr * float(abs(_cos[d0]))
                ky = cr * float(abs(_sin[d0]))
                k0 = 1.0 - kx - ky
                kxm = kx * maskf
                kym = ky * maskf
                q = []
                for d in quartet:
                    h, j = place(i, d % HALF)
                    t = jnp.maximum(a * along[d] + b, 1.0)
                    e = spec[f * ND + d]
                    if d in WESTWARD:
                        row = row_e[pl.ds(f * HALF + WESTWARD.index(d), 1), :]
                        e = jnp.where(sub == 7, jnp.broadcast_to(row, (8, 128)), e)
                    else:
                        row = row_w[pl.ds(f * HALF + EASTWARD.index(d), 1), :]
                        e = jnp.where(sub == 0, jnp.broadcast_to(row, (8, 128)), e)
                    gv = e * t * fac
                    xs, ys = shifted(gv, d, j, lane, halo_n[h], halo_s[h])
                    e = k0 * gv + kxm * xs + kym * ys
                    field[f * ND + d] = e
                    put_row(out_e, out_w, f, d, e, 0, 7)
                    q.append((t - 1.0) * e)
                lo = q[0] - q[2]
                hi = q[1] - q[3]
                fu = fu + float(_cos[d0]) * (lo - hi)
                fv = fv + float(_sin[d0]) * (lo + hi)
            pu = pu + scal(sm, 5, f) * fu
            pv = pv + scal(sm, 5, f) * fv
        push[0] += pu
        push[1] += pv
        copy(g).start()

    for col in (out_w, out_e):
        col[ROWS:COL, :] = jnp.zeros((COL - ROWS, 128), F32)
    for g in range(GROUPS):
        copy(g).wait()


def step_two_call(spec, row_w, row_e, u, v, msq, mask, rn, rs):
    column = jax.ShapeDtypeStruct((COL, 128), F32)
    return pl.pallas_call(
        step_two_kernel,
        in_specs=[SMEM] + [VMEM] * 9,
        out_specs=[HBM] + [VMEM] * 3,
        out_shape=[STAGE, jax.ShapeDtypeStruct((2, 8, 128), F32), column, column],
        scratch_shapes=[
            pltpu.VMEM((ND, 8, 128), F32),
            BUFFER,
            pltpu.SemaphoreType.DMA((GROUPS,)),
        ],
        compiler_params=PARAMS,
        name="step_two",
    )(jnp.asarray(SCAL), spec, row_w, row_e, u, v, msq, mask, rn, rs)


def mend_two_kernel(
    sm, halo_w, halo_e, sent_w, sent_e, out_w, out_e, push_in, u, v, mask, owner, weight, dir_tab,
    end_w, end_e, cells, push,
):
    maskf = mask[...].astype(F32)
    push[...] = push_in[...]
    for s, (halo, ring, src, dst, x) in enumerate(
        ((halo_w, sent_e, out_w, end_w, 0), (halo_e, sent_w, out_e, end_e, 7))
    ):
        cos = dir_tab[2 * s]
        sin = dir_tab[2 * s + 1]
        along = cos * u[x : x + 1, :] + sin * v[x : x + 1, :]
        weigh = jnp.abs(cos) * maskf[x : x + 1]
        total = jnp.zeros((HALF, 128), F32)
        for f in range(NF):
            at = slice(f * HALF, f * HALF + HALF)
            fix = (scal(sm, 2, f) * weigh) * (halo[at, :] - ring[at, :])
            dst[at, :] = src[at, :] + fix
            total = total + (scal(sm, 5, f) * (wind_factor(sm, f, along) - 1.0)) * fix
        dst[ROWS:COL, :] = jnp.zeros((COL - ROWS, 128), F32)
        for c, part in ((0, cos), (1, sin)):
            push[c, x : x + 1, :] = push_in[c, x : x + 1, :] + jnp.sum(part * total, axis=0, keepdims=True)

    uu, vv = u[...], v[...]
    share = weight[...].astype(F32) * maskf
    tau = 0.02 * (uu * uu + vv * vv) + 0.25
    terms = (share, share * tau, share * push[0], share * push[1])
    parts = [split3(t) for t in terms]
    dests = cells.shape[0]
    own = owner[...] & (dests * 512 - 1)
    hi_own = own // 128
    lo_own = own & 127
    row = iota((dests * 16, 128), 0)
    want = (row // 16) * 4 + row % 4
    lo_iota = iota((128, 128), 0)
    kind = iota((16, 128), 0) // 4
    total = jnp.zeros((dests * 16, 128), F32)
    for x in range(8):
        hot = jnp.where(lo_iota == lo_own[x : x + 1], 1.0, 0.0).astype(BF16)
        match = want == hi_own[x : x + 1]
        for p in range(3):
            rows = [parts[k][p][x : x + 1].astype(F32) for k in range(4)]
            tile = jnp.where(
                kind == 0, rows[0],
                jnp.where(kind == 1, rows[1], jnp.where(kind == 2, rows[2], rows[3])),
            )
            lhs = jnp.where(match, jnp.concatenate([tile] * dests, axis=0), 0.0).astype(BF16)
            total = total + lax.dot_general(
                lhs, hot, (((1,), (1,)), ((), ())), preferred_element_type=F32
            )
    cells[...] = total.reshape(dests, 16, 128)


def mend_two_call(
    halo_w, halo_e, sent_w, sent_e, out_w, out_e, push, u, v, mask, owner, weight, dests
):
    column = jax.ShapeDtypeStruct((COL, 128), F32)
    return pl.pallas_call(
        mend_two_kernel,
        in_specs=[SMEM] + [VMEM] * 13,
        out_specs=[VMEM] * 3,
        out_shape=[column, column, jax.ShapeDtypeStruct((dests, 16, 128), F32)],
        scratch_shapes=[pltpu.VMEM((2, 8, 128), F32)],
        compiler_params=PARAMS,
        name="mend_two",
    )(
        jnp.asarray(SCAL), halo_w, halo_e, sent_w, sent_e, out_w, out_e, push, u, v, mask, owner,
        weight, jnp.asarray(DIR_TAB),
    )


def output_kernel(stage, end_w, end_e, out, field, whole, sems_in, sems):
    sub = iota((8, 128), 0)

    def copy_in(g):
        at = pl.ds(g * GB, GB)
        return pltpu.make_async_copy(stage.at[at], field.at[at], sems_in.at[g])

    def copy(g):
        at = pl.ds(g * GB, GB)
        return pltpu.make_async_copy(whole.at[at], out.at[at], sems.at[g])

    for g in range(GROUPS):
        copy_in(g).start()

    @pl.loop(0, GROUPS)
    def _(g):
        copy_in(g).wait()
        for i in range(FG):
            f = g * FG + i
            for d in range(ND):
                if d in WESTWARD:
                    row = end_e[pl.ds(f * HALF + WESTWARD.index(d), 1), :]
                    x = 7
                else:
                    row = end_w[pl.ds(f * HALF + EASTWARD.index(d), 1), :]
                    x = 0
                whole[f * ND + d] = jnp.where(sub == x, jnp.broadcast_to(row, (8, 128)), field[f * ND + d])
        copy(g).start()

    for g in range(GROUPS):
        copy(g).wait()


def output_call(field, end_w, end_e):
    return pl.pallas_call(
        output_kernel,
        in_specs=[HBM, VMEM, VMEM],
        out_specs=HBM,
        out_shape=FIELD,
        scratch_shapes=[
            BUFFER,
            BUFFER,
            pltpu.SemaphoreType.DMA((GROUPS,)),
            pltpu.SemaphoreType.DMA((GROUPS,)),
        ],
        compiler_params=PARAMS,
        name="output",
    )(field, end_w, end_e)


def cell_kernel(parts, stress, rough):
    sums = jnp.sum(parts[...], axis=0)
    w, a, bx, by = (sums[4 * k : 4 * k + 4] for k in range(4))
    total_w = jnp.maximum(w, 1.0)
    sx = bx / total_w
    sy = by / total_w
    low = jnp.maximum(a, 1.0)
    r = jnp.sqrt(1.0 + (bx * bx + by * by) / (low * low)) * a / total_w
    for n in range(4):
        at = slice(n * 128, n * 128 + 128)
        stress[0:1, at] = sx[n : n + 1]
        stress[1:2, at] = sy[n : n + 1]
        rough[0:1, at] = r[n : n + 1]


def cell_call(parts):
    return pl.pallas_call(
        cell_kernel,
        out_shape=[jax.ShapeDtypeStruct((2, 512), F32), jax.ShapeDtypeStruct((1, 512), F32)],
        name="cells",
    )(parts)


def body(spectra, sea_mask, atm_wind, wind_row, owner, weight):
    lons = lax.axis_size("lon")
    lats = lax.axis_size("lat")
    eastward = [(i, (i + 1) % lons) for i in range(lons)]
    westward = [(i, (i - 1) % lons) for i in range(lons)]
    northward = [(i, i + 1) for i in range(lats - 1)]
    southward = [(i + 1, i) for i in range(lats - 1)]

    me = lax.axis_index("lon").astype(jnp.int32)
    mine = sector_call(sea_mask, atm_wind, wind_row, lons)
    spectra, mine = lax.optimization_barrier((spectra, mine))
    own_w, own_e, north, south, msq1 = first_call(spectra)
    table = lax.all_to_all(mine, "lon", 0, 0)
    near_w = lax.ppermute(own_e, "lon", eastward)
    near_e = lax.ppermute(own_w, "lon", westward)
    u, v, side, fn, fs = wind_call(
        me.reshape(1), table, wind_row, msq1, sea_mask, north, south
    )
    rn = lax.ppermute(fn, "lat", northward)
    rs = lax.ppermute(fs, "lat", southward)
    energy, part, in_w, in_e, to_w, to_e = step_one_call(
        spectra, u, v, msq1, sea_mask, rn, rs
    )
    msq2, row_w, row_e, col_w, col_e, fn2, fs2 = mend_one_call(
        near_w, near_e, own_w, own_e, in_w, in_e, to_w, to_e, part, msq1, u, v, sea_mask, side, fn, fs
    )
    halo_w = lax.ppermute(col_e, "lon", eastward)
    halo_e = lax.ppermute(col_w, "lon", westward)
    rn = lax.ppermute(fn2, "lat", northward)
    rs = lax.ppermute(fs2, "lat", southward)
    field, push, out_w, out_e = step_two_call(energy, row_w, row_e, u, v, msq2, sea_mask, rn, rs)
    end_w, end_e, cells = mend_two_call(
        halo_w, halo_e, col_w, col_e, out_w, out_e, push, u, v, sea_mask, owner, weight, lons
    )
    parts = lax.all_to_all(cells, "lon", 0, 0)
    energy = output_call(field, end_w, end_e)
    stress, rough = cell_call(parts)
    return energy, stress, rough.reshape(512)


def solution(mesh):
    in_specs = (
        P(None, "lon", "lat"),
        P("lon", "lat"),
        P(None, ("lat", "lon")),
        P("lon", "lat"),
        P("lon", "lat"),
        P("lon", "lat"),
    )
    out_specs = (P(None, "lon", "lat"), P(None, ("lat", "lon")), P(("lat", "lon")))
    return jax.shard_map(body, mesh=mesh, in_specs=in_specs, out_specs=out_specs, check_vma=False)
```

time: 82.9 us -> 75.9 us (0.916)
  blocking collectives: 13.2 us -> 0 us
  Pallas kernels: 24.2 us -> 32.2 us
  waiting for transfers between devices: 13 us -> 8.53 us
  starting transfers between devices: 30.9 us -> 33.2 us
    all_to_all x1 -> x0, blocking collectives: 13.2 us -> none  [body(): parts = lax.all_to_all(cells, 'lon', 0, 0)]
    pallas_call x2 -> x5, Pallas kernels: 15.9 us -> 23.8 us  [the longest x1 6.85 us: step_two_call(): pl.pallas_call(step_two_kernel, in_specs=[SMEM] + [VMEM] * 9, out_specs=[...]
    all_to_all x0 -> x1, starting transfers between devices: none -> 3.51 us  [body(): parts = lax.all_to_all(cells, 'lon', 0, 0)]
    all_to_all x1, waiting for transfers between devices: 3.84 us -> 0.33 us  [body(): table = lax.all_to_all(mine, 'lon', 0, 0)]
    ppermute x4, waiting for transfers between devices: 2.07 us -> 0.01 us  [the longest x1 0.01 us: body(): halo_w = lax.ppermute(col_e, 'lon', eastward)]
    ppermute x1, starting transfers between devices: 6.16 us -> 5.31 us  [body(): rn = lax.ppermute(fn, 'lat', northward)]
  transfers between devices with their start and end apart: 9 -> 10, of which waited for: 4 -> 4; matrix products, arithmetic and copies ran while one was open for 0% -> 0% of each run, Pallas kernels for 6% -> 33%
where the time goes in v3:
time: 75.9 us; the launch traced here: 75.5 us
  starting transfers between devices  33.2 us (44%)
  Pallas kernels  32.2 us (42%)
  waiting for transfers between devices  8.53 us (11%)
  between operations  0.87 us (1%)
    all_to_all x1, starting transfers between devices, body(): table = lax.all_to_all(mine, 'lon', 0, 0)  8.43 us
    pallas_call x1, Pallas kernels, step_two_call(): pl.pallas_call(step_two_kernel, in_specs=[SMEM] + [VMEM] * 9, out_specs=[...  6.85 us
    pallas_call x1, Pallas kernels, step_one_call(): pl.pallas_call(step_one_kernel, in_specs=[SMEM, HBM] + [VMEM] * 6, out_sp...  6.49 us
    pallas_call x1, Pallas kernels, output_call(): pl.pallas_call(output_kernel, in_specs=[HBM, VMEM, VMEM], out_specs=HBM,...  6.08 us
    ppermute x1, starting transfers between devices, body(): rn = lax.ppermute(fn, 'lat', northward)  5.31 us
    ppermute x1, starting transfers between devices, body(): halo_e = lax.ppermute(col_w, 'lon', westward)  4.5 us
    pallas_call x1, Pallas kernels, first_call(): pl.pallas_call(first_kernel, in_specs=[HBM], out_specs=[VMEM] * 5, out_sh...  4.34 us
    ppermute x1, waiting for transfers between devices, body(): rs = lax.ppermute(fs2, 'lat', southward)  3.82 us
  transfers between devices with their start and end apart: 10, of which 4 were waited for; matrix products, arithmetic and copies ran while one was open for 0% of the time, Pallas kernels for 33%

profile of v3, /device:TPU:1, one launch (start us, length us, event | category | flops | bytes accessed | tf_op | source)
XLA Modules:
  0.0 75.5 jit_solution(7205635885336121151)
XLA Ops:
  0.6 0.0 copy-start
  0.6 0.0 copy-start.3
  0.7 1.6 %sector.1 = f32[16,56,128]{2,1,0:T(8,128)} custom-call(s32[8,128]{1,0:T(8,128)} %mask.11, f32[2,2048]{1,0:T(2,128)} %winds.2, s32[8,128]{1,0:T(8,128)} %wrow.3), custom_call_target="tpu_custom_call" | custom-call | tf_op jit(solution)/shard_map/sector/pallas_call | solution.py:178
  2.2 8.4 %all-to-all-start = ((f32[16,56,128]{2,1,0:T(8,128)}), f32[16,56,128]{2,1,0:T(8,128)S(1)}, u32[]{:S(2)}, u32[]{:S(2)}) async-start(f32[16,56,128]{2,1,0:T(8,128)} %sector.1), calls=%async_computation | async-start | bytes 917504 | tf_op jit(solution)/shard_map/all_to_all | solution.py:697
  10.7 0.0 copy-start.1
  10.7 0.0 copy-start.4
  10.7 4.3 %first.1 = (f32[904,128]{1,0:T(8,128)S(1)}, f32[904,128]{1,0:T(8,128)S(1)}, f32[20,8,128]{2,1,0:T(8,128)S(1)}, f32[20,8,128]{2,1,0:T(8,128)S(1)}, f32[8,128]{1,0:T(8,128)S(1)}) custom-call(f32[1800,8,128]{2,1,0:T(8,128)} %spec_hbm.1), custom_call_target="tpu_custom_call" | custom-call | tf_op jit(solution)/shard_map/first/pallas_call | solution.py:166
  15.0 1.4 %collective-permute-start.2 = (f32[904,128]{1,0:T(8,128)S(1)}, f32[904,128]{1,0:T(8,128)S(1)}, u32[]{:S(2)}, u32[]{:S(2)}) collective-permute-start(f32[904,128]{1,0:T(8,128)S(1)} %get-tuple-element.47.own_e), channel_id=1, source_target_pairs={{0,1},{1,2},{2,3},{3,4},{4,5},{5,6},{6,7},{7,8},{8,9},{9,10},{10,1... | collective-permute-start | bytes 1388552 | tf_op jit(solution)/shard_map/ppermute | solution.py:698
  16.5 3.4 %collective-permute-start.3 = (f32[904,128]{1,0:T(8,128)S(1)}, f32[904,128]{1,0:T(8,128)S(1)}, u32[]{:S(2)}, u32[]{:S(2)}) collective-permute-start(f32[904,128]{1,0:T(8,128)S(1)} %get-tuple-element.48.own_w), channel_id=1, source_target_pairs={{0,15},{1,0},{2,1},{3,2},{4,3},{5,4},{6,5},{7,6},{8,7},{9,8},{10,9... | collective-permute-start | bytes 1388552 | tf_op jit(solution)/shard_map/ppermute | solution.py:699
  19.9 0.3 all-to-all-done.table
  20.2 0.9 %winds.3 = (f32[8,128]{1,0:T(8,128)S(1)}, f32[8,128]{1,0:T(8,128)S(1)}, f32[8,128]{1,0:T(8,128)S(1)}, f32[160,128]{1,0:T(8,128)S(1)}, f32[160,128]{1,0:T(8,128)S(1)}) custom-call(s32[1]{0:T(128)} %bitcast.me_ref, f32[16,56,128]{2,1,0:T(8,128)S(1)} %all-to-all-done.table, s32[8,128]{1,0:T(8,128)S(1)} %copy-done.5, f32[8,128]{1,0:T(8,128)S(1)} %get-tuple-element.39.msq, ...), custom_call_target="tpu_custom_call" | custom-call | tf_op jit(solution)/shard_map/winds/pallas_call | solution.py:257
  21.2 5.3 %collective-permute-start = (f32[160,128]{1,0:T(8,128)S(1)}, f32[160,128]{1,0:T(8,128)S(1)}, u32[]{:S(2)}, u32[]{:S(2)}) collective-permute-start(f32[160,128]{1,0:T(8,128)S(1)} %get-tuple-element.44.fn), channel_id=1, source_target_pairs={{0,16},{16,32},{32,48},{48,64},{64,80},{80,96},{96,112},{1,17},{17... | collective-permute-start | bytes 245768 | tf_op jit(solution)/shard_map/ppermute | solution.py:703
  26.5 1.9 %collective-permute-start.1 = (f32[160,128]{1,0:T(8,128)S(1)}, f32[160,128]{1,0:T(8,128)S(1)}, u32[]{:S(2)}, u32[]{:S(2)}) collective-permute-start(f32[160,128]{1,0:T(8,128)S(1)} %get-tuple-element.45.fs), channel_id=1, source_target_pairs={{16,0},{32,16},{48,32},{64,48},{80,64},{96,80},{112,96},{17,1},{33... | collective-permute-start | bytes 245768 | tf_op jit(solution)/shard_map/ppermute | solution.py:704
  28.4 0.0 collective-permute-done.rn
  28.4 3.8 %collective-permute-done.1.rs = f32[160,128]{1,0:T(8,128)S(1)} collective-permute-done((f32[160,128]{1,0:T(8,128)S(1)}, f32[160,128]{1,0:T(8,128)S(1)}, u32[]{:S(2)}, u32[]{:S(2)}) %collective-permute-start.1) | collective-permute-done | bytes 81952 | tf_op jit(solution)/shard_map/ppermute | solution.py:704
  32.2 6.5 %step_one.1 = (f32[1800,8,128]{2,1,0:T(8,128)S(1)}, f32[8,128]{1,0:T(8,128)S(1)}, f32[904,128]{1,0:T(8,128)S(1)}, f32[904,128]{1,0:T(8,128)S(1)}, f32[904,128]{1,0:T(8,128)S(1)}, /*index=5*/f32[904,128]{1,0:T(8,128)S(1)}) custom-call(f32[384]{0:T(512)S(1)} %copy-done.3, f32[1800,8,128]{2,1,0:T(8,128)} %spec_hbm.1, f32[8,128]{1,0:T(8,128)S(1)} %get-tuple-element.42.u, ...), custom_call_target="tpu_custom_call" | custom-call | tf_op jit(solution)/shard_map/step_one/pallas_call | solution.py:350
  38.7 0.0 copy-start.6
  38.7 0.0 copy-start.7
  38.8 2.1 %mend_one.1 = (f32[8,128]{1,0:T(8,128)S(1)}, f32[904,128]{1,0:T(8,128)S(1)}, f32[904,128]{1,0:T(8,128)S(1)}, f32[904,128]{1,0:T(8,128)S(1)}, f32[904,128]{1,0:T(...) custom-call(f32[384]{0:T(512)S(1)} %copy-done.3, f32[904,128]{1,0:T(8,128)S(1)} %collective-permute-done.2.near_w, ...), custom_call_target="tpu_custom_call" | custom-call | tf_op jit(solution)/shard_map/mend_one/pallas_call | solution.py:444
  40.9 0.4 collective-permute-start.6
  41.3 4.5 %collective-permute-start.7 = (f32[904,128]{1,0:T(8,128)S(1)}, f32[904,128]{1,0:T(8,128)S(1)}, u32[]{:S(2)}, u32[]{:S(2)}) collective-permute-start(f32[904,128]{1,0:T(8,128)S(1)} %get-tuple-element.62.sent_w), channel_id=1, source_target_pairs={{0,15},{1,0},{2,1},{3,2},{4,3},{5,4},{6,5},{7,6},{8,7},{9,8},{10,9... | collective-permute-start | bytes 1388552 | tf_op jit(solution)/shard_map/ppermute | solution.py:712
  45.8 2.4 %collective-permute-start.4 = (f32[160,128]{1,0:T(8,128)S(1)}, f32[160,128]{1,0:T(8,128)S(1)}, u32[]{:S(2)}, u32[]{:S(2)}) collective-permute-start(f32[160,128]{1,0:T(8,128)S(1)} %get-tuple-element.58), channel_id=1, source_target_pairs={{0,16},{16,32},{32,48},{48,64},{64,80},{80,96},{96,112},{1,17},{17... | collective-permute-start | bytes 245768 | tf_op jit(solution)/shard_map/ppermute | solution.py:713
  48.2 1.9 %collective-permute-start.5 = (f32[160,128]{1,0:T(8,128)S(1)}, f32[160,128]{1,0:T(8,128)S(1)}, u32[]{:S(2)}, u32[]{:S(2)}) collective-permute-start(f32[160,128]{1,0:T(8,128)S(1)} %get-tuple-element.59), channel_id=1, source_target_pairs={{16,0},{32,16},{48,32},{64,48},{80,64},{96,80},{112,96},{17,1},{33... | collective-permute-start | bytes 245768 | tf_op jit(solution)/shard_map/ppermute | solution.py:714
  50.1 0.0 collective-permute-done.4.rn
  50.1 3.8 %collective-permute-done.5.rs = f32[160,128]{1,0:T(8,128)S(1)} collective-permute-done((f32[160,128]{1,0:T(8,128)S(1)}, f32[160,128]{1,0:T(8,128)S(1)}, u32[]{:S(2)}, u32[]{:S(2)}) %collective-permute-start.5) | collective-permute-done | bytes 81952 | tf_op jit(solution)/shard_map/ppermute | solution.py:714
  53.9 6.9 %step_two.1 = (f32[7200,8,128]{2,1,0:T(8,128)}, f32[2,8,128]{2,1,0:T(8,128)S(1)}, f32[904,128]{1,0:T(8,128)S(1)}, f32[904,128]{1,0:T(8,128)S(1)}) custom-call(f32[384]{0:T(512)S(1)} %copy-done.3, f32[1800,8,128]{2,1,0:T(8,128)S(1)} %get-tuple-element.46.spec, f32[904,128]{1,0:T(8,128)S(1)} %get-tuple-element.55.row_w, ...), custom_call_target="tpu_custom_call" | custom-call | tf_op jit(solution)/shard_map/step_two/pallas_call | solution.py:526
  60.8 2.3 %mend_two.1 = (f32[904,128]{1,0:T(8,128)S(1)}, f32[904,128]{1,0:T(8,128)S(1)}, f32[16,16,128]{2,1,0:T(8,128)}) custom-call(f32[384]{0:T(512)S(1)} %copy-done.3, f32[904,128]{1,0:T(8,128)S(1)} %collective-permute-done.6.halo_w, f32[904,128]{1,0:T(8,128)S(1)} %collective-permute-done.7.halo_e, f32[904,128]{1,0:T(8,128)S(1)} %get-tuple-element.62.sent_w, ...), custom_call_target="tpu_custom_call" | custom-call | tf_op jit(solution)/shard_map/mend_two/pallas_call | solution.py:598
  63.1 3.5 %all-to-all-start.1 = ((f32[16,16,128]{2,1,0:T(8,128)}), f32[16,16,128]{2,1,0:T(8,128)S(1)}, u32[]{:S(2)}, u32[]{:S(2)}) async-start(f32[16,16,128]{2,1,0:T(8,128)} %get-tuple-element.68), calls=%async_computation.1 | async-start | bytes 262144 | tf_op jit(solution)/shard_map/all_to_all | solution.py:719
  66.7 6.1 %output.1 = f32[1800,8,128]{2,1,0:T(8,128)} custom-call(f32[7200,8,128]{2,1,0:T(8,128)} %get-tuple-element.60.stage, f32[904,128]{1,0:T(8,128)S(1)} %get-tuple-element.66.end_w, f32[904,128]{1,0:T(8,128)S(1)} %get-tuple-element.67.end_e), custom_call_target="tpu_custom_call" | custom-call | tf_op jit(solution)/shard_map/output/pallas_call | solution.py:646
  72.8 0.5 all-to-all-done.1.parts
  73.3 0.6 copy-done.8
  73.9 1.5 %cells.1 = (f32[2,512]{1,0:T(2,128)}, f32[1,512]{1,0:T(1,128)}) custom-call(f32[16,16,128]{2,1,0:T(8,128)} %copy-done.8), custom_call_target="tpu_custom_call" | custom-call | tf_op jit(solution)/shard_map/cells/pallas_call | solution.py:678
  (15 shorter events, 0.0 us)
Async XLA Ops:
  0.6 19.6 %copy-start = (f32[20,8,128]{2,1,0:T(8,128)S(1)}, f32[20,8,128]{2,1,0:T(8,128)}, u32[]{:S(2)}) copy-start(f32[20,8,128]{2,1,0:T(8,128)} %constant.12.clone.lane_tab) | copy-start | bytes 245764
  0.6 31.6 %copy-start.3 = (f32[384]{0:T(512)S(1)}, f32[384]{0:T(512)}, u32[]{:S(2)}) copy-start(f32[384]{0:T(512)} %constant.13.clone.sm) | copy-start | bytes 4612
  0.7 19.6 %copy-start.2 = (s32[8,128]{1,0:T(8,128)S(1)}, s32[8,128]{1,0:T(8,128)}, u32[]{:S(2)}) copy-start(s32[8,128]{1,0:T(8,128)} %mask.11) | copy-start | bytes 12292
  0.7 19.6 %copy-start.5 = (s32[8,128]{1,0:T(8,128)S(1)}, s32[8,128]{1,0:T(8,128)}, u32[]{:S(2)}) copy-start(s32[8,128]{1,0:T(8,128)} %wrow.3) | copy-start | bytes 12292
  2.2 18.0 %all-to-all-start = ((f32[16,56,128]{2,1,0:T(8,128)}), f32[16,56,128]{2,1,0:T(8,128)S(1)}, u32[]{:S(2)}, u32[]{:S(2)}) async-start(f32[16,56,128]{2,1,0:T(8,128)} %sector.1), calls=%async_computation | async-start | bytes 917504 | tf_op jit(solution)/shard_map/all_to_all | solution.py:697
  10.7 28.1 %copy-start.1 = (f32[4,18,128]{2,1,0:T(8,128)S(1)}, f32[4,18,128]{2,1,0:T(8,128)}, u32[]{:S(2)}) copy-start(f32[4,18,128]{2,1,0:T(8,128)} %constant.14.clone.dir_tab) | copy-start | bytes 110596
  10.7 28.1 %copy-start.4 = (f32[50,128]{1,0:T(8,128)S(1)}, f32[50,128]{1,0:T(8,128)}, u32[]{:S(2)}) copy-start(f32[50,128]{1,0:T(8,128)} %constant.15.clone.four) | copy-start | bytes 76804
  15.0 23.7 %collective-permute-start.2 = (f32[904,128]{1,0:T(8,128)S(1)}, f32[904,128]{1,0:T(8,128)S(1)}, u32[]{:S(2)}, u32[]{:S(2)}) collective-permute-start(f32[904,128]{1,0:T(8,128)S(1)} %get-tuple-element.47.own_e), channel_id=1, source_target_pairs={{0,1},{1,2},{2,3},{3,4},{4,5},{5,6},{6,7},{7,8},{8,9},{9,10},{10,1... | collective-permute-start | bytes 1388552 | tf_op jit(solution)/shard_map/ppermute | solution.py:698
  16.5 22.3 %collective-permute-start.3 = (f32[904,128]{1,0:T(8,128)S(1)}, f32[904,128]{1,0:T(8,128)S(1)}, u32[]{:S(2)}, u32[]{:S(2)}) collective-permute-start(f32[904,128]{1,0:T(8,128)S(1)} %get-tuple-element.48.own_w), channel_id=1, source_target_pairs={{0,15},{1,0},{2,1},{3,2},{4,3},{5,4},{6,5},{7,6},{8,7},{9,8},{10,9... | collective-permute-start | bytes 1388552 | tf_op jit(solution)/shard_map/ppermute | solution.py:699
  21.2 7.2 %collective-permute-start = (f32[160,128]{1,0:T(8,128)S(1)}, f32[160,128]{1,0:T(8,128)S(1)}, u32[]{:S(2)}, u32[]{:S(2)}) collective-permute-start(f32[160,128]{1,0:T(8,128)S(1)} %get-tuple-element.44.fn), channel_id=1, source_target_pairs={{0,16},{16,32},{32,48},{48,64},{64,80},{80,96},{96,112},{1,17},{17... | collective-permute-start | bytes 245768 | tf_op jit(solution)/shard_map/ppermute | solution.py:703
  26.5 5.8 %collective-permute-start.1 = (f32[160,128]{1,0:T(8,128)S(1)}, f32[160,128]{1,0:T(8,128)S(1)}, u32[]{:S(2)}, u32[]{:S(2)}) collective-permute-start(f32[160,128]{1,0:T(8,128)S(1)} %get-tuple-element.45.fs), channel_id=1, source_target_pairs={{16,0},{32,16},{48,32},{64,48},{80,64},{96,80},{112,96},{17,1},{33... | collective-permute-start | bytes 245768 | tf_op jit(solution)/shard_map/ppermute | solution.py:704
  38.7 22.1 %copy-start.6 = (s32[8,128]{1,0:T(8,128)S(1)}, s32[8,128]{1,0:T(8,128)}, u32[]{:S(2)}) copy-start(s32[8,128]{1,0:T(8,128)} %owner.1) | copy-start | bytes 12292
  38.7 22.1 %copy-start.7 = (s32[8,128]{1,0:T(8,128)S(1)}, s32[8,128]{1,0:T(8,128)}, u32[]{:S(2)}) copy-start(s32[8,128]{1,0:T(8,128)} %weight.1) | copy-start | bytes 12292
  40.9 19.9 %collective-permute-start.6 = (f32[904,128]{1,0:T(8,128)S(1)}, f32[904,128]{1,0:T(8,128)S(1)}, u32[]{:S(2)}, u32[]{:S(2)}) collective-permute-start(f32[904,128]{1,0:T(8,128)S(1)} %get-tuple-element.61.sent_e), channel_id=1, source_target_pairs={{0,1},{1,2},{2,3},{3,4},{4,5},{5,6},{6,7},{7,8},{8,9},{9,10},{10,1... | collective-permute-start | bytes 1388552 | tf_op jit(solution)/shard_map/ppermute | solution.py:711
  41.3 19.5 %collective-permute-start.7 = (f32[904,128]{1,0:T(8,128)S(1)}, f32[904,128]{1,0:T(8,128)S(1)}, u32[]{:S(2)}, u32[]{:S(2)}) collective-permute-start(f32[904,128]{1,0:T(8,128)S(1)} %get-tuple-element.62.sent_w), channel_id=1, source_target_pairs={{0,15},{1,0},{2,1},{3,2},{4,3},{5,4},{6,5},{7,6},{8,7},{9,8},{10,9... | collective-permute-start | bytes 1388552 | tf_op jit(solution)/shard_map/ppermute | solution.py:712
  45.8 4.3 %collective-permute-start.4 = (f32[160,128]{1,0:T(8,128)S(1)}, f32[160,128]{1,0:T(8,128)S(1)}, u32[]{:S(2)}, u32[]{:S(2)}) collective-permute-start(f32[160,128]{1,0:T(8,128)S(1)} %get-tuple-element.58), channel_id=1, source_target_pairs={{0,16},{16,32},{32,48},{48,64},{64,80},{80,96},{96,112},{1,17},{17... | collective-permute-start | bytes 245768 | tf_op jit(solution)/shard_map/ppermute | solution.py:713
  48.2 5.8 %collective-permute-start.5 = (f32[160,128]{1,0:T(8,128)S(1)}, f32[160,128]{1,0:T(8,128)S(1)}, u32[]{:S(2)}, u32[]{:S(2)}) collective-permute-start(f32[160,128]{1,0:T(8,128)S(1)} %get-tuple-element.59), channel_id=1, source_target_pairs={{16,0},{32,16},{48,32},{64,48},{80,64},{96,80},{112,96},{17,1},{33... | collective-permute-start | bytes 245768 | tf_op jit(solution)/shard_map/ppermute | solution.py:714
  63.1 10.1 %all-to-all-start.1 = ((f32[16,16,128]{2,1,0:T(8,128)}), f32[16,16,128]{2,1,0:T(8,128)S(1)}, u32[]{:S(2)}, u32[]{:S(2)}) async-start(f32[16,16,128]{2,1,0:T(8,128)} %get-tuple-element.68), calls=%async_computation.1 | async-start | bytes 262144 | tf_op jit(solution)/shard_map/all_to_all | solution.py:719
  73.3 0.6 copy-start.8

commit v4 on v3

--- a/solution.py
+++ b/solution.py
@@ -56,7 +56,9 @@
     for f in range(NF):
         for d in range(HALF):
             h, j = place(f % FG, d)
-            values = (_gain[f], _base[f], _cos[d], _sin[d], _four[f], _cour[f])
+            values = (
+                _gain[f], _base[f], _cos[d], _sin[d], _four[f], _cour[f], _slope[f], _push[f]
+            )
             for r, value in enumerate(values):
                 tab[2 * (f // FG) + h, r, j : j + 2] = value
     return tab
@@ -286,19 +288,22 @@
         along[d] = float(_cos[d]) * u + float(_sin[d]) * v
 
 
-def shifted(gv, d, j, lane, halo_n, halo_s):
-    xs = pltpu.roll(gv, 7 if d in WESTWARD else 1, 0)
-    if d < HALF:
-        halo = pltpu.roll(halo_n, 127 - j, 1)
-        ys = jnp.where(lane == 0, halo, pltpu.roll(gv, 1, 1))
-    else:
-        halo = pltpu.roll(halo_s, 127 - j, 1)
-        ys = jnp.where(lane == 127, halo, pltpu.roll(gv, 127, 1))
-    return xs, ys
+def shifted(gv, d):
+    return pltpu.roll(gv, 7 if d in WESTWARD else 1, 0), pltpu.roll(gv, 1 if d < HALF else 127, 1)
+
+
+def lane_patch(tiles_n, tiles_s, i, d, lane):
+    h, j = place(i, d % HALF)
+    tile, at = (tiles_n[h], 0) if d < HALF else (tiles_s[h], 127)
+    return jnp.where(lane == at, pltpu.roll(tile, 127 - j, 1), 0.0)
+
+
+def group_tiles(ref, g):
+    return [ref[pl.ds(pl.multiple_of(g * 16 + 8 * h, 8), 8), :] for h in range(2)]
 
 
 def step_one_kernel(
-    sm, spec_hbm, u, v, msq, mask, rn, rs, out, msq2, in_w, in_e, to_w, to_e, spec, along, sems
+    sm, spec_hbm, u, v, msq, mask, out, msq2, in_w, in_e, to_w, to_e, spec, along, sems
 ):
     def copy(g):
         at = pl.ds(g * GB, GB)
@@ -306,7 +311,6 @@
 
     for g in range(GROUPS):
         copy(g).start()
-    lane = iota((8, 128), 1)
     maskf = mask[...].astype(F32)
     along_table(along, u[...], v[...])
     msq2[...] = jnp.zeros_like(msq2)
@@ -317,9 +321,6 @@
     def _(g):
         copy(g).wait()
         total = jnp.zeros((8, 128), F32)
-        tiles = [pl.ds(pl.multiple_of(g * 16 + 8 * h, 8), 8) for h in range(2)]
-        halo_n = [rn[at, :] for at in tiles]
-        halo_s = [rs[at, :] for at in tiles]
         for i in range(FG):
             f = g * FG + i
             cr = scal(sm, 2, f)
@@ -333,9 +334,8 @@
                 ky = cr * float(abs(_sin[d0]))
                 k0 = 1.0 - kx - ky
                 for d in quartet:
-                    h, j = place(i, d % HALF)
                     gv = spec[f * ND + d] * jnp.maximum(a * along[d] + b, fac)
-                    xs, ys = shifted(gv, d, j, lane, halo_n[h], halo_s[h])
+                    xs, ys = shifted(gv, d)
                     e = k0 * gv + kx * xs + ky * ys
                     out[f * ND + d] = e
                     acc = acc + e
@@ -345,11 +345,11 @@
         msq2[...] += total
 
 
-def step_one_call(spectra, u, v, msq, mask, rn, rs):
+def step_one_call(spectra, u, v, msq, mask):
     column = jax.ShapeDtypeStruct((COL, 128), F32)
     return pl.pallas_call(
         step_one_kernel,
-        in_specs=[SMEM, HBM] + [VMEM] * 6,
+        in_specs=[SMEM, HBM] + [VMEM] * 4,
         out_specs=[VMEM] * 6,
         out_shape=[FIELD, TILE, column, column, column, column],
         scratch_shapes=[
@@ -359,13 +359,13 @@
         ],
         compiler_params=MIDDLE,
         name="step_one",
-    )(jnp.asarray(SCAL), spectra, u, v, msq, mask, rn, rs)
+    )(jnp.asarray(SCAL), spectra, u, v, msq, mask)
 
 
 def mend_one_kernel(
     sm, near_w, near_e, own_w, own_e, in_w, in_e, to_w, to_e, part, msq, u, v, mask, side, fn, fs,
-    lane_tab, dir_tab, four,
-    msq2, row_w, row_e, col_w, col_e, fn2, fs2, corner_n, corner_s,
+    rn, rs, lane_tab, dir_tab, four,
+    msq2, row_w, row_e, col_w, col_e, fn2, fs2, patch_n, patch_s, corner_n, corner_s,
 ):
     row18 = iota((HALF, 128), 0)
     lane18 = iota((HALF, 128), 1)
@@ -408,14 +408,31 @@
     for key, out in (("n", corner_n), ("s", corner_s)):
         for tile in range(TILES):
             out[tile : tile + 1, :] = jnp.sum(acc[(key, tile)], axis=0, keepdims=True)
+    lane = iota((8, 128), 1)
+    for own, halo, dst, odd, at in ((fn, rn, patch_n, 1, 0), (fs, rs, patch_s, 0, 127)):
+        steep = jnp.zeros((8, 128), F32)
+        for n in range(TILES):
+            lt = lane_tab[n]
+            rows = slice(n * 8, n * 8 + 8)
+            fix = lt[5:6] * jnp.abs(lt[3:4]) * (halo[rows, :] - own[rows, :])
+            dst[rows, :] = fix
+            steep = steep + lt[6:7] * fix
+        steep = jnp.sum(jnp.where((lane & 1) == odd, steep, 0.0), axis=1, keepdims=True)
+        msq2[...] += jnp.where(lane == at, steep, 0.0)
     msq2[...] = msq2[...] * maskf
 
+    end = lane18 == jnp.where(up, 0, 127)
     for s, (src, dst, x) in enumerate(((to_e, col_e, 7), (to_w, col_w, 0))):
         along = dir_tab[2 * s] * u[x : x + 1, :] + dir_tab[2 * s + 1] * v[x : x + 1, :]
         fac = maskf[x : x + 1] / (1.0 + four[...] * msq2[x : x + 1, :])
         for f in range(NF):
             at = slice(f * HALF, f * HALF + HALF)
-            dst[at, :] = src[at, :] * wind_factor(sm, f, along) * fac[f : f + 1]
+            i = f % FG
+            row = (2 * (f // FG) + i // 3) * 8 + x
+            fix = jnp.where(up, patch_n[row : row + 1, :], patch_s[row : row + 1, :])
+            fix = jnp.where(lane18 == bin_lane(s, i, row18, up), fix, 0.0)
+            e = src[at, :] + jnp.where(end, jnp.sum(fix, axis=1, keepdims=True), 0.0)
+            dst[at, :] = e * wind_factor(sm, f, along) * fac[f : f + 1]
         dst[ROWS:COL, :] = jnp.zeros((COL - ROWS, 128), F32)
 
     sub = iota((8, 128), 0)
@@ -438,25 +455,25 @@
             dst[n * 8 : n * 8 + 8, :] = e * t * (me / (1.0 + lt[4:5] * qe))
 
 
-def mend_one_call(near_w, near_e, own_w, own_e, in_w, in_e, to_w, to_e, part, msq, u, v, mask, side, fn, fs):
+def mend_one_call(near_w, near_e, own_w, own_e, in_w, in_e, to_w, to_e, part, msq, u, v, mask, side, fn, fs, rn, rs):
     edge = jax.ShapeDtypeStruct((TILES * 8, 128), F32)
     column = jax.ShapeDtypeStruct((COL, 128), F32)
     return pl.pallas_call(
         mend_one_kernel,
-        in_specs=[SMEM] + [VMEM] * 19,
-        out_specs=[VMEM] * 7,
-        out_shape=[TILE, column, column, column, column, edge, edge],
+        in_specs=[SMEM] + [VMEM] * 21,
+        out_specs=[VMEM] * 9,
+        out_shape=[TILE, column, column, column, column, edge, edge, edge, edge],
         scratch_shapes=[pltpu.VMEM((24, 128), F32), pltpu.VMEM((24, 128), F32)],
         compiler_params=PARAMS,
         name="mend_one",
     )(
         jnp.asarray(SCAL), near_w, near_e, own_w, own_e, in_w, in_e, to_w, to_e, part, msq, u, v,
-        mask, side, fn, fs, jnp.asarray(LANE_TAB), jnp.asarray(DIR_TAB), jnp.asarray(FOUR_COL),
+        mask, side, fn, fs, rn, rs, jnp.asarray(LANE_TAB), jnp.asarray(DIR_TAB), jnp.asarray(FOUR_COL),
     )
 
 
 def step_two_kernel(
-    sm, spec, row_w, row_e, u, v, msq, mask, rn, rs, out, push, out_w, out_e, along, field, sems
+    sm, spec, row_w, row_e, u, v, msq, mask, patch_n, patch_s, out, push, out_w, out_e, along, field, sems
 ):
     def copy(g):
         at = pl.ds(g * GB, GB)
@@ -472,9 +489,8 @@
     def _(g):
         pu = jnp.zeros((8, 128), F32)
         pv = jnp.zeros((8, 128), F32)
-        tiles = [pl.ds(pl.multiple_of(g * 16 + 8 * h, 8), 8) for h in range(2)]
-        halo_n = [rn[at, :] for at in tiles]
-        halo_s = [rs[at, :] for at in tiles]
+        tiles_n = group_tiles(patch_n, g)
+        tiles_s = group_tiles(patch_s, g)
         for i in range(FG):
             f = g * FG + i
             a, b, cr = scal(sm, 0, f), scal(sm, 1, f), scal(sm, 2, f)
@@ -490,7 +506,6 @@
                 kym = ky * maskf
                 q = []
                 for d in quartet:
-                    h, j = place(i, d % HALF)
                     t = jnp.maximum(a * along[d] + b, 1.0)
                     e = spec[f * ND + d]
                     if d in WESTWARD:
@@ -499,8 +514,9 @@
                     else:
                         row = row_w[pl.ds(f * HALF + EASTWARD.index(d), 1), :]
                         e = jnp.where(sub == 0, jnp.broadcast_to(row, (8, 128)), e)
+                    e = e + lane_patch(tiles_n, tiles_s, i, d, lane)
                     gv = e * t * fac
-                    xs, ys = shifted(gv, d, j, lane, halo_n[h], halo_s[h])
+                    xs, ys = shifted(gv, d)
                     e = k0 * gv + kxm * xs + kym * ys
                     field[f * ND + d] = e
                     put_row(out_e, out_w, f, d, e, 0, 7)
@@ -521,7 +537,7 @@
         copy(g).wait()
 
 
-def step_two_call(spec, row_w, row_e, u, v, msq, mask, rn, rs):
+def step_two_call(spec, row_w, row_e, u, v, msq, mask, patch_n, patch_s):
     column = jax.ShapeDtypeStruct((COL, 128), F32)
     return pl.pallas_call(
         step_two_kernel,
@@ -535,12 +551,13 @@
         ],
         compiler_params=PARAMS,
         name="step_two",
-    )(jnp.asarray(SCAL), spec, row_w, row_e, u, v, msq, mask, rn, rs)
+    )(jnp.asarray(SCAL), spec, row_w, row_e, u, v, msq, mask, patch_n, patch_s)
 
 
 def mend_two_kernel(
-    sm, halo_w, halo_e, sent_w, sent_e, out_w, out_e, push_in, u, v, mask, owner, weight, dir_tab,
-    end_w, end_e, cells, push,
+    sm, halo_w, halo_e, sent_w, sent_e, out_w, out_e, push_in, u, v, mask, owner, weight,
+    own_n, own_s, rn, rs, lane_tab, dir_tab,
+    end_w, end_e, cells, patch_n, patch_s, push,
 ):
     maskf = mask[...].astype(F32)
     push[...] = push_in[...]
@@ -560,6 +577,27 @@
         dst[ROWS:COL, :] = jnp.zeros((COL - ROWS, 128), F32)
         for c, part in ((0, cos), (1, sin)):
             push[c, x : x + 1, :] = push_in[c, x : x + 1, :] + jnp.sum(part * total, axis=0, keepdims=True)
+    lane = iota((8, 128), 1)
+    for own, halo, dst, odd, at, sign in (
+        (own_n, rn, patch_n, 1, 0, 1.0), (own_s, rs, patch_s, 0, 127, -1.0)
+    ):
+        pick = lambda z: jnp.broadcast_to(z[:, at : at + 1], (8, 128))
+        ue, ve, me = pick(u[...]), pick(v[...]), pick(maskf)
+        tu = jnp.zeros((8, 128), F32)
+        tv = jnp.zeros((8, 128), F32)
+        for n in range(TILES):
+            lt = lane_tab[n]
+            rows = slice(n * 8, n * 8 + 8)
+            cos, sin = sign * lt[2:3], sign * lt[3:4]
+            fix = lt[5:6] * jnp.abs(sin) * me * (halo[rows, :] - own[rows, :])
+            dst[rows, :] = fix
+            rate = jnp.maximum(lt[0:1] * (cos * ue + sin * ve) + lt[1:2], 1.0) - 1.0
+            q = lt[7:8] * rate * fix
+            tu = tu + cos * q
+            tv = tv + sin * q
+        for c, part in ((0, tu), (1, tv)):
+            part = jnp.sum(jnp.where((lane & 1) == odd, part, 0.0), axis=1, keepdims=True)
+            push[c] += jnp.where(lane == at, part, 0.0)
 
     uu, vv = u[...], v[...]
     share = weight[...].astype(F32) * maskf
@@ -592,25 +630,28 @@
 
 
 def mend_two_call(
-    halo_w, halo_e, sent_w, sent_e, out_w, out_e, push, u, v, mask, owner, weight, dests
+    halo_w, halo_e, sent_w, sent_e, out_w, out_e, push, u, v, mask, owner, weight,
+    own_n, own_s, rn, rs, dests,
 ):
+    edge = jax.ShapeDtypeStruct((TILES * 8, 128), F32)
     column = jax.ShapeDtypeStruct((COL, 128), F32)
     return pl.pallas_call(
         mend_two_kernel,
-        in_specs=[SMEM] + [VMEM] * 13,
-        out_specs=[VMEM] * 3,
-        out_shape=[column, column, jax.ShapeDtypeStruct((dests, 16, 128), F32)],
+        in_specs=[SMEM] + [VMEM] * 18,
+        out_specs=[VMEM] * 5,
+        out_shape=[column, column, jax.ShapeDtypeStruct((dests, 16, 128), F32), edge, edge],
         scratch_shapes=[pltpu.VMEM((2, 8, 128), F32)],
         compiler_params=PARAMS,
         name="mend_two",
     )(
         jnp.asarray(SCAL), halo_w, halo_e, sent_w, sent_e, out_w, out_e, push, u, v, mask, owner,
-        weight, jnp.asarray(DIR_TAB),
-    )
-
-
-def output_kernel(stage, end_w, end_e, out, field, whole, sems_in, sems):
+        weight, own_n, own_s, rn, rs, jnp.asarray(LANE_TAB), jnp.asarray(DIR_TAB),
+    )
+
+
+def output_kernel(stage, end_w, end_e, patch_n, patch_s, out, field, whole, sems_in, sems):
     sub = iota((8, 128), 0)
+    lane = iota((8, 128), 1)
 
     def copy_in(g):
         at = pl.ds(g * GB, GB)
@@ -626,6 +667,8 @@
     @pl.loop(0, GROUPS)
     def _(g):
         copy_in(g).wait()
+        tiles_n = group_tiles(patch_n, g)
+        tiles_s = group_tiles(patch_s, g)
         for i in range(FG):
             f = g * FG + i
             for d in range(ND):
@@ -635,17 +678,18 @@
                 else:
                     row = end_w[pl.ds(f * HALF + EASTWARD.index(d), 1), :]
                     x = 0
-                whole[f * ND + d] = jnp.where(sub == x, jnp.broadcast_to(row, (8, 128)), field[f * ND + d])
+                e = jnp.where(sub == x, jnp.broadcast_to(row, (8, 128)), field[f * ND + d])
+                whole[f * ND + d] = e + lane_patch(tiles_n, tiles_s, i, d, lane)
         copy(g).start()
 
     for g in range(GROUPS):
         copy(g).wait()
 
 
-def output_call(field, end_w, end_e):
+def output_call(field, end_w, end_e, patch_n, patch_s):
     return pl.pallas_call(
         output_kernel,
-        in_specs=[HBM, VMEM, VMEM],
+        in_specs=[HBM] + [VMEM] * 4,
         out_specs=HBM,
         out_shape=FIELD,
         scratch_shapes=[
@@ -656,7 +700,7 @@
         ],
         compiler_params=PARAMS,
         name="output",
-    )(field, end_w, end_e)
+    )(field, end_w, end_e, patch_n, patch_s)
 
 
 def cell_kernel(parts, stress, rough):
@@ -703,21 +747,25 @@
     rn = lax.ppermute(fn, "lat", northward)
     rs = lax.ppermute(fs, "lat", southward)
     energy, part, in_w, in_e, to_w, to_e = step_one_call(
-        spectra, u, v, msq1, sea_mask, rn, rs
-    )
-    msq2, row_w, row_e, col_w, col_e, fn2, fs2 = mend_one_call(
-        near_w, near_e, own_w, own_e, in_w, in_e, to_w, to_e, part, msq1, u, v, sea_mask, side, fn, fs
+        spectra, u, v, msq1, sea_mask
+    )
+    msq2, row_w, row_e, col_w, col_e, fn2, fs2, patch_n, patch_s = mend_one_call(
+        near_w, near_e, own_w, own_e, in_w, in_e, to_w, to_e, part, msq1, u, v, sea_mask, side,
+        fn, fs, rn, rs,
     )
     halo_w = lax.ppermute(col_e, "lon", eastward)
     halo_e = lax.ppermute(col_w, "lon", westward)
     rn = lax.ppermute(fn2, "lat", northward)
     rs = lax.ppermute(fs2, "lat", southward)
-    field, push, out_w, out_e = step_two_call(energy, row_w, row_e, u, v, msq2, sea_mask, rn, rs)
-    end_w, end_e, cells = mend_two_call(
-        halo_w, halo_e, col_w, col_e, out_w, out_e, push, u, v, sea_mask, owner, weight, lons
+    field, push, out_w, out_e = step_two_call(
+        energy, row_w, row_e, u, v, msq2, sea_mask, patch_n, patch_s
+    )
+    end_w, end_e, cells, patch_n, patch_s = mend_two_call(
+        halo_w, halo_e, col_w, col_e, out_w, out_e, push, u, v, sea_mask, owner, weight,
+        fn2, fs2, rn, rs, lons,
     )
     parts = lax.all_to_all(cells, "lon", 0, 0)
-    energy = output_call(field, end_w, end_e)
+    energy = output_call(field, end_w, end_e, patch_n, patch_s)
     stress, rough = cell_call(parts)
     return energy, stress, rough.reshape(512)
 

time: 75.9 us -> 70.6 us (0.930)
  waiting for transfers between devices: 8.53 us -> 0.98 us
  starting transfers between devices: 33.2 us -> 35 us
    ppermute x1, waiting for transfers between devices: 3.82 us -> 0.01 us  [body(): rs = lax.ppermute(fs, 'lat', southward)]
    ppermute x1, waiting for transfers between devices: 3.82 us -> 0.01 us  [body(): rs = lax.ppermute(fs2, 'lat', southward)]
    ppermute x1, starting transfers between devices: 2.4 us -> 4.19 us  [body(): rn = lax.ppermute(fn2, 'lat', northward)]
  transfers between devices with their start and end apart: 10 -> 10, of which waited for: 4 -> 2; matrix products, arithmetic and copies ran while one was open for 0% -> 0% of each run, Pallas kernels for 33% -> 35%
where the time goes in v4:
time: 70.6 us; the launch traced here: 70.1 us
  starting transfers between devices  35 us (50%)
  Pallas kernels  32.6 us (46%)
  waiting for transfers between devices  0.98 us (1%)
  between operations  0.9 us (1%)
    all_to_all x1, starting transfers between devices, body(): table = lax.all_to_all(mine, 'lon', 0, 0)  8.43 us
    pallas_call x1, Pallas kernels, step_two_call(): pl.pallas_call(step_two_kernel, in_specs=[SMEM] + [VMEM] * 9, out_specs=[...  7.61 us
    pallas_call x1, Pallas kernels, output_call(): pl.pallas_call(output_kernel, in_specs=[HBM] + [VMEM] * 4, out_specs=HBM,...  6.35 us
    ppermute x1, starting transfers between devices, body(): rn = lax.ppermute(fn, 'lat', northward)  5.31 us
    pallas_call x1, Pallas kernels, step_one_call(): pl.pallas_call(step_one_kernel, in_specs=[SMEM, HBM] + [VMEM] * 4, out_sp...  5.08 us
    ppermute x1, starting transfers between devices, body(): halo_e = lax.ppermute(col_w, 'lon', westward)  4.5 us
    pallas_call x1, Pallas kernels, first_call(): pl.pallas_call(first_kernel, in_specs=[HBM], out_specs=[VMEM] * 5, out_sh...  4.41 us
    ppermute x1, starting transfers between devices, body(): rn = lax.ppermute(fn2, 'lat', northward)  4.19 us
  transfers between devices with their start and end apart: 10, of which 2 were waited for; matrix products, arithmetic and copies ran while one was open for 0% of the time, Pallas kernels for 35%

profile of v4, /device:TPU:1, one launch (start us, length us, event | category | flops | bytes accessed | tf_op | source)
XLA Modules:
  0.0 70.1 jit_solution(5806562457822619318)
XLA Ops:
  0.6 0.0 copy-start
  0.6 0.0 copy-start.3
  0.7 1.6 %sector.1 = f32[16,56,128]{2,1,0:T(8,128)} custom-call(s32[8,128]{1,0:T(8,128)} %mask.11, f32[2,2048]{1,0:T(2,128)} %winds.2, s32[8,128]{1,0:T(8,128)} %wrow.3), custom_call_target="tpu_custom_call" | custom-call | tf_op jit(solution)/shard_map/sector/pallas_call | solution.py:180
  2.2 8.4 %all-to-all-start = ((f32[16,56,128]{2,1,0:T(8,128)}), f32[16,56,128]{2,1,0:T(8,128)S(1)}, u32[]{:S(2)}, u32[]{:S(2)}) async-start(f32[16,56,128]{2,1,0:T(8,128)} %sector.1), calls=%async_computation | async-start | bytes 917504 | tf_op jit(solution)/shard_map/all_to_all | solution.py:741
  10.7 0.0 copy-start.1
  10.7 0.0 copy-start.4
  10.7 4.4 %first.1 = (f32[904,128]{1,0:T(8,128)S(1)}, f32[904,128]{1,0:T(8,128)S(1)}, f32[20,8,128]{2,1,0:T(8,128)S(1)}, f32[20,8,128]{2,1,0:T(8,128)S(1)}, f32[8,128]{1,0:T(8,128)S(1)}) custom-call(f32[1800,8,128]{2,1,0:T(8,128)} %spec_hbm.1), custom_call_target="tpu_custom_call" | custom-call | tf_op jit(solution)/shard_map/first/pallas_call | solution.py:168
  15.1 1.4 %collective-permute-start = (f32[904,128]{1,0:T(8,128)S(1)}, f32[904,128]{1,0:T(8,128)S(1)}, u32[]{:S(2)}, u32[]{:S(2)}) collective-permute-start(f32[904,128]{1,0:T(8,128)S(1)} %get-tuple-element.49.own_e), channel_id=1, source_target_pairs={{0,1},{1,2},{2,3},{3,4},{4,5},{5,6},{6,7},{7,8},{8,9},{9,10},{10,1... | collective-permute-start | bytes 1388552 | tf_op jit(solution)/shard_map/ppermute | solution.py:742
  16.6 3.4 %collective-permute-start.1 = (f32[904,128]{1,0:T(8,128)S(1)}, f32[904,128]{1,0:T(8,128)S(1)}, u32[]{:S(2)}, u32[]{:S(2)}) collective-permute-start(f32[904,128]{1,0:T(8,128)S(1)} %get-tuple-element.50.own_w), channel_id=1, source_target_pairs={{0,15},{1,0},{2,1},{3,2},{4,3},{5,4},{6,5},{7,6},{8,7},{9,8},{10,9... | collective-permute-start | bytes 1388552 | tf_op jit(solution)/shard_map/ppermute | solution.py:743
  20.0 0.3 all-to-all-done.table
  20.2 0.9 %winds.3 = (f32[8,128]{1,0:T(8,128)S(1)}, f32[8,128]{1,0:T(8,128)S(1)}, f32[8,128]{1,0:T(8,128)S(1)}, f32[160,128]{1,0:T(8,128)S(1)}, f32[160,128]{1,0:T(8,128)S(1)}) custom-call(s32[1]{0:T(128)} %bitcast.me_ref, f32[16,56,128]{2,1,0:T(8,128)S(1)} %all-to-all-done.table, s32[8,128]{1,0:T(8,128)S(1)} %copy-done.5, f32[8,128]{1,0:T(8,128)S(1)} %get-tuple-element.43.msq, ...), custom_call_target="tpu_custom_call" | custom-call | tf_op jit(solution)/shard_map/winds/pallas_call | solution.py:259
  21.2 5.3 %collective-permute-start.2 = (f32[160,128]{1,0:T(8,128)S(1)}, f32[160,128]{1,0:T(8,128)S(1)}, u32[]{:S(2)}, u32[]{:S(2)}) collective-permute-start(f32[160,128]{1,0:T(8,128)S(1)} %get-tuple-element.57.fn), channel_id=1, source_target_pairs={{0,16},{16,32},{32,48},{48,64},{64,80},{80,96},{96,112},{1,17},{17... | collective-permute-start | bytes 245768 | tf_op jit(solution)/shard_map/ppermute | solution.py:747
  26.5 1.9 %collective-permute-start.3 = (f32[160,128]{1,0:T(8,128)S(1)}, f32[160,128]{1,0:T(8,128)S(1)}, u32[]{:S(2)}, u32[]{:S(2)}) collective-permute-start(f32[160,128]{1,0:T(8,128)S(1)} %get-tuple-element.58.fs), channel_id=1, source_target_pairs={{16,0},{32,16},{48,32},{64,48},{80,64},{96,80},{112,96},{17,1},{33... | collective-permute-start | bytes 245768 | tf_op jit(solution)/shard_map/ppermute | solution.py:748
  28.4 5.1 %step_one.1 = (f32[1800,8,128]{2,1,0:T(8,128)S(1)}, f32[8,128]{1,0:T(8,128)S(1)}, f32[904,128]{1,0:T(8,128)S(1)}, f32[904,128]{1,0:T(8,128)S(1)}, f32[904,128]{1,0:T(8,128)S(1)}, /*index=5*/f32[904,128]{1,0:T(8,128)S(1)}) custom-call(f32[384]{0:T(512)S(1)} %copy-done.3, f32[1800,8,128]{2,1,0:T(8,128)} %spec_hbm.1, f32[8,128]{1,0:T(8,128)S(1)} %get-tuple-element.46.u, ...), custom_call_target="tpu_custom_call" | custom-call | tf_op jit(solution)/shard_map/step_one/pallas_call | solution.py:350
  33.5 0.0 copy-start.6
  33.5 0.0 copy-start.7
  33.5 0.0 collective-permute-done.near_w
  33.5 0.0 collective-permute-done.1.near_e
  33.6 2.6 %mend_one.1 = (f32[8,128]{1,0:T(8,128)S(1)}, f32[904,128]{1,0:T(8,128)S(1)}, f32[904,128]{1,0:T(8,128)S(1)}, f32[904,128]{1,0:T(8,128)S(1)}, f32[904,128]{1,0:T(...) custom-call(f32[384]{0:T(512)S(1)} %copy-done.3, ...), custom_call_target="tpu_custom_call" | custom-call | tf_op jit(solution)/shard_map/mend_one/pallas_call | solution.py:461
  36.2 0.4 collective-permute-start.4
  36.5 4.5 %collective-permute-start.5 = (f32[904,128]{1,0:T(8,128)S(1)}, f32[904,128]{1,0:T(8,128)S(1)}, u32[]{:S(2)}, u32[]{:S(2)}) collective-permute-start(f32[904,128]{1,0:T(8,128)S(1)} %get-tuple-element.66.sent_w), channel_id=1, source_target_pairs={{0,15},{1,0},{2,1},{3,2},{4,3},{5,4},{6,5},{7,6},{8,7},{9,8},{10,9... | collective-permute-start | bytes 1388552 | tf_op jit(solution)/shard_map/ppermute | solution.py:757
  41.0 4.2 %collective-permute-start.6 = (f32[160,128]{1,0:T(8,128)S(1)}, f32[160,128]{1,0:T(8,128)S(1)}, u32[]{:S(2)}, u32[]{:S(2)}) collective-permute-start(f32[160,128]{1,0:T(8,128)S(1)} %get-tuple-element.70.own_n), channel_id=1, source_target_pairs={{0,16},{16,32},{32,48},{48,64},{64,80},{80,96},{96,112},{1,17},{17... | collective-permute-start | bytes 245768 | tf_op jit(solution)/shard_map/ppermute | solution.py:758
  45.2 1.9 %collective-permute-start.7 = (f32[160,128]{1,0:T(8,128)S(1)}, f32[160,128]{1,0:T(8,128)S(1)}, u32[]{:S(2)}, u32[]{:S(2)}) collective-permute-start(f32[160,128]{1,0:T(8,128)S(1)} %get-tuple-element.71.own_s), channel_id=1, source_target_pairs={{16,0},{32,16},{48,32},{64,48},{80,64},{96,80},{112,96},{17,1},{33... | collective-permute-start | bytes 245768 | tf_op jit(solution)/shard_map/ppermute | solution.py:759
  47.1 7.6 %step_two.1 = (f32[7200,8,128]{2,1,0:T(8,128)}, f32[2,8,128]{2,1,0:T(8,128)S(1)}, f32[904,128]{1,0:T(8,128)S(1)}, f32[904,128]{1,0:T(8,128)S(1)}) custom-call(f32[384]{0:T(512)S(1)} %copy-done.3, f32[1800,8,128]{2,1,0:T(8,128)S(1)} %get-tuple-element.48.spec, f32[904,128]{1,0:T(8,128)S(1)} %get-tuple-element.59.row_w, ...), custom_call_target="tpu_custom_call" | custom-call | tf_op jit(solution)/shard_map/step_two/pallas_call | solution.py:542
  54.8 0.0 collective-permute-done.7.rs
  54.8 0.0 collective-permute-done.4.halo_w
  54.8 2.6 %mend_two.1 = (f32[904,128]{1,0:T(8,128)S(1)}, f32[904,128]{1,0:T(8,128)S(1)}, f32[16,16,128]{2,1,0:T(8,128)}, f32[160,128]{1,0:T(8,128)S(1)}, f32[160,128]{1,0:T(8,128)S(1)}) custom-call(f32[384]{0:T(512)S(1)} %copy-done.3, f32[904,128]{1,0:T(8,128)S(1)} %collective-permute-done.4.halo_w, f32[904,128]{1,0:T(8,128)S(1)} %collective-permute-done.5.halo_e, ...), custom_call_target="tpu_custom_call" | custom-call | tf_op jit(solution)/shard_map/mend_two/pallas_call | solution.py:638
  57.4 3.5 %all-to-all-start.1 = ((f32[16,16,128]{2,1,0:T(8,128)}), f32[16,16,128]{2,1,0:T(8,128)S(1)}, u32[]{:S(2)}, u32[]{:S(2)}) async-start(f32[16,16,128]{2,1,0:T(8,128)} %get-tuple-element.76), calls=%async_computation.1 | async-start | bytes 262144 | tf_op jit(solution)/shard_map/all_to_all | solution.py:767
  60.9 6.3 %output.1 = f32[1800,8,128]{2,1,0:T(8,128)} custom-call(f32[7200,8,128]{2,1,0:T(8,128)} %get-tuple-element.64.stage, f32[904,128]{1,0:T(8,128)S(1)} %get-tuple-element.72.end_w, f32[904,128]{1,0:T(8,128)S(1)} %get-tuple-element.73.end_e, f32[160,128]{1,0:T(8,128)S(1)} %get-tuple-element.74.patch_n, f32[160,128]{1,0:T(8,128)S(1)} %get-tuple-element.75.patch_s), custom_call_target="tpu_custom_call" | custom-call | tf_op jit(solution)/shard_map/output/pallas_call | solution.py:690
  67.3 0.7 %all-to-all-done.1.parts = f32[16,16,128]{2,1,0:T(8,128)S(1)} async-done(((f32[16,16,128]{2,1,0:T(8,128)}), f32[16,16,128]{2,1,0:T(8,128)S(1)}, u32[]{:S(2)}, u32[]{:S(2)}) %all-to-all-start.1) | async-done | bytes 131104 | tf_op jit(solution)/shard_map/all_to_all | solution.py:767
  68.0 0.6 copy-done.8
  68.6 1.5 %cells.1 = (f32[2,512]{1,0:T(2,128)}, f32[1,512]{1,0:T(1,128)}) custom-call(f32[16,16,128]{2,1,0:T(8,128)} %copy-done.8), custom_call_target="tpu_custom_call" | custom-call | tf_op jit(solution)/shard_map/cells/pallas_call | solution.py:722
  (15 shorter events, 0.0 us)
Async XLA Ops:
  0.6 19.6 %copy-start = (f32[20,8,128]{2,1,0:T(8,128)S(1)}, f32[20,8,128]{2,1,0:T(8,128)}, u32[]{:S(2)}) copy-start(f32[20,8,128]{2,1,0:T(8,128)} %constant.12.clone.lane_tab) | copy-start | bytes 245764
  0.6 27.8 %copy-start.3 = (f32[384]{0:T(512)S(1)}, f32[384]{0:T(512)}, u32[]{:S(2)}) copy-start(f32[384]{0:T(512)} %constant.13.clone.sm) | copy-start | bytes 4612
  0.7 19.6 %copy-start.2 = (s32[8,128]{1,0:T(8,128)S(1)}, s32[8,128]{1,0:T(8,128)}, u32[]{:S(2)}) copy-start(s32[8,128]{1,0:T(8,128)} %mask.11) | copy-start | bytes 12292
  0.7 19.6 %copy-start.5 = (s32[8,128]{1,0:T(8,128)S(1)}, s32[8,128]{1,0:T(8,128)}, u32[]{:S(2)}) copy-start(s32[8,128]{1,0:T(8,128)} %wrow.3) | copy-start | bytes 12292
  2.2 18.0 %all-to-all-start = ((f32[16,56,128]{2,1,0:T(8,128)}), f32[16,56,128]{2,1,0:T(8,128)S(1)}, u32[]{:S(2)}, u32[]{:S(2)}) async-start(f32[16,56,128]{2,1,0:T(8,128)} %sector.1), calls=%async_computation | async-start | bytes 917504 | tf_op jit(solution)/shard_map/all_to_all | solution.py:741
  10.7 22.9 %copy-start.1 = (f32[4,18,128]{2,1,0:T(8,128)S(1)}, f32[4,18,128]{2,1,0:T(8,128)}, u32[]{:S(2)}) copy-start(f32[4,18,128]{2,1,0:T(8,128)} %constant.14.clone.dir_tab) | copy-start | bytes 110596
  10.7 22.9 %copy-start.4 = (f32[50,128]{1,0:T(8,128)S(1)}, f32[50,128]{1,0:T(8,128)}, u32[]{:S(2)}) copy-start(f32[50,128]{1,0:T(8,128)} %constant.15.clone.four) | copy-start | bytes 76804
  15.1 18.4 %collective-permute-start = (f32[904,128]{1,0:T(8,128)S(1)}, f32[904,128]{1,0:T(8,128)S(1)}, u32[]{:S(2)}, u32[]{:S(2)}) collective-permute-start(f32[904,128]{1,0:T(8,128)S(1)} %get-tuple-element.49.own_e), channel_id=1, source_target_pairs={{0,1},{1,2},{2,3},{3,4},{4,5},{5,6},{6,7},{7,8},{8,9},{9,10},{10,1... | collective-permute-start | bytes 1388552 | tf_op jit(solution)/shard_map/ppermute | solution.py:742
  16.6 17.0 %collective-permute-start.1 = (f32[904,128]{1,0:T(8,128)S(1)}, f32[904,128]{1,0:T(8,128)S(1)}, u32[]{:S(2)}, u32[]{:S(2)}) collective-permute-start(f32[904,128]{1,0:T(8,128)S(1)} %get-tuple-element.50.own_w), channel_id=1, source_target_pairs={{0,15},{1,0},{2,1},{3,2},{4,3},{5,4},{6,5},{7,6},{8,7},{9,8},{10,9... | collective-permute-start | bytes 1388552 | tf_op jit(solution)/shard_map/ppermute | solution.py:743
  21.2 12.4 %collective-permute-start.2 = (f32[160,128]{1,0:T(8,128)S(1)}, f32[160,128]{1,0:T(8,128)S(1)}, u32[]{:S(2)}, u32[]{:S(2)}) collective-permute-start(f32[160,128]{1,0:T(8,128)S(1)} %get-tuple-element.57.fn), channel_id=1, source_target_pairs={{0,16},{16,32},{32,48},{48,64},{64,80},{80,96},{96,112},{1,17},{17... | collective-permute-start | bytes 245768 | tf_op jit(solution)/shard_map/ppermute | solution.py:747
  26.5 7.1 %collective-permute-start.3 = (f32[160,128]{1,0:T(8,128)S(1)}, f32[160,128]{1,0:T(8,128)S(1)}, u32[]{:S(2)}, u32[]{:S(2)}) collective-permute-start(f32[160,128]{1,0:T(8,128)S(1)} %get-tuple-element.58.fs), channel_id=1, source_target_pairs={{16,0},{32,16},{48,32},{64,48},{80,64},{96,80},{112,96},{17,1},{33... | collective-permute-start | bytes 245768 | tf_op jit(solution)/shard_map/ppermute | solution.py:748
  33.5 21.3 %copy-start.6 = (s32[8,128]{1,0:T(8,128)S(1)}, s32[8,128]{1,0:T(8,128)}, u32[]{:S(2)}) copy-start(s32[8,128]{1,0:T(8,128)} %owner.1) | copy-start | bytes 12292
  33.5 21.3 %copy-start.7 = (s32[8,128]{1,0:T(8,128)S(1)}, s32[8,128]{1,0:T(8,128)}, u32[]{:S(2)}) copy-start(s32[8,128]{1,0:T(8,128)} %weight.1) | copy-start | bytes 12292
  36.2 18.6 %collective-permute-start.4 = (f32[904,128]{1,0:T(8,128)S(1)}, f32[904,128]{1,0:T(8,128)S(1)}, u32[]{:S(2)}, u32[]{:S(2)}) collective-permute-start(f32[904,128]{1,0:T(8,128)S(1)} %get-tuple-element.65.sent_e), channel_id=1, source_target_pairs={{0,1},{1,2},{2,3},{3,4},{4,5},{5,6},{6,7},{7,8},{8,9},{9,10},{10,1... | collective-permute-start | bytes 1388552 | tf_op jit(solution)/shard_map/ppermute | solution.py:756
  36.5 18.3 %collective-permute-start.5 = (f32[904,128]{1,0:T(8,128)S(1)}, f32[904,128]{1,0:T(8,128)S(1)}, u32[]{:S(2)}, u32[]{:S(2)}) collective-permute-start(f32[904,128]{1,0:T(8,128)S(1)} %get-tuple-element.66.sent_w), channel_id=1, source_target_pairs={{0,15},{1,0},{2,1},{3,2},{4,3},{5,4},{6,5},{7,6},{8,7},{9,8},{10,9... | collective-permute-start | bytes 1388552 | tf_op jit(solution)/shard_map/ppermute | solution.py:757
  41.0 13.7 %collective-permute-start.6 = (f32[160,128]{1,0:T(8,128)S(1)}, f32[160,128]{1,0:T(8,128)S(1)}, u32[]{:S(2)}, u32[]{:S(2)}) collective-permute-start(f32[160,128]{1,0:T(8,128)S(1)} %get-tuple-element.70.own_n), channel_id=1, source_target_pairs={{0,16},{16,32},{32,48},{48,64},{64,80},{80,96},{96,112},{1,17},{17... | collective-permute-start | bytes 245768 | tf_op jit(solution)/shard_map/ppermute | solution.py:758
  45.2 9.6 %collective-permute-start.7 = (f32[160,128]{1,0:T(8,128)S(1)}, f32[160,128]{1,0:T(8,128)S(1)}, u32[]{:S(2)}, u32[]{:S(2)}) collective-permute-start(f32[160,128]{1,0:T(8,128)S(1)} %get-tuple-element.71.own_s), channel_id=1, source_target_pairs={{16,0},{32,16},{48,32},{64,48},{80,64},{96,80},{112,96},{17,1},{33... | collective-permute-start | bytes 245768 | tf_op jit(solution)/shard_map/ppermute | solution.py:759
  57.4 10.6 %all-to-all-start.1 = ((f32[16,16,128]{2,1,0:T(8,128)}), f32[16,16,128]{2,1,0:T(8,128)S(1)}, u32[]{:S(2)}, u32[]{:S(2)}) async-start(f32[16,16,128]{2,1,0:T(8,128)} %get-tuple-element.76), calls=%async_computation.1 | async-start | bytes 262144 | tf_op jit(solution)/shard_map/all_to_all | solution.py:767
  68.0 0.6 copy-start.8

commit v5 on v4

--- a/solution.py
+++ b/solution.py
@@ -100,7 +100,7 @@
     return packed
 
 
-def first_kernel(spec_hbm, near_w, near_e, north, south, msq, spec, sems):
+def first_kernel(uneven, spec_hbm, near_w, near_e, send_a, send_b, north, south, msq, spec, sems):
     lane = iota((8, 128), 1)
 
     def copy(g):
@@ -135,6 +135,9 @@
     for near, x in ((near_w, 0), (near_e, 7)):
         near[ROWS : ROWS + 1, :] = q[x : x + 1]
         near[ROWS + 1 : COL, :] = jnp.zeros((COL - ROWS - 1, 128), F32)
+    east, west = near_e[...], near_w[...]
+    send_a[...] = jnp.where(uneven[0] == 1, west, east)
+    send_b[...] = jnp.where(uneven[0] == 1, east, west)
 
 
 def sector_kernel(mask, winds, wrow, mine):
@@ -162,18 +165,18 @@
 ALONE = pltpu.CompilerParams(vmem_limit_bytes=54 * 2**20)
 
 
-def first_call(spectra):
+def first_call(uneven, spectra):
     edge = jax.ShapeDtypeStruct((COL, 128), F32)
     pack = jax.ShapeDtypeStruct((TILES, 8, 128), F32)
     return pl.pallas_call(
         first_kernel,
-        in_specs=[HBM],
-        out_specs=[VMEM] * 5,
-        out_shape=[edge, edge, pack, pack, TILE],
+        in_specs=[SMEM, HBM],
+        out_specs=[VMEM] * 7,
+        out_shape=[edge, edge, edge, edge, pack, pack, TILE],
         scratch_shapes=[BUFFER, pltpu.SemaphoreType.DMA((GROUPS,))],
         compiler_params=WIDE,
         name="first",
-    )(spectra)
+    )(uneven, spectra)
 
 
 def sector_call(mask, winds, wrow, lons):
@@ -365,7 +368,7 @@
 def mend_one_kernel(
     sm, near_w, near_e, own_w, own_e, in_w, in_e, to_w, to_e, part, msq, u, v, mask, side, fn, fs,
     rn, rs, lane_tab, dir_tab, four,
-    msq2, row_w, row_e, col_w, col_e, fn2, fs2, patch_n, patch_s, corner_n, corner_s,
+    msq2, row_w, row_e, col_w, col_e, fn2, fs2, patch_n, patch_s, corner,
 ):
     row18 = iota((HALF, 128), 0)
     lane18 = iota((HALF, 128), 1)
@@ -400,14 +403,12 @@
                 jnp.broadcast_to(g1[:, 0:1], (HALF, 128)),
             )
             ends = jnp.where(lane18 == bin_lane(s, i, row18, up), ends, 0.0)
-            for key, val in (("n", jnp.where(up, ends, 0.0)), ("s", jnp.where(up, 0.0, ends))):
-                have = acc.get((key, tile))
-                acc[(key, tile)] = val if have is None else have + val
+            acc[tile] = acc[tile] + ends if tile in acc else ends
         dst[ROWS:COL, :] = jnp.zeros((COL - ROWS, 128), F32)
         msq2[x : x + 1, :] = part[x : x + 1, :] + jnp.sum(steep, axis=0, keepdims=True)
-    for key, out in (("n", corner_n), ("s", corner_s)):
-        for tile in range(TILES):
-            out[tile : tile + 1, :] = jnp.sum(acc[(key, tile)], axis=0, keepdims=True)
+    for tile in range(TILES):
+        corner[tile : tile + 1, :] = jnp.sum(acc[tile], axis=0, keepdims=True)
+
     lane = iota((8, 128), 1)
     for own, halo, dst, odd, at in ((fn, rn, patch_n, 1, 0), (fs, rs, patch_s, 0, 127)):
         steep = jnp.zeros((8, 128), F32)
@@ -436,7 +437,7 @@
         dst[ROWS:COL, :] = jnp.zeros((COL - ROWS, 128), F32)
 
     sub = iota((8, 128), 0)
-    for own, corner, dst, at, sign in ((fn, corner_n, fn2, 127, 1.0), (fs, corner_s, fs2, 0, -1.0)):
+    for own, dst, at, sign in ((fn, fn2, 127, 1.0), (fs, fs2, 0, -1.0)):
         pick = lambda z: jnp.broadcast_to(z[:, at : at + 1], (8, 128))
         ue, ve, me, qe = pick(u[...]), pick(v[...]), pick(maskf), pick(msq2[...])
         for n in range(TILES):
@@ -463,7 +464,7 @@
         in_specs=[SMEM] + [VMEM] * 21,
         out_specs=[VMEM] * 9,
         out_shape=[TILE, column, column, column, column, edge, edge, edge, edge],
-        scratch_shapes=[pltpu.VMEM((24, 128), F32), pltpu.VMEM((24, 128), F32)],
+        scratch_shapes=[pltpu.VMEM((24, 128), F32)],
         compiler_params=PARAMS,
         name="mend_one",
     )(
@@ -722,6 +723,7 @@
     return pl.pallas_call(
         cell_kernel,
         out_shape=[jax.ShapeDtypeStruct((2, 512), F32), jax.ShapeDtypeStruct((1, 512), F32)],
+        compiler_params=ALONE,
         name="cells",
     )(parts)
 
@@ -729,23 +731,37 @@
 def body(spectra, sea_mask, atm_wind, wind_row, owner, weight):
     lons = lax.axis_size("lon")
     lats = lax.axis_size("lat")
-    eastward = [(i, (i + 1) % lons) for i in range(lons)]
-    westward = [(i, (i - 1) % lons) for i in range(lons)]
-    northward = [(i, i + 1) for i in range(lats - 1)]
-    southward = [(i + 1, i) for i in range(lats - 1)]
-
     me = lax.axis_index("lon").astype(jnp.int32)
+    odd = (lax.axis_index("lat") & 1) == 1
+    uneven = (lax.axis_index("lon") & 1) == 1
+    pairs = [(i, i ^ 1) for i in range(lons)]
+    others = [(i, (i + 1 if i & 1 else i - 1) % lons) for i in range(lons)]
+
+    def arrive(send_a, send_b):
+        first = lax.ppermute(send_a, "lon", pairs)
+        second = lax.ppermute(send_b, "lon", others)
+        return jnp.where(uneven, first, second), jnp.where(uneven, second, first)
+
+    def trade(east, west):
+        return arrive(jnp.where(uneven, west, east), jnp.where(uneven, east, west))
+
+    inside = [(i, i ^ 1) for i in range(lats)]
+    across = [(i, i + 1 if i & 1 else i - 1) for i in range(1, lats - 1)]
+
+    def swap(north, south):
+        first = lax.ppermute(jnp.where(odd, south, north), "lat", inside)
+        second = lax.ppermute(jnp.where(odd, north, south), "lat", across)
+        return jnp.where(odd, first, second), jnp.where(odd, second, first)
+
     mine = sector_call(sea_mask, atm_wind, wind_row, lons)
     spectra, mine = lax.optimization_barrier((spectra, mine))
-    own_w, own_e, north, south, msq1 = first_call(spectra)
+    own_w, own_e, send_a, send_b, north, south, msq1 = first_call((me & 1).reshape(1), spectra)
     table = lax.all_to_all(mine, "lon", 0, 0)
-    near_w = lax.ppermute(own_e, "lon", eastward)
-    near_e = lax.ppermute(own_w, "lon", westward)
+    near_w, near_e = arrive(send_a, send_b)
     u, v, side, fn, fs = wind_call(
         me.reshape(1), table, wind_row, msq1, sea_mask, north, south
     )
-    rn = lax.ppermute(fn, "lat", northward)
-    rs = lax.ppermute(fs, "lat", southward)
+    rn, rs = swap(fn, fs)
     energy, part, in_w, in_e, to_w, to_e = step_one_call(
         spectra, u, v, msq1, sea_mask
     )
@@ -753,10 +769,8 @@
         near_w, near_e, own_w, own_e, in_w, in_e, to_w, to_e, part, msq1, u, v, sea_mask, side,
         fn, fs, rn, rs,
     )
-    halo_w = lax.ppermute(col_e, "lon", eastward)
-    halo_e = lax.ppermute(col_w, "lon", westward)
-    rn = lax.ppermute(fn2, "lat", northward)
-    rs = lax.ppermute(fs2, "lat", southward)
+    halo_w, halo_e = trade(col_e, col_w)
+    rn, rs = swap(fn2, fs2)
     field, push, out_w, out_e = step_two_call(
         energy, row_w, row_e, u, v, msq2, sea_mask, patch_n, patch_s
     )

time: 70.6 us -> 68.3 us (0.967)
  starting transfers between devices: 35 us -> 31.2 us
  other arithmetic: 0 us -> 1.28 us
    ppermute x8, starting transfers between devices: 23.1 us -> 18.3 us  [the longest x2 10.9 us: swap(): second = lax.ppermute(jnp.where(odd, north, south), 'lat', across)]
    select_n x0 -> x7, other arithmetic: none -> 1.28 us  [the longest x2 1.15 us: arrive(): return (jnp.where(uneven, first, second), jnp.where(uneven, second, first))]
    all_to_all x1, starting transfers between devices: 3.51 us -> 4.41 us  [body(): parts = lax.all_to_all(cells, 'lon', 0, 0)]
  transfers between devices with their start and end apart: 10 -> 10, of which waited for: 2 -> 2; matrix products, arithmetic and copies ran while one was open for 0% -> 2% of each run, Pallas kernels for 35% -> 36%
where the time goes in v5:
time: 68.3 us; the launch traced here: 67.5 us
  Pallas kernels  32.7 us (48%)
  starting transfers between devices  31.2 us (46%)
  other arithmetic  1.28 us (2%)
  between operations  0.95 us (1%)
  local copies, waits for them, and re-layouts  0.69 us (1%)
  waiting for transfers between devices  0.69 us (1%)
    ppermute x2, starting transfers between devices, swap(): second = lax.ppermute(jnp.where(odd, north, south), 'lat', across)  10.9 us
    all_to_all x1, starting transfers between devices, body(): table = lax.all_to_all(mine, 'lon', 0, 0)  8.43 us
    pallas_call x1, Pallas kernels, step_two_call(): pl.pallas_call(step_two_kernel, in_specs=[SMEM] + [VMEM] * 9, out_specs=[...  7.61 us
    ppermute x2, starting transfers between devices, arrive(): second = lax.ppermute(send_b, 'lon', others)  7.23 us
    pallas_call x1, Pallas kernels, output_call(): pl.pallas_call(output_kernel, in_specs=[HBM] + [VMEM] * 4, out_specs=HBM,...  6.35 us
    pallas_call x1, Pallas kernels, step_one_call(): pl.pallas_call(step_one_kernel, in_specs=[SMEM, HBM] + [VMEM] * 4, out_sp...  5.08 us
    pallas_call x1, Pallas kernels, first_call(): pl.pallas_call(first_kernel, in_specs=[SMEM, HBM], out_specs=[VMEM] * 7,...  4.52 us
    all_to_all x1, starting transfers between devices, body(): parts = lax.all_to_all(cells, 'lon', 0, 0)  4.41 us
  transfers between devices with their start and end apart: 10, of which 2 were waited for; matrix products, arithmetic and copies ran while one was open for 2% of the time, Pallas kernels for 36%

profile of v5, /device:TPU:1, one launch (start us, length us, event | category | flops | bytes accessed | tf_op | source)
XLA Modules:
  0.0 67.5 jit_solution(14255152292182428401)
XLA Ops:
  0.6 0.0 copy-start
  0.6 0.0 copy-start.3
  0.7 1.6 %sector.1 = f32[16,56,128]{2,1,0:T(8,128)} custom-call(s32[8,128]{1,0:T(8,128)} %mask.11, f32[2,2048]{1,0:T(2,128)} %winds.2, s32[8,128]{1,0:T(8,128)} %wrow.3), custom_call_target="tpu_custom_call" | custom-call | tf_op jit(solution)/shard_map/sector/pallas_call | solution.py:183
  2.2 8.4 %all-to-all-start = ((f32[16,56,128]{2,1,0:T(8,128)}), f32[16,56,128]{2,1,0:T(8,128)S(1)}, u32[]{:S(2)}, u32[]{:S(2)}) async-start(f32[16,56,128]{2,1,0:T(8,128)} %sector.1), calls=%async_computation | async-start | bytes 917504 | tf_op jit(solution)/shard_map/all_to_all | solution.py:759
  10.7 0.0 copy-start.1
  10.7 0.0 copy-start.4
  10.7 4.5 %first.1 = (f32[904,128]{1,0:T(8,128)S(1)}, f32[904,128]{1,0:T(8,128)S(1)}, f32[904,128]{1,0:T(8,128)S(1)}, f32[904,128]{1,0:T(8,128)S(1)}, f32[20,8,128]{2,1,0:...) custom-call(s32[1]{0:T(128)} %bitcast.1.uneven, f32[1800,8,128]{2,1,0:T(8,128)} %spec_hbm.1), custom_call_target="tpu_custom_call" | custom-call | tf_op jit(solution)/shard_map/first/pallas_call | solution.py:171
  15.2 4.8 %collective-permute-start.1 = (f32[904,128]{1,0:T(8,128)S(1)}, f32[904,128]{1,0:T(8,128)S(1)}, u32[]{:S(2)}, u32[]{:S(2)}) collective-permute-start(f32[904,128]{1,0:T(8,128)S(1)} %get-tuple-element.52), channel_id=1, source_target_pairs={{0,15},{1,2},{2,1},{3,4},{4,3},{5,6},{6,5},{7,8},{8,7},{9,10},{10,... | collective-permute-start | bytes 1388552 | tf_op jit(solution)/shard_map/ppermute | solution.py:742
  20.0 0.2 all-to-all-done.table
  20.2 0.9 %winds.3 = (f32[8,128]{1,0:T(8,128)S(1)}, f32[8,128]{1,0:T(8,128)S(1)}, f32[8,128]{1,0:T(8,128)S(1)}, f32[160,128]{1,0:T(8,128)S(1)}, f32[160,128]{1,0:T(8,128)S(1)}) custom-call(s32[1]{0:T(128)} %bitcast.me_ref, f32[16,56,128]{2,1,0:T(8,128)S(1)} %all-to-all-done.table, s32[8,128]{1,0:T(8,128)S(1)} %copy-done.5, f32[8,128]{1,0:T(8,128)S(1)} %get-tuple-element.45.msq, ...), custom_call_target="tpu_custom_call" | custom-call | tf_op jit(solution)/shard_map/winds/pallas_call | solution.py:262
  21.2 5.4 %collective-permute-start.3 = (f32[160,128]{1,0:T(8,128)S(1)}, f32[160,128]{1,0:T(8,128)S(1)}, u32[]{:S(2)}, u32[]{:S(2)}) collective-permute-start(f32[160,128]{1,0:T(8,128)S(1)} %get-tuple-element.95), channel_id=1, source_target_pairs={{16,32},{32,16},{48,64},{64,48},{80,96},{96,80},{17,33},{33,17},{4... | collective-permute-start | bytes 245768 | tf_op jit(solution)/shard_map/ppermute | solution.py:753
  26.6 0.1 collective-permute-start.2
  26.7 5.1 %step_one.1 = (f32[1800,8,128]{2,1,0:T(8,128)S(1)}, f32[8,128]{1,0:T(8,128)S(1)}, f32[904,128]{1,0:T(8,128)S(1)}, f32[904,128]{1,0:T(8,128)S(1)}, f32[904,128]{1,0:T(8,128)S(1)}, /*index=5*/f32[904,128]{1,0:T(8,128)S(1)}) custom-call(f32[384]{0:T(512)S(1)} %copy-done.3, f32[1800,8,128]{2,1,0:T(8,128)} %spec_hbm.1, f32[8,128]{1,0:T(8,128)S(1)} %get-tuple-element.48.u, ...), custom_call_target="tpu_custom_call" | custom-call | tf_op jit(solution)/shard_map/step_one/pallas_call | solution.py:353
  31.8 0.0 collective-permute-done
  31.8 1.1 %broadcast_select_fusion.4 = (f32[904,128]{1,0:T(8,128)S(1)}, f32[904,128]{1,0:T(8,128)S(1)}) fusion(f32[904,128]{1,0:T(8,128)S(1)} %collective-permute-done.1, f32[904,128]{1,0:T(8,128)} %collective-permute-done, pred[]{:T(512)S(6)} %eq.6), kind=kLoop, calls=%fused_computation.4 | loop fusion | flops 231424 | bytes 1851393 | tf_op jit(solution)/shard_map/jit(_where)/select_n | solution.py:743
  32.9 0.0 collective-permute-done.3
  32.9 0.0 collective-permute-done.2
  32.9 2.5 %mend_one.1 = (f32[8,128]{1,0:T(8,128)S(1)}, f32[904,128]{1,0:T(8,128)S(1)}, f32[904,128]{1,0:T(8,128)S(1)}, f32[904,128]{1,0:T(8,128)S(1)}, f32[904,128]{1,0:T(...) custom-call(f32[384]{0:T(512)S(1)} %copy-done.3, ...), custom_call_target="tpu_custom_call" | custom-call | tf_op jit(solution)/shard_map/mend_one/pallas_call | solution.py:462
  35.5 0.0 copy-start.6
  35.5 0.0 copy-start.7
  35.5 0.1 broadcast_select_fusion.2
  35.6 2.5 %collective-permute-start.5 = (f32[904,128]{1,0:T(8,128)S(1)}, f32[904,128]{1,0:T(8,128)S(1)}, u32[]{:S(2)}, u32[]{:S(2)}) collective-permute-start(f32[904,128]{1,0:T(8,128)S(1)} %get-tuple-element.85), channel_id=1, source_target_pairs={{0,15},{1,2},{2,1},{3,4},{4,3},{5,6},{6,5},{7,8},{8,7},{9,10},{10,... | collective-permute-start | bytes 1388552 | tf_op jit(solution)/shard_map/ppermute | solution.py:742
  38.1 5.5 %collective-permute-start.7 = (f32[160,128]{1,0:T(8,128)S(1)}, f32[160,128]{1,0:T(8,128)S(1)}, u32[]{:S(2)}, u32[]{:S(2)}) collective-permute-start(f32[160,128]{1,0:T(8,128)S(1)} %get-tuple-element.91), channel_id=1, source_target_pairs={{16,32},{32,16},{48,64},{64,48},{80,96},{96,80},{17,33},{33,17},{4... | collective-permute-start | bytes 245768 | tf_op jit(solution)/shard_map/ppermute | solution.py:753
  43.6 0.1 collective-permute-start.6
  43.7 7.6 %step_two.1 = (f32[7200,8,128]{2,1,0:T(8,128)}, f32[2,8,128]{2,1,0:T(8,128)S(1)}, f32[904,128]{1,0:T(8,128)S(1)}, f32[904,128]{1,0:T(8,128)S(1)}) custom-call(f32[384]{0:T(512)S(1)} %copy-done.3, f32[1800,8,128]{2,1,0:T(8,128)S(1)} %get-tuple-element.50.spec, f32[904,128]{1,0:T(8,128)S(1)} %get-tuple-element.63.row_w, ...), custom_call_target="tpu_custom_call" | custom-call | tf_op jit(solution)/shard_map/step_two/pallas_call | solution.py:543
  51.4 0.1 broadcast_select_fusion
  51.5 2.6 %mend_two.1 = (f32[904,128]{1,0:T(8,128)S(1)}, f32[904,128]{1,0:T(8,128)S(1)}, f32[16,16,128]{2,1,0:T(8,128)}, f32[160,128]{1,0:T(8,128)S(1)}, f32[160,128]{1,0:T(8,128)S(1)}) custom-call(f32[384]{0:T(512)S(1)} %copy-done.3, f32[904,128]{1,0:T(8,128)S(1)} %get-tuple-element.84.halo_w, f32[904,128]{1,0:T(8,128)S(1)} %get-tuple-element.83.halo_e, ...), custom_call_target="tpu_custom_call" | custom-call | tf_op jit(solution)/shard_map/mend_two/pallas_call | solution.py:639
  54.1 4.4 %all-to-all-start.1 = ((f32[16,16,128]{2,1,0:T(8,128)}), f32[16,16,128]{2,1,0:T(8,128)S(1)}, u32[]{:S(2)}, u32[]{:S(2)}) async-start(f32[16,16,128]{2,1,0:T(8,128)} %get-tuple-element.80), calls=%async_computation.1 | async-start | bytes 262144 | tf_op jit(solution)/shard_map/all_to_all | solution.py:781
  58.5 6.3 %output.1 = f32[1800,8,128]{2,1,0:T(8,128)} custom-call(f32[7200,8,128]{2,1,0:T(8,128)} %get-tuple-element.68.stage, f32[904,128]{1,0:T(8,128)S(1)} %get-tuple-element.76.end_w, f32[904,128]{1,0:T(8,128)S(1)} %get-tuple-element.77.end_e, f32[160,128]{1,0:T(8,128)S(1)} %get-tuple-element.78.patch_n, f32[160,128]{1,0:T(8,128)S(1)} %get-tuple-element.79.patch_s), custom_call_target="tpu_custom_call" | custom-call | tf_op jit(solution)/shard_map/output/pallas_call | solution.py:691
  64.8 0.4 all-to-all-done.1.parts
  65.3 0.6 copy-done.8
  65.9 1.5 %cells.1 = (f32[2,512]{1,0:T(2,128)}, f32[1,512]{1,0:T(1,128)}) custom-call(f32[16,16,128]{2,1,0:T(8,128)} %copy-done.8), custom_call_target="tpu_custom_call" | custom-call | tf_op jit(solution)/shard_map/cells/pallas_call | solution.py:723
  (22 shorter events, 0.1 us)
Async XLA Ops:
  0.6 19.6 %copy-start = (f32[20,8,128]{2,1,0:T(8,128)S(1)}, f32[20,8,128]{2,1,0:T(8,128)}, u32[]{:S(2)}) copy-start(f32[20,8,128]{2,1,0:T(8,128)} %constant.19.clone.lane_tab) | copy-start | bytes 245764
  0.6 26.0 %copy-start.3 = (f32[384]{0:T(512)S(1)}, f32[384]{0:T(512)}, u32[]{:S(2)}) copy-start(f32[384]{0:T(512)} %constant.20.clone.sm) | copy-start | bytes 4612
  0.7 19.6 %copy-start.2 = (s32[8,128]{1,0:T(8,128)S(1)}, s32[8,128]{1,0:T(8,128)}, u32[]{:S(2)}) copy-start(s32[8,128]{1,0:T(8,128)} %mask.11) | copy-start | bytes 12292
  0.7 19.6 %copy-start.5 = (s32[8,128]{1,0:T(8,128)S(1)}, s32[8,128]{1,0:T(8,128)}, u32[]{:S(2)}) copy-start(s32[8,128]{1,0:T(8,128)} %wrow.3) | copy-start | bytes 12292
  2.2 18.0 %all-to-all-start = ((f32[16,56,128]{2,1,0:T(8,128)}), f32[16,56,128]{2,1,0:T(8,128)S(1)}, u32[]{:S(2)}, u32[]{:S(2)}) async-start(f32[16,56,128]{2,1,0:T(8,128)} %sector.1), calls=%async_computation | async-start | bytes 917504 | tf_op jit(solution)/shard_map/all_to_all | solution.py:759
  10.7 22.2 %copy-start.1 = (f32[4,18,128]{2,1,0:T(8,128)S(1)}, f32[4,18,128]{2,1,0:T(8,128)}, u32[]{:S(2)}) copy-start(f32[4,18,128]{2,1,0:T(8,128)} %constant.21.clone.dir_tab) | copy-start | bytes 110596
  10.7 22.2 %copy-start.4 = (f32[50,128]{1,0:T(8,128)S(1)}, f32[50,128]{1,0:T(8,128)}, u32[]{:S(2)}) copy-start(f32[50,128]{1,0:T(8,128)} %constant.22.clone.four) | copy-start | bytes 76804
  15.2 16.5 %collective-permute-start.1 = (f32[904,128]{1,0:T(8,128)S(1)}, f32[904,128]{1,0:T(8,128)S(1)}, u32[]{:S(2)}, u32[]{:S(2)}) collective-permute-start(f32[904,128]{1,0:T(8,128)S(1)} %get-tuple-element.52), channel_id=1, source_target_pairs={{0,15},{1,2},{2,1},{3,4},{4,3},{5,6},{6,5},{7,8},{8,7},{9,10},{10,... | collective-permute-start | bytes 1388552 | tf_op jit(solution)/shard_map/ppermute | solution.py:742
  20.0 11.8 %collective-permute-start = (f32[904,128]{1,0:T(8,128)S(1)}, f32[904,128]{1,0:T(8,128)}, u32[]{:S(2)}, u32[]{:S(2)}) collective-permute-start(f32[904,128]{1,0:T(8,128)S(1)} %get-tuple-element.51), channel_id=1, source_target_pairs={{0,1},{1,0},{2,3},{3,2},{4,5},{5,4},{6,7},{7,6},{8,9},{9,8},{10,11... | collective-permute-start | bytes 1388552 | tf_op jit(solution)/shard_map/ppermute | solution.py:741
  21.2 11.7 %collective-permute-start.3 = (f32[160,128]{1,0:T(8,128)S(1)}, f32[160,128]{1,0:T(8,128)S(1)}, u32[]{:S(2)}, u32[]{:S(2)}) collective-permute-start(f32[160,128]{1,0:T(8,128)S(1)} %get-tuple-element.95), channel_id=1, source_target_pairs={{16,32},{32,16},{48,64},{64,48},{80,96},{96,80},{17,33},{33,17},{4... | collective-permute-start | bytes 245768 | tf_op jit(solution)/shard_map/ppermute | solution.py:753
  26.6 6.3 %collective-permute-start.2 = (f32[160,128]{1,0:T(8,128)S(1)}, f32[160,128]{1,0:T(8,128)S(1)}, u32[]{:S(2)}, u32[]{:S(2)}) collective-permute-start(f32[160,128]{1,0:T(8,128)S(1)} %get-tuple-element.96), channel_id=1, source_target_pairs={{0,16},{16,0},{32,48},{48,32},{64,80},{80,64},{96,112},{112,96},{1... | collective-permute-start | bytes 245768 | tf_op jit(solution)/shard_map/ppermute | solution.py:752
  35.5 16.0 %copy-start.6 = (s32[8,128]{1,0:T(8,128)S(1)}, s32[8,128]{1,0:T(8,128)}, u32[]{:S(2)}) copy-start(s32[8,128]{1,0:T(8,128)} %owner.1) | copy-start | bytes 12292
  35.5 16.0 %copy-start.7 = (s32[8,128]{1,0:T(8,128)S(1)}, s32[8,128]{1,0:T(8,128)}, u32[]{:S(2)}) copy-start(s32[8,128]{1,0:T(8,128)} %weight.1) | copy-start | bytes 12292
  35.6 15.8 %collective-permute-start.5 = (f32[904,128]{1,0:T(8,128)S(1)}, f32[904,128]{1,0:T(8,128)S(1)}, u32[]{:S(2)}, u32[]{:S(2)}) collective-permute-start(f32[904,128]{1,0:T(8,128)S(1)} %get-tuple-element.85), channel_id=1, source_target_pairs={{0,15},{1,2},{2,1},{3,4},{4,3},{5,6},{6,5},{7,8},{8,7},{9,10},{10,... | collective-permute-start | bytes 1388552 | tf_op jit(solution)/shard_map/ppermute | solution.py:742
  38.1 13.3 %collective-permute-start.4 = (f32[904,128]{1,0:T(8,128)S(1)}, f32[904,128]{1,0:T(8,128)S(1)}, u32[]{:S(2)}, u32[]{:S(2)}) collective-permute-start(f32[904,128]{1,0:T(8,128)S(1)} %get-tuple-element.86), channel_id=1, source_target_pairs={{0,1},{1,0},{2,3},{3,2},{4,5},{5,4},{6,7},{7,6},{8,9},{9,8},{10,11... | collective-permute-start | bytes 1388552 | tf_op jit(solution)/shard_map/ppermute | solution.py:741
  38.1 13.2 %collective-permute-start.7 = (f32[160,128]{1,0:T(8,128)S(1)}, f32[160,128]{1,0:T(8,128)S(1)}, u32[]{:S(2)}, u32[]{:S(2)}) collective-permute-start(f32[160,128]{1,0:T(8,128)S(1)} %get-tuple-element.91), channel_id=1, source_target_pairs={{16,32},{32,16},{48,64},{64,48},{80,96},{96,80},{17,33},{33,17},{4... | collective-permute-start | bytes 245768 | tf_op jit(solution)/shard_map/ppermute | solution.py:753
  43.6 7.7 %collective-permute-start.6 = (f32[160,128]{1,0:T(8,128)S(1)}, f32[160,128]{1,0:T(8,128)S(1)}, u32[]{:S(2)}, u32[]{:S(2)}) collective-permute-start(f32[160,128]{1,0:T(8,128)S(1)} %get-tuple-element.92), channel_id=1, source_target_pairs={{0,16},{16,0},{32,48},{48,32},{64,80},{80,64},{96,112},{112,96},{1... | collective-permute-start | bytes 245768 | tf_op jit(solution)/shard_map/ppermute | solution.py:752
  54.1 11.2 %all-to-all-start.1 = ((f32[16,16,128]{2,1,0:T(8,128)}), f32[16,16,128]{2,1,0:T(8,128)S(1)}, u32[]{:S(2)}, u32[]{:S(2)}) async-start(f32[16,16,128]{2,1,0:T(8,128)} %get-tuple-element.80), calls=%async_computation.1 | async-start | bytes 262144 | tf_op jit(solution)/shard_map/all_to_all | solution.py:781
  65.3 0.6 copy-start.8

commit v6 on v5

--- a/solution.py
+++ b/solution.py
@@ -190,12 +190,9 @@
     )(mask, winds, wrow)
 
 
-def split3(x):
+def split2(x):
     a = x.astype(BF16)
-    r = x - a.astype(F32)
-    b = r.astype(BF16)
-    c = (r - b.astype(F32)).astype(BF16)
-    return a, b, c
+    return a, (x - a.astype(F32)).astype(BF16)
 
 
 def wind_kernel(
@@ -220,7 +217,7 @@
         [table[:, 16 * c : 16 * c + 16].reshape(hi_count, 128) for c in range(2)], axis=1
     )
     got = None
-    for part in split3(tab):
+    for part in split2(tab):
         term = lax.dot_general(
             part, hot, (((0,), (0,)), ((), ())), preferred_element_type=F32
         )
@@ -604,7 +601,7 @@
     share = weight[...].astype(F32) * maskf
     tau = 0.02 * (uu * uu + vv * vv) + 0.25
     terms = (share, share * tau, share * push[0], share * push[1])
-    parts = [split3(t) for t in terms]
+    parts = [split2(t) for t in terms]
     dests = cells.shape[0]
     own = owner[...] & (dests * 512 - 1)
     hi_own = own // 128
@@ -617,7 +614,7 @@
     for x in range(8):
         hot = jnp.where(lo_iota == lo_own[x : x + 1], 1.0, 0.0).astype(BF16)
         match = want == hi_own[x : x + 1]
-        for p in range(3):
+        for p in range(2):
             rows = [parts[k][p][x : x + 1].astype(F32) for k in range(4)]
             tile = jnp.where(
                 kind == 0, rows[0],
@@ -738,8 +735,8 @@
     others = [(i, (i + 1 if i & 1 else i - 1) % lons) for i in range(lons)]
 
     def arrive(send_a, send_b):
+        second = lax.ppermute(send_b, "lon", others)
         first = lax.ppermute(send_a, "lon", pairs)
-        second = lax.ppermute(send_b, "lon", others)
         return jnp.where(uneven, first, second), jnp.where(uneven, second, first)
 
     def trade(east, west):
@@ -749,8 +746,8 @@
     across = [(i, i + 1 if i & 1 else i - 1) for i in range(1, lats - 1)]
 
     def swap(north, south):
+        second = lax.ppermute(jnp.where(odd, north, south), "lat", across)
         first = lax.ppermute(jnp.where(odd, south, north), "lat", inside)
-        second = lax.ppermute(jnp.where(odd, north, south), "lat", across)
         return jnp.where(odd, first, second), jnp.where(odd, second, first)
 
     mine = sector_call(sea_mask, atm_wind, wind_row, lons)

time: 68.3 us -> 68.1 us (level)
  no operation moved by 1% of the time
where the time goes in v6:
time: 68.1 us; the launch traced here: 67.3 us
  Pallas kernels  32.4 us (48%)
  starting transfers between devices  31.3 us (46%)
  other arithmetic  1.28 us (2%)
  between operations  0.95 us (1%)
  local copies, waits for them, and re-layouts  0.69 us (1%)
  waiting for transfers between devices  0.69 us (1%)
    ppermute x2, starting transfers between devices, swap(): second = lax.ppermute(jnp.where(odd, north, south), 'lat', across)  10.9 us
    all_to_all x1, starting transfers between devices, body(): table = lax.all_to_all(mine, 'lon', 0, 0)  8.43 us
    pallas_call x1, Pallas kernels, step_two_call(): pl.pallas_call(step_two_kernel, in_specs=[SMEM] + [VMEM] * 9, out_specs=[...  7.61 us
    ppermute x2, starting transfers between devices, arrive(): second = lax.ppermute(send_b, 'lon', others)  7.37 us
    pallas_call x1, Pallas kernels, output_call(): pl.pallas_call(output_kernel, in_specs=[HBM] + [VMEM] * 4, out_specs=HBM,...  6.35 us
    pallas_call x1, Pallas kernels, step_one_call(): pl.pallas_call(step_one_kernel, in_specs=[SMEM, HBM] + [VMEM] * 4, out_sp...  5.08 us
    pallas_call x1, Pallas kernels, first_call(): pl.pallas_call(first_kernel, in_specs=[SMEM, HBM], out_specs=[VMEM] * 7,...  4.52 us
    all_to_all x1, starting transfers between devices, body(): parts = lax.all_to_all(cells, 'lon', 0, 0)  4.41 us
  transfers between devices with their start and end apart: 10, of which 2 were waited for; matrix products, arithmetic and copies ran while one was open for 2% of the time, Pallas kernels for 36%

profile of v6, /device:TPU:1, one launch (start us, length us, event | category | flops | bytes accessed | tf_op | source)
XLA Modules:
  0.0 67.3 jit_solution(5937461902474236918)
XLA Ops:
  0.6 0.0 copy-start
  0.6 0.0 copy-start.3
  0.7 1.6 %sector.1 = f32[16,56,128]{2,1,0:T(8,128)} custom-call(s32[8,128]{1,0:T(8,128)} %mask.11, f32[2,2048]{1,0:T(2,128)} %winds.2, s32[8,128]{1,0:T(8,128)} %wrow.3), custom_call_target="tpu_custom_call" | custom-call | tf_op jit(solution)/shard_map/sector/pallas_call | solution.py:183
  2.2 8.4 %all-to-all-start = ((f32[16,56,128]{2,1,0:T(8,128)}), f32[16,56,128]{2,1,0:T(8,128)S(1)}, u32[]{:S(2)}, u32[]{:S(2)}) async-start(f32[16,56,128]{2,1,0:T(8,128)} %sector.1), calls=%async_computation | async-start | bytes 917504 | tf_op jit(solution)/shard_map/all_to_all | solution.py:756
  10.7 0.0 copy-start.1
  10.7 0.0 copy-start.4
  10.7 4.5 %first.1 = (f32[904,128]{1,0:T(8,128)S(1)}, f32[904,128]{1,0:T(8,128)S(1)}, f32[904,128]{1,0:T(8,128)S(1)}, f32[904,128]{1,0:T(8,128)S(1)}, f32[20,8,128]{2,1,0:...) custom-call(s32[1]{0:T(128)} %bitcast.1.uneven, f32[1800,8,128]{2,1,0:T(8,128)} %spec_hbm.1), custom_call_target="tpu_custom_call" | custom-call | tf_op jit(solution)/shard_map/first/pallas_call | solution.py:171
  15.2 4.8 %collective-permute-start.1 = (f32[904,128]{1,0:T(8,128)S(1)}, f32[904,128]{1,0:T(8,128)S(1)}, u32[]{:S(2)}, u32[]{:S(2)}) collective-permute-start(f32[904,128]{1,0:T(8,128)S(1)} %get-tuple-element.52), channel_id=1, source_target_pairs={{0,15},{1,2},{2,1},{3,4},{4,3},{5,6},{6,5},{7,8},{8,7},{9,10},{10,... | collective-permute-start | bytes 1388552 | tf_op jit(solution)/shard_map/ppermute | solution.py:738
  20.0 0.2 all-to-all-done.table
  20.2 0.8 %winds.3 = (f32[8,128]{1,0:T(8,128)S(1)}, f32[8,128]{1,0:T(8,128)S(1)}, f32[8,128]{1,0:T(8,128)S(1)}, f32[160,128]{1,0:T(8,128)S(1)}, f32[160,128]{1,0:T(8,128)S(1)}) custom-call(s32[1]{0:T(128)} %bitcast.me_ref, f32[16,56,128]{2,1,0:T(8,128)S(1)} %all-to-all-done.table, s32[8,128]{1,0:T(8,128)S(1)} %copy-done.5, f32[8,128]{1,0:T(8,128)S(1)} %get-tuple-element.45.msq, ...), custom_call_target="tpu_custom_call" | custom-call | tf_op jit(solution)/shard_map/winds/pallas_call | solution.py:259
  21.1 5.4 %collective-permute-start.3 = (f32[160,128]{1,0:T(8,128)S(1)}, f32[160,128]{1,0:T(8,128)S(1)}, u32[]{:S(2)}, u32[]{:S(2)}) collective-permute-start(f32[160,128]{1,0:T(8,128)S(1)} %get-tuple-element.95), channel_id=1, source_target_pairs={{16,32},{32,16},{48,64},{64,48},{80,96},{96,80},{17,33},{33,17},{4... | collective-permute-start | bytes 245768 | tf_op jit(solution)/shard_map/ppermute | solution.py:749
  26.4 0.1 collective-permute-start.2
  26.5 5.1 %step_one.1 = (f32[1800,8,128]{2,1,0:T(8,128)S(1)}, f32[8,128]{1,0:T(8,128)S(1)}, f32[904,128]{1,0:T(8,128)S(1)}, f32[904,128]{1,0:T(8,128)S(1)}, f32[904,128]{1,0:T(8,128)S(1)}, /*index=5*/f32[904,128]{1,0:T(8,128)S(1)}) custom-call(f32[384]{0:T(512)S(1)} %copy-done.3, f32[1800,8,128]{2,1,0:T(8,128)} %spec_hbm.1, f32[8,128]{1,0:T(8,128)S(1)} %get-tuple-element.48.u, ...), custom_call_target="tpu_custom_call" | custom-call | tf_op jit(solution)/shard_map/step_one/pallas_call | solution.py:350
  31.6 0.0 collective-permute-done.1
  31.6 0.0 collective-permute-done
  31.7 1.1 %broadcast_select_fusion.4 = (f32[904,128]{1,0:T(8,128)S(1)}, f32[904,128]{1,0:T(8,128)S(1)}) fusion(f32[904,128]{1,0:T(8,128)S(1)} %collective-permute-done.1, f32[904,128]{1,0:T(8,128)} %collective-permute-done, pred[]{:T(512)S(6)} %eq.6), kind=kLoop, calls=%fused_computation.4 | loop fusion | flops 231424 | bytes 1851393 | tf_op jit(solution)/shard_map/jit(_where)/select_n | solution.py:740
  32.7 0.0 collective-permute-done.3
  32.8 2.5 %mend_one.1 = (f32[8,128]{1,0:T(8,128)S(1)}, f32[904,128]{1,0:T(8,128)S(1)}, f32[904,128]{1,0:T(8,128)S(1)}, f32[904,128]{1,0:T(8,128)S(1)}, f32[904,128]{1,0:T(...) custom-call(f32[384]{0:T(512)S(1)} %copy-done.3, ...), custom_call_target="tpu_custom_call" | custom-call | tf_op jit(solution)/shard_map/mend_one/pallas_call | solution.py:459
  35.4 0.0 copy-start.6
  35.4 0.0 copy-start.7
  35.4 0.1 broadcast_select_fusion.2
  35.4 2.6 %collective-permute-start.5 = (f32[904,128]{1,0:T(8,128)S(1)}, f32[904,128]{1,0:T(8,128)S(1)}, u32[]{:S(2)}, u32[]{:S(2)}) collective-permute-start(f32[904,128]{1,0:T(8,128)S(1)} %get-tuple-element.85), channel_id=1, source_target_pairs={{0,15},{1,2},{2,1},{3,4},{4,3},{5,6},{6,5},{7,8},{8,7},{9,10},{10,... | collective-permute-start | bytes 1388552 | tf_op jit(solution)/shard_map/ppermute | solution.py:738
  38.1 5.5 %collective-permute-start.7 = (f32[160,128]{1,0:T(8,128)S(1)}, f32[160,128]{1,0:T(8,128)S(1)}, u32[]{:S(2)}, u32[]{:S(2)}) collective-permute-start(f32[160,128]{1,0:T(8,128)S(1)} %get-tuple-element.91), channel_id=1, source_target_pairs={{16,32},{32,16},{48,64},{64,48},{80,96},{96,80},{17,33},{33,17},{4... | collective-permute-start | bytes 245768 | tf_op jit(solution)/shard_map/ppermute | solution.py:749
  43.6 0.1 collective-permute-start.6
  43.7 7.6 %step_two.1 = (f32[7200,8,128]{2,1,0:T(8,128)}, f32[2,8,128]{2,1,0:T(8,128)S(1)}, f32[904,128]{1,0:T(8,128)S(1)}, f32[904,128]{1,0:T(8,128)S(1)}) custom-call(f32[384]{0:T(512)S(1)} %copy-done.3, f32[1800,8,128]{2,1,0:T(8,128)S(1)} %get-tuple-element.50.spec, f32[904,128]{1,0:T(8,128)S(1)} %get-tuple-element.63.row_w, ...), custom_call_target="tpu_custom_call" | custom-call | tf_op jit(solution)/shard_map/step_two/pallas_call | solution.py:540
  51.4 0.1 broadcast_select_fusion
  51.5 2.4 %mend_two.1 = (f32[904,128]{1,0:T(8,128)S(1)}, f32[904,128]{1,0:T(8,128)S(1)}, f32[16,16,128]{2,1,0:T(8,128)}, f32[160,128]{1,0:T(8,128)S(1)}, f32[160,128]{1,0:T(8,128)S(1)}) custom-call(f32[384]{0:T(512)S(1)} %copy-done.3, f32[904,128]{1,0:T(8,128)S(1)} %get-tuple-element.84.halo_w, f32[904,128]{1,0:T(8,128)S(1)} %get-tuple-element.83.halo_e, ...), custom_call_target="tpu_custom_call" | custom-call | tf_op jit(solution)/shard_map/mend_two/pallas_call | solution.py:636
  53.9 4.4 %all-to-all-start.1 = ((f32[16,16,128]{2,1,0:T(8,128)}), f32[16,16,128]{2,1,0:T(8,128)S(1)}, u32[]{:S(2)}, u32[]{:S(2)}) async-start(f32[16,16,128]{2,1,0:T(8,128)} %get-tuple-element.80), calls=%async_computation.1 | async-start | bytes 262144 | tf_op jit(solution)/shard_map/all_to_all | solution.py:778
  58.3 6.3 %output.1 = f32[1800,8,128]{2,1,0:T(8,128)} custom-call(f32[7200,8,128]{2,1,0:T(8,128)} %get-tuple-element.68.stage, f32[904,128]{1,0:T(8,128)S(1)} %get-tuple-element.76.end_w, f32[904,128]{1,0:T(8,128)S(1)} %get-tuple-element.77.end_e, f32[160,128]{1,0:T(8,128)S(1)} %get-tuple-element.78.patch_n, f32[160,128]{1,0:T(8,128)S(1)} %get-tuple-element.79.patch_s), custom_call_target="tpu_custom_call" | custom-call | tf_op jit(solution)/shard_map/output/pallas_call | solution.py:688
  64.7 0.4 all-to-all-done.1.parts
  65.1 0.6 copy-done.8
  65.8 1.5 %cells.1 = (f32[2,512]{1,0:T(2,128)}, f32[1,512]{1,0:T(1,128)}) custom-call(f32[16,16,128]{2,1,0:T(8,128)} %copy-done.8), custom_call_target="tpu_custom_call" | custom-call | tf_op jit(solution)/shard_map/cells/pallas_call | solution.py:720
  (22 shorter events, 0.1 us)
Async XLA Ops:
  0.6 19.6 %copy-start = (f32[20,8,128]{2,1,0:T(8,128)S(1)}, f32[20,8,128]{2,1,0:T(8,128)}, u32[]{:S(2)}) copy-start(f32[20,8,128]{2,1,0:T(8,128)} %constant.19.clone.lane_tab) | copy-start | bytes 245764
  0.6 25.9 %copy-start.3 = (f32[384]{0:T(512)S(1)}, f32[384]{0:T(512)}, u32[]{:S(2)}) copy-start(f32[384]{0:T(512)} %constant.20.clone.sm) | copy-start | bytes 4612
  0.7 19.6 %copy-start.2 = (s32[8,128]{1,0:T(8,128)S(1)}, s32[8,128]{1,0:T(8,128)}, u32[]{:S(2)}) copy-start(s32[8,128]{1,0:T(8,128)} %mask.11) | copy-start | bytes 12292
  0.7 19.6 %copy-start.5 = (s32[8,128]{1,0:T(8,128)S(1)}, s32[8,128]{1,0:T(8,128)}, u32[]{:S(2)}) copy-start(s32[8,128]{1,0:T(8,128)} %wrow.3) | copy-start | bytes 12292
  2.2 18.0 %all-to-all-start = ((f32[16,56,128]{2,1,0:T(8,128)}), f32[16,56,128]{2,1,0:T(8,128)S(1)}, u32[]{:S(2)}, u32[]{:S(2)}) async-start(f32[16,56,128]{2,1,0:T(8,128)} %sector.1), calls=%async_computation | async-start | bytes 917504 | tf_op jit(solution)/shard_map/all_to_all | solution.py:756
  10.7 22.1 %copy-start.1 = (f32[4,18,128]{2,1,0:T(8,128)S(1)}, f32[4,18,128]{2,1,0:T(8,128)}, u32[]{:S(2)}) copy-start(f32[4,18,128]{2,1,0:T(8,128)} %constant.21.clone.dir_tab) | copy-start | bytes 110596
  10.7 22.1 %copy-start.4 = (f32[50,128]{1,0:T(8,128)S(1)}, f32[50,128]{1,0:T(8,128)}, u32[]{:S(2)}) copy-start(f32[50,128]{1,0:T(8,128)} %constant.22.clone.four) | copy-start | bytes 76804
  15.2 16.4 %collective-permute-start.1 = (f32[904,128]{1,0:T(8,128)S(1)}, f32[904,128]{1,0:T(8,128)S(1)}, u32[]{:S(2)}, u32[]{:S(2)}) collective-permute-start(f32[904,128]{1,0:T(8,128)S(1)} %get-tuple-element.52), channel_id=1, source_target_pairs={{0,15},{1,2},{2,1},{3,4},{4,3},{5,6},{6,5},{7,8},{8,7},{9,10},{10,... | collective-permute-start | bytes 1388552 | tf_op jit(solution)/shard_map/ppermute | solution.py:738
  20.0 11.6 %collective-permute-start = (f32[904,128]{1,0:T(8,128)S(1)}, f32[904,128]{1,0:T(8,128)}, u32[]{:S(2)}, u32[]{:S(2)}) collective-permute-start(f32[904,128]{1,0:T(8,128)S(1)} %get-tuple-element.51), channel_id=1, source_target_pairs={{0,1},{1,0},{2,3},{3,2},{4,5},{5,4},{6,7},{7,6},{8,9},{9,8},{10,11... | collective-permute-start | bytes 1388552 | tf_op jit(solution)/shard_map/ppermute | solution.py:739
  21.1 11.7 %collective-permute-start.3 = (f32[160,128]{1,0:T(8,128)S(1)}, f32[160,128]{1,0:T(8,128)S(1)}, u32[]{:S(2)}, u32[]{:S(2)}) collective-permute-start(f32[160,128]{1,0:T(8,128)S(1)} %get-tuple-element.95), channel_id=1, source_target_pairs={{16,32},{32,16},{48,64},{64,48},{80,96},{96,80},{17,33},{33,17},{4... | collective-permute-start | bytes 245768 | tf_op jit(solution)/shard_map/ppermute | solution.py:749
  26.4 6.3 %collective-permute-start.2 = (f32[160,128]{1,0:T(8,128)S(1)}, f32[160,128]{1,0:T(8,128)S(1)}, u32[]{:S(2)}, u32[]{:S(2)}) collective-permute-start(f32[160,128]{1,0:T(8,128)S(1)} %get-tuple-element.96), channel_id=1, source_target_pairs={{0,16},{16,0},{32,48},{48,32},{64,80},{80,64},{96,112},{112,96},{1... | collective-permute-start | bytes 245768 | tf_op jit(solution)/shard_map/ppermute | solution.py:750
  35.4 16.1 %copy-start.6 = (s32[8,128]{1,0:T(8,128)S(1)}, s32[8,128]{1,0:T(8,128)}, u32[]{:S(2)}) copy-start(s32[8,128]{1,0:T(8,128)} %owner.1) | copy-start | bytes 12292
  35.4 16.1 %copy-start.7 = (s32[8,128]{1,0:T(8,128)S(1)}, s32[8,128]{1,0:T(8,128)}, u32[]{:S(2)}) copy-start(s32[8,128]{1,0:T(8,128)} %weight.1) | copy-start | bytes 12292
  35.4 15.9 %collective-permute-start.5 = (f32[904,128]{1,0:T(8,128)S(1)}, f32[904,128]{1,0:T(8,128)S(1)}, u32[]{:S(2)}, u32[]{:S(2)}) collective-permute-start(f32[904,128]{1,0:T(8,128)S(1)} %get-tuple-element.85), channel_id=1, source_target_pairs={{0,15},{1,2},{2,1},{3,4},{4,3},{5,6},{6,5},{7,8},{8,7},{9,10},{10,... | collective-permute-start | bytes 1388552 | tf_op jit(solution)/shard_map/ppermute | solution.py:738
  38.1 13.3 %collective-permute-start.4 = (f32[904,128]{1,0:T(8,128)S(1)}, f32[904,128]{1,0:T(8,128)S(1)}, u32[]{:S(2)}, u32[]{:S(2)}) collective-permute-start(f32[904,128]{1,0:T(8,128)S(1)} %get-tuple-element.86), channel_id=1, source_target_pairs={{0,1},{1,0},{2,3},{3,2},{4,5},{5,4},{6,7},{7,6},{8,9},{9,8},{10,11... | collective-permute-start | bytes 1388552 | tf_op jit(solution)/shard_map/ppermute | solution.py:739
  38.1 13.2 %collective-permute-start.7 = (f32[160,128]{1,0:T(8,128)S(1)}, f32[160,128]{1,0:T(8,128)S(1)}, u32[]{:S(2)}, u32[]{:S(2)}) collective-permute-start(f32[160,128]{1,0:T(8,128)S(1)} %get-tuple-element.91), channel_id=1, source_target_pairs={{16,32},{32,16},{48,64},{64,48},{80,96},{96,80},{17,33},{33,17},{4... | collective-permute-start | bytes 245768 | tf_op jit(solution)/shard_map/ppermute | solution.py:749
  43.6 7.7 %collective-permute-start.6 = (f32[160,128]{1,0:T(8,128)S(1)}, f32[160,128]{1,0:T(8,128)S(1)}, u32[]{:S(2)}, u32[]{:S(2)}) collective-permute-start(f32[160,128]{1,0:T(8,128)S(1)} %get-tuple-element.92), channel_id=1, source_target_pairs={{0,16},{16,0},{32,48},{48,32},{64,80},{80,64},{96,112},{112,96},{1... | collective-permute-start | bytes 245768 | tf_op jit(solution)/shard_map/ppermute | solution.py:750
  53.9 11.2 %all-to-all-start.1 = ((f32[16,16,128]{2,1,0:T(8,128)}), f32[16,16,128]{2,1,0:T(8,128)S(1)}, u32[]{:S(2)}, u32[]{:S(2)}) async-start(f32[16,16,128]{2,1,0:T(8,128)} %get-tuple-element.80), calls=%async_computation.1 | async-start | bytes 262144 | tf_op jit(solution)/shard_map/all_to_all | solution.py:778
  65.1 0.6 copy-start.8
